TPU v7x, 32 devices: a whole 2x2x4 slice. The times are simulated.
32 devices in a mesh: ew: 8 (over z, y), ns: 4 (over x, core).
Axes of the slice: x: 2, y: 2, z: 4, core: 2. Of those that a mesh axis runs over, the one named last changes fastest.
Arguments:
- theta: float32 [16, 32, 1024], P(None, 'ns', 'ew'), may hold values from -6 to 6
- velocity: float32 [2, 16, 32, 1024], P(None, None, 'ns', 'ew'), may hold values from -1.2 to 1.2
- diffusivity: float32 [16, 32, 1024], P(None, 'ns', 'ew'), may hold values from 0.02 to 0.2
- land_mask: int32 [4, 8], P('ns', 'ew'), may hold values from 0 to 1, as said below
- fold_partner: int32 [8], P('ew'), may hold values from 0 to 7, as said below
- atm_flux: bfloat16 [4, 8, 6, 128], P('ns', 'ew'), may hold values from -6 to 6
- remap_src: int32 [4, 8, 4], P('ns', 'ew'), may hold values from 0 to 7, as said below
- remap_weights: bfloat16 [4, 8, 4, 128, 1024], P('ns', 'ew'), may hold values from -0.25 to 0.25
Outputs:
- theta_out: float32 [16, 32, 1024], P(None, 'ns', 'ew')
- ocean_flux: float32 [4, 8, 6, 1024], P('ns', 'ew')
Inputs may be any that keep to these rules, and one draw needn't show every extreme that they name: A pairing of the block columns: fold_partner[fold_partner[e]] = e and fold_partner[e] != e. `land_mask`: the top block row is wet. `remap_src`: distinct columns of an ocean block; one of them is (its own column + 4) mod 8.
All inputs are finite; a program needn't handle non-finite values.
Results may differ from a plain program's by a relative error of at most 0.0007.
Values may be sent and summed in bfloat16 or wider, within the bound.
No kernel may reach another device: no remote copies, remote signals or barrier semaphores. Data moves between devices by JAX's collectives and lax.ppermute only.
A program may use at most 64 MiB of HBM per device.

v0:
```python
import jax
import jax.numpy as jnp
from jax import lax
from jax.sharding import PartitionSpec as P

STEPS = 3


COEFS = (0.5, -0.3, 0.2, 0.4, -0.25, 0.35)


def with_halo(block, sides, width, periodic):
    for axis, dim in sides:
        count = lax.axis_size(axis)
        forward = [(i, i + 1) for i in range(count - 1)]
        if periodic:
            forward.append((count - 1, 0))
        backward = [(target, source) for source, target in forward]
        low = lax.ppermute(
            lax.slice_in_dim(block, block.shape[dim] - width, None, axis=dim), axis, forward
        )
        high = lax.ppermute(lax.slice_in_dim(block, 0, width, axis=dim), axis, backward)
        block = jnp.concatenate([low, block, high], axis=dim)
    return block


def local(
    theta, velocity, diffusivity, land_mask, fold_partner, atm_flux, remap_src, remap_weights
):
    levels, rows, cols = theta.shape
    my_col = lax.axis_index("ew")
    sources = remap_src[0, 0]
    lists = lax.all_gather(remap_src, "ew", axis=1, tiled=True)
    needed = jnp.any(lists[0] == my_col, axis=1)
    outgoing = jnp.where(
        needed[:, None, None], atm_flux[0, 0][None], jnp.zeros_like(atm_flux[0, 0])[None]
    )
    incoming = lax.all_to_all(outgoing, "ew", split_axis=0, concat_axis=0, tiled=True)
    chosen = incoming[sources]
    local_flux = jnp.einsum(
        "pka,pao->ko", chosen, remap_weights[0, 0], preferred_element_type=jnp.float32
    )
    coef = jnp.array(COEFS, jnp.float32)
    forcing = 0.1 * jnp.einsum("k,ko->o", coef, local_flux).reshape(rows, cols)
    wet = land_mask[0, 0].astype(jnp.float32)
    partner = fold_partner[0]
    is_top = lax.axis_index("ns") == lax.axis_size("ns") - 1
    wanted = partner * cols + cols - 1 - jnp.arange(cols, dtype=jnp.int32)
    east_u = velocity[0]
    north_v = velocity[1]
    field = theta
    for step in range(STEPS):
        rim_x = with_halo(field, (("ew", 2),), 1, True)
        rim_y = with_halo(field, (("ns", 1),), 1, False)
        piece = lax.all_gather(field[:, -1, :], "ew", axis=1, tiled=True)
        width = piece.shape[1]
        inside = (wanted >= 0) & (wanted < width)
        picked = jnp.take(piece, jnp.clip(wanted, 0, width - 1), axis=1)
        folded = jnp.where(inside[None, :], picked, 0.0)
        ghost = jnp.where(is_top, folded, rim_y[:, -1, :])
        east = rim_x[:, :, 2:]
        west = rim_x[:, :, :-2]
        south = rim_y[:, :-2, :]
        north = jnp.concatenate([rim_y[:, 2:-1, :], ghost[:, None, :]], 1)
        lap = east + west + north + south - 4.0 * field
        adv = 0.5 * (east_u * (east - west) + north_v * (north - south))
        tend = diffusivity * lap - adv
        tend = tend.at[0].add(forcing)
        field = field + wet * tend
    return (field, local_flux[None, None])


def solution(mesh):
    return jax.shard_map(
        local,
        mesh=mesh,
        in_specs=(
            P(None, "ns", "ew"),
            P(None, None, "ns", "ew"),
            P(None, "ns", "ew"),
            P("ns", "ew"),
            P("ew"),
            P("ns", "ew", None, None),
            P("ns", "ew", None),
            P("ns", "ew", None, None, None),
        ),
        out_specs=(P(None, "ns", "ew"), P("ns", "ew", None, None)),
        check_vma=False,
    )
```

profile of v0, /device:TPU:2, one launch (start us, length us, event | category | flops | bytes accessed | tf_op | source)
XLA Modules:
  0.0 129.7 jit_solution(6962227218700493615)
XLA Ops:
  0.6 1.0 fusion.23
  1.6 1.9 %collective-permute-start.3 = (f32[16,1,128]{2,1,0:T(1,128)S(1)}, f32[16,1,128]{2,1,0:T(1,128)S(1)}, u32[]{:S(2)}, u32[]{:S(2)}) collective-permute-start(f32[16,1,128]{2,1,0:T(1,128)S(1)} %get-tuple-element.60), channel_id=1, source_target_pairs={{0,1},{1,2},{2,3},{4,5},{5,6},{6,7},{8,9},{9,10},{10,11},{12,13},{... | collective-permute-start | bytes 24584 | tf_op jit(solution)/shard_map/ppermute | solution.py:19
  3.5 3.6 %collective-permute-start.2 = (f32[16,1,128]{2,0,1:T(8,128)S(1)}, f32[16,1,128]{2,0,1:T(8,128)S(1)}, u32[]{:S(2)}, u32[]{:S(2)}) collective-permute-start(f32[16,1,128]{2,0,1:T(8,128)S(1)} %bitcast.106), channel_id=1, source_target_pairs={{1,0},{2,1},{3,2},{5,4},{6,5},{7,6},{9,8},{10,9},{11,10},{13,12},{... | collective-permute-start | bytes 24584 | tf_op jit(solution)/shard_map/ppermute | solution.py:22
  7.2 1.0 fusion.22
  8.2 4.6 %collective-permute-start = (f32[16,8,1]{2,1,0:T(8,128)S(1)}, f32[16,8,1]{2,1,0:T(8,128)S(1)}, u32[]{:S(2)}, u32[]{:S(2)}) collective-permute-start(f32[16,8,1]{2,1,0:T(8,128)S(1)} %get-tuple-element.58), channel_id=1, source_target_pairs={{4,0},{8,4},{12,8},{16,12},{20,16},{24,20},{28,24},{0,28},{5,1},{9... | collective-permute-start | bytes 1544 | tf_op jit(solution)/shard_map/ppermute | solution.py:22
  12.8 0.7 copy-done.6
  13.5 20.9 %all_gather.13 = s32[1,8,4]{2,0,1:T(1,128)S(1)} all-gather(s32[1,1,4]{2,0,1:T(1,128)S(1)} %bitcast.110), channel_id=1, replica_groups=mesh['ew'=8,'ns'=4] {'ew'}, dimensions={1}, use_global_device_ids=true | all-gather | bytes 144 | tf_op jit(solution)/shard_map/all_gather | solution.py:33
  34.6 0.4 copy-done.4
  35.0 0.7 broadcast_select_fusion
  35.7 3.5 %all-to-all-start = ((bf16[8,6,128]{2,1,0:T(8,128)(2,1)}), bf16[8,6,128]{2,1,0:T(8,128)(2,1)S(1)}, u32[]{:S(2)}, u32[]{:S(2)}) async-start(bf16[8,6,128]{2,1,0:T(8,128)(2,1)} %broadcast_select_fusion), calls=%async_computation | async-start | bytes 32768 | tf_op jit(solution)/shard_map/all_to_all | solution.py:38
  39.9 21.3 %all-gather = f32[16,1,1024]{2,1,0:T(1,128)S(1)} all-gather(f32[16,1,128]{2,1,0:T(1,128)S(1)} %get-tuple-element.60), channel_id=2, replica_groups=mesh['ew'=8,'ns'=4] {'ew'}, dimensions={2}, use_global_device_ids=true | all-gather | bytes 73728 | tf_op jit(solution)/shard_map/all_gather | solution.py:55
  61.4 0.6 gather_fusion.1
  63.0 0.6 gather_fusion
  63.8 0.4 copy-done.5
  64.4 1.9 %collective-permute-start.7 = (f32[16,1,128]{2,1,0:T(1,128)S(1)}, f32[16,1,128]{2,1,0:T(1,128)S(1)}, u32[]{:S(2)}, u32[]{:S(2)}) collective-permute-start(f32[16,1,128]{2,1,0:T(1,128)S(1)} %get-tuple-element.56), channel_id=1, source_target_pairs={{0,1},{1,2},{2,3},{4,5},{5,6},{6,7},{8,9},{9,10},{10,11},{12,13},{... | collective-permute-start | bytes 24584 | tf_op jit(solution)/shard_map/ppermute | solution.py:19
  66.4 3.6 %collective-permute-start.6 = (f32[16,1,128]{2,0,1:T(8,128)S(1)}, f32[16,1,128]{2,0,1:T(8,128)S(1)}, u32[]{:S(2)}, u32[]{:S(2)}) collective-permute-start(f32[16,1,128]{2,0,1:T(8,128)S(1)} %bitcast.107), channel_id=1, source_target_pairs={{1,0},{2,1},{3,2},{5,4},{6,5},{7,6},{9,8},{10,9},{11,10},{13,12},{... | collective-permute-start | bytes 24584 | tf_op jit(solution)/shard_map/ppermute | solution.py:22
  70.0 16.6 %all-gather.1 = f32[16,1,1024]{2,1,0:T(1,128)S(1)} all-gather(f32[16,1,128]{2,1,0:T(1,128)S(1)} %get-tuple-element.56), channel_id=3, replica_groups=mesh['ew'=8,'ns'=4] {'ew'}, dimensions={2}, use_global_device_ids=true | all-gather | bytes 73728 | tf_op jit(solution)/shard_map/all_gather | solution.py:55
  86.9 0.7 gather_fusion.2
  87.6 2.0 %collective-permute-start.4 = (f32[16,8,1]{2,1,0:T(8,128)S(1)}, f32[16,8,1]{2,1,0:T(8,128)S(1)}, u32[]{:S(2)}, u32[]{:S(2)}) collective-permute-start(f32[16,8,1]{2,1,0:T(8,128)S(1)} %get-tuple-element.54), channel_id=1, source_target_pairs={{4,0},{8,4},{12,8},{16,12},{20,16},{24,20},{28,24},{0,28},{5,1},{9... | collective-permute-start | bytes 1544 | tf_op jit(solution)/shard_map/ppermute | solution.py:22
  89.6 0.4 collective-permute-start.5
  90.0 0.6 copy.132
  90.6 1.5 %collective-permute-done.4 = f32[16,8,1]{2,1,0:T(8,128)S(1)} collective-permute-done((f32[16,8,1]{2,1,0:T(8,128)S(1)}, f32[16,8,1]{2,1,0:T(8,128)S(1)}, u32[]{:S(2)}, u32[]{:S(2)}) %collective-permute-start.4) | collective-permute-done | bytes 544 | tf_op jit(solution)/shard_map/ppermute | solution.py:22
  92.2 4.4 %collective-permute-done.5 = f32[16,8,1]{2,1,0:T(8,128)S(1)} collective-permute-done((f32[16,8,1]{2,1,0:T(8,128)S(1)}, f32[16,8,1]{2,1,0:T(8,128)S(1)}, u32[]{:S(2)}, u32[]{:S(2)}) %collective-permute-start.5) | collective-permute-done | bytes 544 | tf_op jit(solution)/shard_map/ppermute | solution.py:19
  96.8 1.9 %collective-permute-start.11 = (f32[16,1,128]{2,1,0:T(1,128)S(1)}, f32[16,1,128]{2,1,0:T(1,128)S(1)}, u32[]{:S(2)}, u32[]{:S(2)}) collective-permute-start(f32[16,1,128]{2,1,0:T(1,128)S(1)} %get-tuple-element.52), channel_id=1, source_target_pairs={{0,1},{1,2},{2,3},{4,5},{5,6},{6,7},{8,9},{9,10},{10,11},{12,13},{... | collective-permute-start | bytes 24584 | tf_op jit(solution)/shard_map/ppermute | solution.py:19
  98.7 3.6 %collective-permute-start.10 = (f32[16,1,128]{2,0,1:T(8,128)S(1)}, f32[16,1,128]{2,0,1:T(8,128)S(1)}, u32[]{:S(2)}, u32[]{:S(2)}) collective-permute-start(f32[16,1,128]{2,0,1:T(8,128)S(1)} %bitcast.108), channel_id=1, source_target_pairs={{1,0},{2,1},{3,2},{5,4},{6,5},{7,6},{9,8},{10,9},{11,10},{13,12},{... | collective-permute-start | bytes 24584 | tf_op jit(solution)/shard_map/ppermute | solution.py:22
  102.4 16.6 %all-gather.2 = f32[16,1,1024]{2,1,0:T(1,128)S(1)} all-gather(f32[16,1,128]{2,1,0:T(1,128)S(1)} %get-tuple-element.52), channel_id=4, replica_groups=mesh['ew'=8,'ns'=4] {'ew'}, dimensions={2}, use_global_device_ids=true | all-gather | bytes 73728 | tf_op jit(solution)/shard_map/all_gather | solution.py:55
  119.2 0.7 gather_fusion.3
  119.9 2.0 %collective-permute-start.8 = (f32[16,8,1]{2,1,0:T(8,128)S(1)}, f32[16,8,1]{2,1,0:T(8,128)S(1)}, u32[]{:S(2)}, u32[]{:S(2)}) collective-permute-start(f32[16,8,1]{2,1,0:T(8,128)S(1)} %get-tuple-element.50), channel_id=1, source_target_pairs={{4,0},{8,4},{12,8},{16,12},{20,16},{24,20},{28,24},{0,28},{5,1},{9... | collective-permute-start | bytes 1544 | tf_op jit(solution)/shard_map/ppermute | solution.py:22
  122.0 0.4 collective-permute-start.9
  122.4 2.2 %collective-permute-done.8 = f32[16,8,1]{2,1,0:T(8,128)S(1)} collective-permute-done((f32[16,8,1]{2,1,0:T(8,128)S(1)}, f32[16,8,1]{2,1,0:T(8,128)S(1)}, u32[]{:S(2)}, u32[]{:S(2)}) %collective-permute-start.8) | collective-permute-done | bytes 544 | tf_op jit(solution)/shard_map/ppermute | solution.py:22
  124.5 4.4 %collective-permute-done.9 = f32[16,8,1]{2,1,0:T(8,128)S(1)} collective-permute-done((f32[16,8,1]{2,1,0:T(8,128)S(1)}, f32[16,8,1]{2,1,0:T(8,128)S(1)}, u32[]{:S(2)}, u32[]{:S(2)}) %collective-permute-start.9) | collective-permute-done | bytes 544 | tf_op jit(solution)/shard_map/ppermute | solution.py:19
  129.1 0.6 multiply_add_fusion
  (53 shorter events, 2.1 us)
Async XLA Ops:
  0.6 62.9 %copy-start = (bf16[1,1,4,128,1024]{4,3,2,1,0:T(8,128)(2,1)S(1)}, bf16[1,1,4,128,1024]{4,3,2,1,0:T(8,128)(2,1)}, u32[]{:S(2)}) copy-start(bf16[1,1,4,128,1024]{4,3,2,1,0:T(8,128)(2,1)} %param.24) | copy-start | bytes 3145732
  1.6 61.2 %collective-permute-start.3 = (f32[16,1,128]{2,1,0:T(1,128)S(1)}, f32[16,1,128]{2,1,0:T(1,128)S(1)}, u32[]{:S(2)}, u32[]{:S(2)}) collective-permute-start(f32[16,1,128]{2,1,0:T(1,128)S(1)} %get-tuple-element.60), channel_id=1, source_target_pairs={{0,1},{1,2},{2,3},{4,5},{5,6},{6,7},{8,9},{9,10},{10,11},{12,13},{... | collective-permute-start | bytes 24584 | tf_op jit(solution)/shard_map/ppermute | solution.py:19
  3.5 59.2 %collective-permute-start.2 = (f32[16,1,128]{2,0,1:T(8,128)S(1)}, f32[16,1,128]{2,0,1:T(8,128)S(1)}, u32[]{:S(2)}, u32[]{:S(2)}) collective-permute-start(f32[16,1,128]{2,0,1:T(8,128)S(1)} %bitcast.106), channel_id=1, source_target_pairs={{1,0},{2,1},{3,2},{5,4},{6,5},{7,6},{9,8},{10,9},{11,10},{13,12},{... | collective-permute-start | bytes 24584 | tf_op jit(solution)/shard_map/ppermute | solution.py:22
  8.2 54.6 %collective-permute-start = (f32[16,8,1]{2,1,0:T(8,128)S(1)}, f32[16,8,1]{2,1,0:T(8,128)S(1)}, u32[]{:S(2)}, u32[]{:S(2)}) collective-permute-start(f32[16,8,1]{2,1,0:T(8,128)S(1)} %get-tuple-element.58), channel_id=1, source_target_pairs={{4,0},{8,4},{12,8},{16,12},{20,16},{24,20},{28,24},{0,28},{5,1},{9... | collective-permute-start | bytes 1544 | tf_op jit(solution)/shard_map/ppermute | solution.py:22
  12.8 50.0 %collective-permute-start.1 = (f32[16,8,1]{2,1,0:T(8,128)S(1)}, f32[16,8,1]{2,1,0:T(8,128)S(1)}, u32[]{:S(2)}, u32[]{:S(2)}) collective-permute-start(f32[16,8,1]{2,1,0:T(8,128)S(1)} %get-tuple-element.57), channel_id=1, source_target_pairs={{0,4},{4,8},{8,12},{12,16},{16,20},{20,24},{24,28},{28,0},{1,5},{5... | collective-permute-start | bytes 1544 | tf_op jit(solution)/shard_map/ppermute | solution.py:19
  12.8 0.7 copy-start.6
  34.3 0.7 copy-start.4
  35.7 25.5 %copy-start.1 = (f32[16,8,128]{2,1,0:T(8,128)S(1)}, f32[16,8,128]{2,1,0:T(8,128)}, u32[]{:S(2)}) copy-start(f32[16,8,128]{2,1,0:T(8,128)} %param.17) | copy-start | bytes 196612
  35.7 27.3 %all-to-all-start = ((bf16[8,6,128]{2,1,0:T(8,128)(2,1)}), bf16[8,6,128]{2,1,0:T(8,128)(2,1)S(1)}, u32[]{:S(2)}, u32[]{:S(2)}) async-start(bf16[8,6,128]{2,1,0:T(8,128)(2,1)} %broadcast_select_fusion), calls=%async_computation | async-start | bytes 32768 | tf_op jit(solution)/shard_map/all_to_all | solution.py:38
  61.1 1.7 %copy-start.3 = (f32[16,8,128]{2,1,0:T(8,128)S(1)}, f32[16,8,128]{2,1,0:T(8,128)}, u32[]{:S(2)}) copy-start(f32[16,8,128]{2,1,0:T(8,128)} %param.19) | copy-start | bytes 196612
  61.4 1.5 %copy-start.2 = (f32[2,16,8,128]{3,2,1,0:T(8,128)S(1)}, f32[2,16,8,128]{3,2,1,0:T(8,128)}, u32[]{:S(2)}) copy-start(f32[2,16,8,128]{3,2,1,0:T(8,128)} %param.18) | copy-start | bytes 393220
  63.5 0.7 copy-start.5
  64.4 32.1 %collective-permute-start.7 = (f32[16,1,128]{2,1,0:T(1,128)S(1)}, f32[16,1,128]{2,1,0:T(1,128)S(1)}, u32[]{:S(2)}, u32[]{:S(2)}) collective-permute-start(f32[16,1,128]{2,1,0:T(1,128)S(1)} %get-tuple-element.56), channel_id=1, source_target_pairs={{0,1},{1,2},{2,3},{4,5},{5,6},{6,7},{8,9},{9,10},{10,11},{12,13},{... | collective-permute-start | bytes 24584 | tf_op jit(solution)/shard_map/ppermute | solution.py:19
  66.4 24.3 %collective-permute-start.6 = (f32[16,1,128]{2,0,1:T(8,128)S(1)}, f32[16,1,128]{2,0,1:T(8,128)S(1)}, u32[]{:S(2)}, u32[]{:S(2)}) collective-permute-start(f32[16,1,128]{2,0,1:T(8,128)S(1)} %bitcast.107), channel_id=1, source_target_pairs={{1,0},{2,1},{3,2},{5,4},{6,5},{7,6},{9,8},{10,9},{11,10},{13,12},{... | collective-permute-start | bytes 24584 | tf_op jit(solution)/shard_map/ppermute | solution.py:22
  87.6 4.6 %collective-permute-start.4 = (f32[16,8,1]{2,1,0:T(8,128)S(1)}, f32[16,8,1]{2,1,0:T(8,128)S(1)}, u32[]{:S(2)}, u32[]{:S(2)}) collective-permute-start(f32[16,8,1]{2,1,0:T(8,128)S(1)} %get-tuple-element.54), channel_id=1, source_target_pairs={{4,0},{8,4},{12,8},{16,12},{20,16},{24,20},{28,24},{0,28},{5,1},{9... | collective-permute-start | bytes 1544 | tf_op jit(solution)/shard_map/ppermute | solution.py:22
  89.6 7.0 %collective-permute-start.5 = (f32[16,8,1]{2,1,0:T(8,128)S(1)}, f32[16,8,1]{2,1,0:T(8,128)S(1)}, u32[]{:S(2)}, u32[]{:S(2)}) collective-permute-start(f32[16,8,1]{2,1,0:T(8,128)S(1)} %get-tuple-element.53), channel_id=1, source_target_pairs={{0,4},{4,8},{8,12},{12,16},{16,20},{20,24},{24,28},{28,0},{1,5},{5... | collective-permute-start | bytes 1544 | tf_op jit(solution)/shard_map/ppermute | solution.py:19
  96.8 32.1 %collective-permute-start.11 = (f32[16,1,128]{2,1,0:T(1,128)S(1)}, f32[16,1,128]{2,1,0:T(1,128)S(1)}, u32[]{:S(2)}, u32[]{:S(2)}) collective-permute-start(f32[16,1,128]{2,1,0:T(1,128)S(1)} %get-tuple-element.52), channel_id=1, source_target_pairs={{0,1},{1,2},{2,3},{4,5},{5,6},{6,7},{8,9},{9,10},{10,11},{12,13},{... | collective-permute-start | bytes 24584 | tf_op jit(solution)/shard_map/ppermute | solution.py:19
  98.7 23.6 %collective-permute-start.10 = (f32[16,1,128]{2,0,1:T(8,128)S(1)}, f32[16,1,128]{2,0,1:T(8,128)S(1)}, u32[]{:S(2)}, u32[]{:S(2)}) collective-permute-start(f32[16,1,128]{2,0,1:T(8,128)S(1)} %bitcast.108), channel_id=1, source_target_pairs={{1,0},{2,1},{3,2},{5,4},{6,5},{7,6},{9,8},{10,9},{11,10},{13,12},{... | collective-permute-start | bytes 24584 | tf_op jit(solution)/shard_map/ppermute | solution.py:22
  119.9 4.6 %collective-permute-start.8 = (f32[16,8,1]{2,1,0:T(8,128)S(1)}, f32[16,8,1]{2,1,0:T(8,128)S(1)}, u32[]{:S(2)}, u32[]{:S(2)}) collective-permute-start(f32[16,8,1]{2,1,0:T(8,128)S(1)} %get-tuple-element.50), channel_id=1, source_target_pairs={{4,0},{8,4},{12,8},{16,12},{20,16},{24,20},{28,24},{0,28},{5,1},{9... | collective-permute-start | bytes 1544 | tf_op jit(solution)/shard_map/ppermute | solution.py:22
  122.0 7.0 %collective-permute-start.9 = (f32[16,8,1]{2,1,0:T(8,128)S(1)}, f32[16,8,1]{2,1,0:T(8,128)S(1)}, u32[]{:S(2)}, u32[]{:S(2)}) collective-permute-start(f32[16,8,1]{2,1,0:T(8,128)S(1)} %get-tuple-element.49), channel_id=1, source_target_pairs={{0,4},{4,8},{8,12},{12,16},{16,20},{20,24},{24,28},{28,0},{1,5},{5... | collective-permute-start | bytes 1544 | tf_op jit(solution)/shard_map/ppermute | solution.py:19
where the time goes:
time: 130 us
  blocking collectives  75.3 us (58%)
  starting transfers between devices  29.6 us (23%)
  waiting for transfers between devices  12.5 us (10%)
  local copies, waits for them, and re-layouts  7.6 us (6%)
  between operations  2.26 us (2%)
  other arithmetic  2.04 us (2%)
    all_gather x3, blocking collectives, local(): piece = lax.all_gather(field[:, -1, :], 'ew', axis=1, tiled=True)  54.5 us
    all_gather x1, blocking collectives, local(): lists = lax.all_gather(remap_src, 'ew', axis=1, tiled=True)  20.9 us
    ppermute x6, starting transfers between devices, with_halo(): lax.ppermute(lax.slice_in_dim(block, 0, width, axis=dim), axis, backward)  19.6 us
    ppermute x6, waiting for transfers between devices, with_halo(): lax.ppermute(lax.slice_in_dim(block, block.shape[dim] - width, None, axis...  8.76 us
    ppermute x6, starting transfers between devices, with_halo(): lax.ppermute(lax.slice_in_dim(block, block.shape[dim] - width, None, axis...  6.57 us
    ppermute x6, waiting for transfers between devices, with_halo(): lax.ppermute(lax.slice_in_dim(block, 0, width, axis=dim), axis, backward)  3.71 us
    all_to_all x1, starting transfers between devices, local(): lax.all_to_all(outgoing, 'ew', split_axis=0, concat_axis=0, tiled=True)  3.47 us
  transfers between devices with their start and end apart: 13, of which 4 were waited for; matrix products, arithmetic and copies ran while one was open for 4% of the time, Pallas kernels for 0%

commit v1 on v0

v1 whole, which is shorter than its diff:
```python
import jax
import jax.numpy as jnp
from jax import lax
from jax.experimental import pallas as pl
from jax.experimental.pallas import tpu as pltpu
from jax.sharding import PartitionSpec as P

COEFS = (0.5, -0.3, 0.2, 0.4, -0.25, 0.35)
VMEM = pl.BlockSpec(memory_space=pltpu.VMEM)
SMEM = pl.BlockSpec(memory_space=pltpu.SMEM)
HBM = pl.BlockSpec(memory_space=pltpu.HBM)
PARAMS = pltpu.CompilerParams(vmem_limit_bytes=16 * 1024 * 1024)
F32 = jnp.float32
BF16 = jnp.bfloat16
KINDS = 6
BLOCK = 16


def stencil(t, east, west, north, south, u, v, d):
    return t + d * (east + west + north + south - 4.0 * t) - 0.5 * (u * (east - west) + v * (north - south))


def split(rows, devices):
    each = -(-rows // devices)
    return each, -(-rows // each)


class Place:
    def __init__(self):
        self.count, self.block_rows = lax.axis_size("ew"), lax.axis_size("ns")
        self.devices = self.count * self.block_rows
        self.e, self.n = lax.axis_index("ew"), lax.axis_index("ns")
        self.top = self.block_rows - 1
        self.is_top = self.n == self.top
        self.has_south = self.n > 0
        self.even = lax.rem(self.n, 2) == 0
        self.east = lax.rem(self.e + 1, self.count)
        self.west = lax.rem(self.e + self.count - 1, self.count)
        self.above = jnp.minimum(self.n + 1, self.top)
        self.below = jnp.maximum(self.n - 1, 0)

    def slot(self, e, n):
        return e * self.block_rows + n


def fill(size, rows):
    parts, at = [], 0
    for index in sorted(rows):
        if index > at:
            parts.append(jnp.zeros((index - at, size), F32))
        parts.append(rows[index])
        at = index + 1
    if at < size:
        parts.append(jnp.zeros((size - at, size), F32))
    return jnp.concatenate(parts, axis=0)


def turn(field):
    return field.reshape(field.shape[0] * field.shape[1], field.shape[2]).T


def shifted(field, axis, back):
    size = field.shape[axis]
    return pltpu.roll(field, size - 1 if back else 1, axis)


def first_kernel(
    mask_ref, partner_ref, theta_hbm, vel_hbm, diff_hbm, atm_hbm, weights_hbm,
    out_ref, near_ref, far_ref, theta_ref, coef_ref, weights_ref,
    atm_ref, bulk_ref, sems,
):
    here = Place()
    copies = [
        pltpu.make_async_copy(theta_hbm, theta_ref, sems.at[0]),
        pltpu.make_async_copy(vel_hbm, coef_ref.at[pl.ds(0, 2)], sems.at[1]),
        pltpu.make_async_copy(diff_hbm, coef_ref.at[2], sems.at[2]),
        pltpu.make_async_copy(atm_hbm, atm_ref, sems.at[3]),
        pltpu.make_async_copy(weights_hbm, weights_ref, sems.at[4]),
    ]
    for copy in copies:
        copy.start()
    for copy in copies[:4]:
        copy.wait()
    levels, rows, cols = theta_ref.shape
    wet = mask_ref[0, 0].astype(F32)
    t = theta_ref[...]
    u, v, d = wet * coef_ref[0], wet * coef_ref[1], wet * coef_ref[2]
    coef_ref[0], coef_ref[1], coef_ref[2] = u, v, d
    ahead = stencil(
        t, shifted(t, 2, True), shifted(t, 2, False), shifted(t, 1, True), shifted(t, 1, False), u, v, d
    )
    last = rows - 1
    for kind, (field, row) in enumerate(((t, 0), (t, 1), (ahead, 1), (u, 0), (v, 0), (d, 0))):
        low, high = field[:, row, :], field[:, last - row, :]
        near_ref[kind] = jnp.where(here.even, high, low)
        far_ref[kind] = jnp.where(here.even, low, high)
        bulk_ref[pl.ds(kind * levels, levels), :] = high
    turned, across = turn(t), [turn(u), turn(v), turn(d)]
    lane = lax.broadcasted_iota(jnp.int32, (1, cols), 1)
    second = jnp.where(lane == 0, partner_ref[0].astype(F32), turned[1:2])
    columns = [turned[0:1], second, turned[cols - 2 : cols - 1], turned[cols - 1 : cols]]
    atm = atm_ref[...].astype(F32)
    at = 7 + atm.shape[0]
    rest = jnp.zeros((BLOCK - at, cols), F32)
    to_west = jnp.concatenate(columns + [part[0:1] for part in across] + [atm, rest], axis=0)
    to_east = jnp.concatenate(columns + [part[cols - 1 : cols] for part in across] + [atm, rest], axis=0)
    line = lax.broadcasted_iota(jnp.int32, (BLOCK, cols), 0)
    each, holders = split(KINDS * levels, here.devices)
    for target in range(here.devices):
        block = jnp.where(target // here.block_rows == here.east, to_east, to_west)
        if target < holders:
            for k in range(each):
                piece = bulk_ref[pl.ds(k * holders + target, 1), :]
                block = jnp.where(line == at + k, piece, block)
        out_ref[target] = block.astype(BF16)
    copies[4].wait()


def middle_kernel(
    mask_ref, partner_ref, src_ref, theta_ref, coef_ref, weights_ref, recv_ref, near_ref, far_ref,
    flux_ref, force_ref, next_ref, out_ref,
):
    here = Place()
    levels, rows, cols = theta_ref.shape
    fields = flux_ref.shape[0]
    wet = mask_ref[0, 0].astype(F32)

    total = None
    for pair in range(weights_ref.shape[0]):
        block = recv_ref[here.slot(src_ref[0, 0, pair], here.n)][7 : 7 + fields]
        term = jnp.dot(block, weights_ref[pair], preferred_element_type=F32)
        total = term if total is None else total + term
    force = jnp.zeros((rows, cols), F32)
    for k in range(fields):
        grid = jnp.concatenate([total[k : k + 1, r * cols : (r + 1) * cols] for r in range(rows)], axis=0)
        flux_ref[k] = grid
        force = force + COEFS[k] * grid
    force = wet * (0.1 * force)
    force_ref[...] = force

    t = theta_ref[...]
    lane = lax.broadcasted_iota(jnp.int32, t.shape, 2)
    line = lax.broadcasted_iota(jnp.int32, t.shape, 1)
    level = lax.broadcasted_iota(jnp.int32, t.shape, 0)
    from_west = recv_ref[here.slot(here.west, here.n)].astype(F32)
    from_east = recv_ref[here.slot(here.east, here.n)].astype(F32)
    folded = recv_ref[here.slot(partner_ref[0], here.n)].astype(F32)
    sides = fill(cols, {0: from_west[3:4], cols - 1: from_east[0:1]}).T.reshape(t.shape)
    corner = fill(cols, {0: folded[3:4], 1: folded[2:3], cols - 2: folded[1:2], cols - 1: folded[0:1]})
    corner = corner.T.reshape(t.shape)[:, rows - 1, :]
    above = jnp.where(here.is_top, corner, jnp.where(here.even, near_ref[0], far_ref[0]))
    below = jnp.where(here.has_south, jnp.where(here.even, far_ref[0], near_ref[0]), 0.0)
    east = jnp.where(lane == cols - 1, sides, shifted(t, 2, True))
    west = jnp.where(lane == 0, sides, shifted(t, 2, False))
    north = jnp.where(line == rows - 1, above[:, None, :], shifted(t, 1, True))
    south = jnp.where(line == 0, below[:, None, :], shifted(t, 1, False))
    t = stencil(t, east, west, north, south, coef_ref[0], coef_ref[1], coef_ref[2])
    t = t + jnp.where(level == 0, force[None], 0.0)
    next_ref[...] = t

    each, _ = split(KINDS * levels, here.devices)
    at = 7 + fields
    held = [recv_ref[here.slot(s, here.top)].astype(F32) for s in range(here.count)]
    partners = jnp.concatenate([block[1:2] for block in held], axis=0)[:, 0:1]
    routed = []
    for k in range(each):
        pick = jnp.zeros((here.count, cols), F32)
        for s in range(here.count):
            pick = jnp.where(partners == float(s), held[s][at + k : at + k + 1], pick)
        routed.append(pick)

    turned = turn(t)
    columns = [turned[0:1], turned[1:2], turned[cols - 2 : cols - 1], turned[cols - 1 : cols]]
    across = jnp.concatenate([force, jnp.zeros((cols - rows, cols), F32)], axis=0).T
    high = [force[rows - 1 : rows], force[rows - 2 : rows - 1]]
    rest = [jnp.zeros((BLOCK - 7, cols), F32)]
    low = force[0:1], force[1:2]
    line = lax.broadcasted_iota(jnp.int32, (BLOCK, cols), 0)
    base = jnp.concatenate(columns + high + [across[0:1]] + rest, axis=0)
    to_east = jnp.where(line == 6, across[cols - 1 : cols], base)
    to_below = jnp.where(line == 4, low[0], jnp.where(line == 5, low[1], base))
    for target in range(here.devices):
        e, n = target // here.block_rows, target % here.block_rows
        block = jnp.where(n == here.n - 1, to_below, jnp.where(e == here.east, to_east, base))
        for k in range(each):
            block = jnp.where(line == 7 + k, routed[k][e : e + 1], block)
        out_ref[target] = block.astype(BF16)


def last_kernel(
    partner_ref, theta_ref, coef_ref, next_ref, force_ref, first_ref, second_ref, near_ref, far_ref, result_ref
):
    here = Place()
    levels, rows, cols = theta_ref.shape
    last = rows - 1
    partner = partner_ref[0]

    def got(e, n):
        return second_ref[here.slot(e, n)].astype(F32)

    each, holders = split(KINDS * levels, here.devices)
    bulk = [second_ref[i].astype(F32)[7 : 7 + each] for i in range(holders)]
    bulk = jnp.concatenate([part[k : k + 1] for k in range(each) for part in bulk], axis=0)
    mirror = cols - 1 - lax.broadcasted_iota(jnp.int32, (KINDS * levels, cols), 1)
    bulk = jnp.take_along_axis(bulk[: KINDS * levels], mirror, axis=1)
    north, south = [], []
    for kind in range(KINDS):
        fold = bulk[kind * levels : (kind + 1) * levels]
        fold = -fold if kind in (3, 4) else fold
        near, far = near_ref[kind], far_ref[kind]
        north.append(jnp.where(here.is_top, fold, jnp.where(here.even, near, far)))
        south.append(jnp.where(here.has_south, jnp.where(here.even, far, near), 0.0))

    west, east = got(here.west, here.n), got(here.east, here.n)
    over, under = got(here.e, here.above), got(here.e, here.below)
    fold = got(partner, here.n)
    fold_east = got(lax.rem(partner + 1, here.count), here.n)
    fold_west = got(lax.rem(partner + here.count - 1, here.count), here.n)
    over_west, over_east = got(here.west, here.above), got(here.east, here.above)
    under_west, under_east = got(here.west, here.below), got(here.east, here.below)
    is_top, has_south = here.is_top, here.has_south
    ends = fill(
        cols,
        {
            0: jnp.where(is_top, fold[3:4], over[0:1]),
            1: under[0:1],
            2: jnp.where(is_top, fold_east[0:1], over_west[3:4]),
            3: under_west[3:4],
            cols - 4: under_east[0:1],
            cols - 3: jnp.where(is_top, fold_west[3:4], over_east[0:1]),
            cols - 2: under[3:4],
            cols - 1: jnp.where(is_top, fold[0:1], over[3:4]),
        },
    ).T.reshape(theta_ref.shape)
    lane = lax.broadcasted_iota(jnp.int32, (levels, cols), 1)
    level = lax.broadcasted_iota(jnp.int32, (levels, cols), 0)

    def capped(row, values, lanes):
        low = pltpu.roll(values, cols - lanes, 1) if lanes else values
        high = pltpu.roll(values, lanes, 1) if lanes else values
        return jnp.where(lane == 0, low, jnp.where(lane == cols - 1, high, row))

    def forced(row, force):
        return row + jnp.where(level == 0, force, 0.0)

    north_ends = jnp.where(is_top, ends[:, last, :], ends[:, 0, :])
    north_inner = jnp.where(is_top, ends[:, last - 1, :], ends[:, 1, :])
    south_ends, south_inner = ends[:, last, :], ends[:, last - 1, :]
    flip = cols - 1 - lax.broadcasted_iota(jnp.int32, (8, cols), 1)
    flipped = jnp.take_along_axis(fold[0:8], flip, axis=1)
    north_force = [jnp.where(is_top, flipped[k : k + 1], over[k : k + 1]) for k in (4, 5)]
    south_force = [under[4:5], under[5:6]]
    t0 = theta_ref[...]

    def rim(rows_of, inside, outward, force, edge, inner, at):
        edge_row = stencil(
            rows_of[0], shifted(rows_of[0], 1, True), shifted(rows_of[0], 1, False),
            rows_of[1] if outward else inside, inside if outward else rows_of[1], *rows_of[3:],
        )
        return capped(forced(edge_row, force[0]), edge, at), capped(forced(rows_of[2], force[1]), inner, at)

    north_one, north_two = rim(north, t0[:, last, :], True, north_force, north_ends, north_inner, 0)
    south_one, south_two = rim(south, t0[:, 0, :], False, south_force, south_ends, south_inner, 1)
    south_one, south_two = jnp.where(has_south, south_one, 0.0), jnp.where(has_south, south_two, 0.0)
    u, v, d = coef_ref[0], coef_ref[1], coef_ref[2]
    shape = t0.shape
    wide = lax.broadcasted_iota(jnp.int32, shape, 2)
    line = lax.broadcasted_iota(jnp.int32, shape, 1)
    force = jnp.where(lax.broadcasted_iota(jnp.int32, shape, 0) == 0, force_ref[...][None], 0.0)
    missing = (line == last) & (wide >= 2) & (wide < cols - 2) & is_top
    t = next_ref[...]
    t = t + jnp.where(missing, (d - 0.5 * v) * north[0][:, None, :], 0.0)

    def outer(row, beyond, inside, outward, rows_of, force_row, diagonal, lanes):
        low, high = pltpu.roll(diagonal, cols - lanes, 1), pltpu.roll(diagonal, lanes, 1)
        result = stencil(
            row, jnp.where(lane == cols - 1, high, shifted(row, 1, True)),
            jnp.where(lane == 0, low, shifted(row, 1, False)),
            beyond if outward else inside, inside if outward else beyond, *rows_of[3:],
        )
        return forced(result, force_row)

    north_next = outer(north_one, north_two, t[:, last, :], True, north, north_force[0], north_ends, 2)
    south_next = outer(south_one, south_two, t[:, 0, :], False, south, south_force[0], south_ends, 3)
    south_next = jnp.where(has_south, south_next, 0.0)

    turned = turn(t)
    first_west = first_ref[here.slot(here.west, here.n)].astype(F32)
    first_east = first_ref[here.slot(here.east, here.n)].astype(F32)
    top_west, top_east = jnp.zeros((1, cols), F32), jnp.zeros((1, cols), F32)
    for s in range(here.count):
        block = got(s, here.n)
        top_west = jnp.where(first_west[1:2, 0:1] == float(s), block[0:1], top_west)
        top_east = jnp.where(first_east[1:2, 0:1] == float(s), block[3:4], top_east)

    def pair(low, high):
        return jnp.concatenate([low, high, jnp.zeros((6, cols), F32)], axis=0)

    side = pair(west[3:4], east[0:1])
    place = lax.rem(lax.broadcasted_iota(jnp.int32, (8, cols), 1), rows)
    corner = jnp.where(
        is_top, pair(top_west, top_east), pltpu.roll(pair(over_west[3:4], over_east[0:1]), rows - 1, 1)
    )
    side_north = jnp.where(place == last, corner, shifted(side, 1, True))
    corner = pltpu.roll(pair(under_west[3:4], under_east[0:1]), cols - rows + 1, 1)
    side_south = jnp.where(place == 0, jnp.where(has_south, corner, 0.0), shifted(side, 1, False))
    side_next = stencil(
        side, pair(turned[0:1], east[1:2]), pair(west[2:3], turned[cols - 1 : cols]), side_north, side_south,
        *[pair(first_west[k : k + 1], first_east[k : k + 1]) for k in (4, 5, 6)],
    ) + pair(west[6:7], east[6:7])

    def advance(t, sides, above, below):
        return force + stencil(
            t,
            jnp.where(wide == cols - 1, sides, shifted(t, 2, True)),
            jnp.where(wide == 0, sides, shifted(t, 2, False)),
            jnp.where(line == last, above[:, None, :], shifted(t, 1, True)),
            jnp.where(line == 0, below[:, None, :], shifted(t, 1, False)),
            u, v, d,
        )

    def columns(low, high):
        return fill(cols, {0: low, cols - 1: high}).T.reshape(shape)

    t = advance(t, columns(west[3:4], east[0:1]), north_one, south_one)
    result_ref[...] = advance(t, columns(side_next[0:1], side_next[1:2]), north_next, south_next)


def exchange(blocks):
    return lax.all_to_all(blocks, ("ew", "ns"), split_axis=0, concat_axis=0, tiled=True)


def swap(rows, first):
    pairs = [(i, i + 1) for i in range(first, lax.axis_size("ns") - 1, 2)]
    return lax.ppermute(rows, "ns", pairs + [(b, a) for a, b in pairs])


def local(theta, velocity, diffusivity, land_mask, fold_partner, atm_flux, remap_src, remap_weights):
    levels, rows, cols = theta.shape
    fields = atm_flux.shape[2]
    shape = jax.ShapeDtypeStruct
    devices = lax.axis_size("ew") * lax.axis_size("ns")
    whole = shape(theta.shape, F32)
    blocks = shape((devices, BLOCK, cols), BF16)
    edge = shape((KINDS, levels, cols), F32)
    weights = remap_weights[0, 0]
    out, near, far, field, coef, weights = pl.pallas_call(
        first_kernel,
        out_shape=(blocks, edge, edge, whole, shape((3,) + theta.shape, F32), shape(weights.shape, BF16)),
        in_specs=[SMEM] * 2 + [HBM] * 5,
        out_specs=(VMEM,) * 6,
        scratch_shapes=[
            pltpu.VMEM((fields, cols), BF16),
            pltpu.VMEM((KINDS * levels, cols), F32),
            pltpu.SemaphoreType.DMA((5,)),
        ],
        compiler_params=PARAMS,
        name="first",
    )(land_mask, fold_partner, theta, velocity, diffusivity, atm_flux[0, 0], weights)
    first = exchange(out)
    near, far = swap(near, 0), swap(far, 1)
    flux, force, after, out = pl.pallas_call(
        middle_kernel,
        out_shape=(shape((fields, rows, cols), F32), shape((rows, cols), F32), whole, blocks),
        in_specs=[SMEM] * 3 + [VMEM] * 6,
        out_specs=(VMEM,) * 4,
        compiler_params=PARAMS,
        name="middle",
    )(land_mask, fold_partner, remap_src, field, coef, weights, first, near, far)
    second = exchange(out)
    field = pl.pallas_call(
        last_kernel,
        out_shape=whole,
        in_specs=[SMEM] + [VMEM] * 8,
        out_specs=VMEM,
        compiler_params=PARAMS,
        name="last",
    )(fold_partner, field, coef, after, force, first, second, near, far)
    return field, flux.reshape(1, 1, fields, rows * cols)


def solution(mesh):
    return jax.shard_map(
        local,
        mesh=mesh,
        in_specs=(
            P(None, "ns", "ew"),
            P(None, None, "ns", "ew"),
            P(None, "ns", "ew"),
            P("ns", "ew"),
            P("ew"),
            P("ns", "ew", None, None),
            P("ns", "ew", None),
            P("ns", "ew", None, None, None),
        ),
        out_specs=(P(None, "ns", "ew"), P("ns", "ew", None, None)),
        check_vma=False,
    )
```

time: 130 us -> 38 us (0.29)
  the two profiles are of different devices: /device:TPU:2 before, /device:TPU:0 now
where the time goes in v1:
time: 38 us; the launch traced here: 37.6 us
  blocking collectives  11.2 us (29%)
  starting transfers between devices  8.27 us (22%)
  waiting for transfers between devices  7.25 us (19%)
  local copies, waits for them, and re-layouts  5.14 us (14%)
  Pallas kernels  3.7 us (10%)
  between operations  1.96 us (5%)
    all_to_all x1, blocking collectives, exchange(): lax.all_to_all(blocks, ('ew', 'ns'), split_axis=0, concat_axis=0, tiled=T...  11.2 us
    all_to_all x1, starting transfers between devices, exchange(): lax.all_to_all(blocks, ('ew', 'ns'), split_axis=0, concat_axis=0, tiled=T...  7.3 us
    all_to_all x1, waiting for transfers between devices, exchange(): lax.all_to_all(blocks, ('ew', 'ns'), split_axis=0, concat_axis=0, tiled=T...  6.93 us
    unnamed x12, local copies, waits for them, and re-layouts  5.14 us
    pallas_call x1, Pallas kernels, local(): pl.pallas_call(middle_kernel, out_shape=(shape((fields, rows, cols), F32)...  1.41 us
    pallas_call x1, Pallas kernels, local(): pl.pallas_call(first_kernel, out_shape=(blocks, edge, edge, whole, shape(...  1.25 us
    pallas_call x1, Pallas kernels, local(): pl.pallas_call(last_kernel, out_shape=whole, in_specs=[SMEM] + [VMEM] * 8...  1.03 us
    ppermute x2, starting transfers between devices, swap(): return lax.ppermute(rows, 'ns', pairs + [(b, a) for a, b in pairs])  0.97 us
  transfers between devices with their start and end apart: 3, of which 2 were waited for; matrix products, arithmetic and copies ran while one was open for 0% of the time, Pallas kernels for 0%

profile of v1, /device:TPU:0, one launch (start us, length us, event | category | flops | bytes accessed | tf_op | source)
XLA Modules:
  0.0 37.6 jit_solution(3790187155784078233)
XLA Ops:
  1.9 0.0 copy-start.4
  1.9 0.7 %copy-done.4 = bf16[1,1,6,128]{3,2,1,0:T(8,128)(2,1)S(1)} copy-done((bf16[1,1,6,128]{3,2,1,0:T(8,128)(2,1)S(1)}, bf16[1,1,6,128]{3,2,1,0:T(8,128)(2,1)}, u32[]{:S(2)}) %copy-start.4) | copy-done | bytes 1560
  2.6 0.0 copy-start
  2.6 1.2 %copy-done = bf16[1,1,4,128,1024]{4,3,2,1,0:T(8,128)(2,1)S(1)} copy-done((bf16[1,1,4,128,1024]{4,3,2,1,0:T(8,128)(2,1)S(1)}, bf16[1,1,4,128,1024]{4,3,2,1,0:T(8,128)(2,1)}, u32[]{:S(2)}) %copy-start) | copy-done | bytes 1048600
  3.8 0.0 copy-start.1
  3.8 0.9 %copy-done.1 = f32[2,16,8,128]{3,2,1,0:T(8,128)S(1)} copy-done((f32[2,16,8,128]{3,2,1,0:T(8,128)S(1)}, f32[2,16,8,128]{3,2,1,0:T(8,128)}, u32[]{:S(2)}) %copy-start.1) | copy-done | bytes 131096
  4.7 0.0 copy-start.2
  4.7 0.8 %copy-done.2 = f32[16,8,128]{2,1,0:T(8,128)S(1)} copy-done((f32[16,8,128]{2,1,0:T(8,128)S(1)}, f32[16,8,128]{2,1,0:T(8,128)}, u32[]{:S(2)}) %copy-start.2) | copy-done | bytes 65560
  5.6 0.0 copy-start.3
  5.6 0.8 %copy-done.3 = f32[16,8,128]{2,1,0:T(8,128)S(1)} copy-done((f32[16,8,128]{2,1,0:T(8,128)S(1)}, f32[16,8,128]{2,1,0:T(8,128)}, u32[]{:S(2)}) %copy-start.3) | copy-done | bytes 65560
  6.4 1.3 %first.1 = (bf16[32,16,128]{2,1,0:T(8,128)(2,1)}, f32[6,16,128]{2,1,0:T(8,128)S(1)}, f32[6,16,128]{2,1,0:T(8,128)S(1)}, f32[16,8,128]{2,1,0:T(8,128)S(1)}, f32[3...) custom-call(s32[1,1]{1,0:T(1,128)S(6)} %copy.12.mask_ref, s32[1]{0:T(128)S(6)} %copy.13.partner_ref, ...), custom_call_target="tpu_custom_call" | custom-call | tf_op jit(solution)/shard_map/first/pallas_call | solution.py:347
  7.7 7.3 %all-to-all-start = ((bf16[32,16,128]{2,1,0:T(8,128)(2,1)}), bf16[32,16,128]{2,1,0:T(8,128)(2,1)S(1)}, u32[]{:S(2)}, u32[]{:S(2)}) async-start(bf16[32,16,128]{2,1,0:T(8,128)(2,1)} %get-tuple-element.15), calls=%async_computation | async-start | bytes 262144 | tf_op jit(solution)/shard_map/all_to_all | solution.py:330
  15.0 0.3 collective-permute-start
  15.3 0.7 %collective-permute-start.1 = (f32[6,16,128]{2,1,0:T(8,128)S(1)}, f32[6,16,128]{2,1,0:T(8,128)S(1)}, u32[]{:S(2)}, u32[]{:S(2)}) collective-permute-start(f32[6,16,128]{2,1,0:T(8,128)S(1)} %get-tuple-element.17), channel_id=1, source_target_pairs={{1,2},{2,1},{5,6},{6,5},{9,10},{10,9},{13,14},{14,13},{17,18},{18,... | collective-permute-start | bytes 147464 | tf_op jit(solution)/shard_map/ppermute | solution.py:335
  16.0 0.3 collective-permute-done.near_ref
  16.3 0.0 collective-permute-done.1.far_ref
  16.3 6.9 %all-to-all-done.recv_ref.first_ref = bf16[32,16,128]{2,1,0:T(8,128)(2,1)S(1)} async-done(((bf16[32,16,128]{2,1,0:T(8,128)(2,1)}), bf16[32,16,128]{2,1,0:T(8,128)(2,1)S(1)}, u32[]{:S(2)}, u32[]{:S(2)}) %all-to-all-start) | async-done | bytes 131104 | tf_op jit(solution)/shard_map/all_to_all | solution.py:330
  23.2 0.0 copy-start.5
  23.2 0.7 %copy-done.5 = s32[1,1,4]{2,1,0:T(1,128)S(1)} copy-done((s32[1,1,4]{2,1,0:T(1,128)S(1)}, s32[1,1,4]{2,1,0:T(1,128)}, u32[]{:S(2)}) %copy-start.5) | copy-done | bytes 40
  23.9 1.4 %middle.1 = (f32[6,8,128]{2,1,0:T(8,128)}, f32[8,128]{1,0:T(8,128)S(1)}, f32[16,8,128]{2,1,0:T(8,128)S(1)}, bf16[32,16,128]{2,1,0:T(8,128)(2,1)S(1)}) custom-call(s32[1,1]{1,0:T(1,128)S(6)} %copy.12.mask_ref, s32[1]{0:T(128)S(6)} %copy.13.partner_ref, s32[1,1,4]{2,1,0:T(1,128)S(1)} %copy-done.5, f32[16,8,128]{2,1,0:T(8,128)S(1)} %get-tuple-element.12.theta_ref, ...), custom_call_target="tpu_custom_call" | custom-call | tf_op jit(solution)/shard_map/middle/pallas_call | solution.py:362
  25.3 11.2 %all_to_all.10.second_ref = bf16[32,16,128]{2,1,0:T(8,128)(2,1)S(1)} all-to-all(bf16[32,16,128]{2,1,0:T(8,128)(2,1)S(1)} %get-tuple-element.20), channel_id=1, replica_groups=mesh['ew'=8,'ns'=4] {'ew','ns'}, dimensions={0} | all-to-all | bytes 262144 | tf_op jit(solution)/shard_map/all_to_all | solution.py:330
  36.5 1.0 %last.1 = f32[16,8,128]{2,1,0:T(8,128)} custom-call(s32[1]{0:T(128)S(6)} %copy.13.partner_ref, f32[16,8,128]{2,1,0:T(8,128)S(1)} %get-tuple-element.12.theta_ref, f32[3,16,8,128]{3,2,1,0:T(8,128)S(1)} %get-tuple-element.13.coef_ref, f32[16,8,128]{2,1,0:T(8,128)S(1)} %get-tuple-element.18.next_ref, f32[8,128]{1,0:T(8,128)S(1)} %get-tuple-element.19.force_ref, ...), custom_call_target="tpu_custom_call" | custom-call | tf_op jit(solution)/shard_map/last/pallas_call | solution.py:371
Async XLA Ops:
  1.9 0.7 %copy-start.4 = (bf16[1,1,6,128]{3,2,1,0:T(8,128)(2,1)S(1)}, bf16[1,1,6,128]{3,2,1,0:T(8,128)(2,1)}, u32[]{:S(2)}) copy-start(bf16[1,1,6,128]{3,2,1,0:T(8,128)(2,1)} %param.13) | copy-start | bytes 4612
  2.6 1.2 %copy-start = (bf16[1,1,4,128,1024]{4,3,2,1,0:T(8,128)(2,1)S(1)}, bf16[1,1,4,128,1024]{4,3,2,1,0:T(8,128)(2,1)}, u32[]{:S(2)}) copy-start(bf16[1,1,4,128,1024]{4,3,2,1,0:T(8,128)(2,1)} %param.15) | copy-start | bytes 3145732
  3.8 0.9 %copy-start.1 = (f32[2,16,8,128]{3,2,1,0:T(8,128)S(1)}, f32[2,16,8,128]{3,2,1,0:T(8,128)}, u32[]{:S(2)}) copy-start(f32[2,16,8,128]{3,2,1,0:T(8,128)} %vel_hbm.1) | copy-start | bytes 393220
  4.7 0.8 %copy-start.2 = (f32[16,8,128]{2,1,0:T(8,128)S(1)}, f32[16,8,128]{2,1,0:T(8,128)}, u32[]{:S(2)}) copy-start(f32[16,8,128]{2,1,0:T(8,128)} %theta_hbm.1) | copy-start | bytes 196612
  5.6 0.8 %copy-start.3 = (f32[16,8,128]{2,1,0:T(8,128)S(1)}, f32[16,8,128]{2,1,0:T(8,128)}, u32[]{:S(2)}) copy-start(f32[16,8,128]{2,1,0:T(8,128)} %diff_hbm.1) | copy-start | bytes 196612
  7.7 15.5 %all-to-all-start = ((bf16[32,16,128]{2,1,0:T(8,128)(2,1)}), bf16[32,16,128]{2,1,0:T(8,128)(2,1)S(1)}, u32[]{:S(2)}, u32[]{:S(2)}) async-start(bf16[32,16,128]{2,1,0:T(8,128)(2,1)} %get-tuple-element.15), calls=%async_computation | async-start | bytes 262144 | tf_op jit(solution)/shard_map/all_to_all | solution.py:330
  15.0 1.3 %collective-permute-start = (f32[6,16,128]{2,1,0:T(8,128)S(1)}, f32[6,16,128]{2,1,0:T(8,128)S(1)}, u32[]{:S(2)}, u32[]{:S(2)}) collective-permute-start(f32[6,16,128]{2,1,0:T(8,128)S(1)} %get-tuple-element.16), channel_id=1, source_target_pairs={{0,1},{2,3},{1,0},{3,2},{4,5},{6,7},{5,4},{7,6},{8,9},{10,11},{9,8... | collective-permute-start | bytes 147464 | tf_op jit(solution)/shard_map/ppermute | solution.py:335
  15.3 1.0 %collective-permute-start.1 = (f32[6,16,128]{2,1,0:T(8,128)S(1)}, f32[6,16,128]{2,1,0:T(8,128)S(1)}, u32[]{:S(2)}, u32[]{:S(2)}) collective-permute-start(f32[6,16,128]{2,1,0:T(8,128)S(1)} %get-tuple-element.17), channel_id=1, source_target_pairs={{1,2},{2,1},{5,6},{6,5},{9,10},{10,9},{13,14},{14,13},{17,18},{18,... | collective-permute-start | bytes 147464 | tf_op jit(solution)/shard_map/ppermute | solution.py:335
  23.2 0.7 %copy-start.5 = (s32[1,1,4]{2,1,0:T(1,128)S(1)}, s32[1,1,4]{2,1,0:T(1,128)}, u32[]{:S(2)}) copy-start(s32[1,1,4]{2,1,0:T(1,128)} %src_ref.1) | copy-start | bytes 52

commit v2 on v1

v2 whole, which is shorter than its diff:
```python
import jax
import jax.numpy as jnp
from jax import lax
from jax.experimental import pallas as pl
from jax.experimental.pallas import tpu as pltpu
from jax.sharding import PartitionSpec as P

COEFS = (0.5, -0.3, 0.2, 0.4, -0.25, 0.35)
VMEM = pl.BlockSpec(memory_space=pltpu.VMEM)
SMEM = pl.BlockSpec(memory_space=pltpu.SMEM)
HBM = pl.BlockSpec(memory_space=pltpu.HBM)
PARAMS = pltpu.CompilerParams(vmem_limit_bytes=16 * 1024 * 1024)
F32 = jnp.float32
BF16 = jnp.bfloat16
KINDS = 6
BLOCK, TILE = 16, 8
FORCE_SLOT, WET_SLOT = 4, 5


def tendency(t, east, west, north, south, u, v, d):
    return d * (east + west + north + south - 4.0 * t) - 0.5 * (u * (east - west) + v * (north - south))


def stencil(t, *others):
    return t + tendency(t, *others)


class Place:
    def __init__(self):
        self.count, self.block_rows = lax.axis_size("ew"), lax.axis_size("ns")
        self.devices = self.count * self.block_rows
        self.e, self.n = lax.axis_index("ew"), lax.axis_index("ns")
        self.top = self.block_rows - 1
        self.is_top = self.n == self.top
        self.has_south = self.n > 0
        self.even = lax.rem(self.n, 2) == 0
        self.east = lax.rem(self.e + 1, self.count)
        self.west = lax.rem(self.e + self.count - 1, self.count)
        self.above = jnp.minimum(self.n + 1, self.top)
        self.below = jnp.maximum(self.n - 1, 0)
        self.pair = jnp.where(self.even, self.n + 1, self.n - 1)
        self.other = jnp.where(self.even, self.below, self.above)
        self.half = self.count // 2

    def slot(self, e, n):
        return e * self.block_rows + n


def fill(size, rows):
    parts, at = [], 0
    for index in sorted(rows):
        if index > at:
            parts.append(jnp.zeros((index - at, size), F32))
        parts.append(rows[index])
        at = index + 1
    if at < size:
        parts.append(jnp.zeros((size - at, size), F32))
    return jnp.concatenate(parts, axis=0)


def turn(field):
    return field.reshape(field.shape[0] * field.shape[1], field.shape[2]).T


def shifted(field, axis, back):
    size = field.shape[axis]
    return pltpu.roll(field, size - 1 if back else 1, axis)


def first_kernel(
    mask_hbm, partner_hbm, src_hbm, theta_hbm, vel_hbm, diff_hbm, atm_hbm, weights_hbm,
    out_ref, theta_ref, coef_ref, weights_ref, mask_ref, partner_ref, src_ref,
    atm_ref, bulk_ref, sems,
):
    here = Place()
    pairs = [
        (theta_hbm, theta_ref), (vel_hbm, coef_ref.at[pl.ds(0, 2)]), (diff_hbm, coef_ref.at[2]),
        (atm_hbm, atm_ref), (partner_hbm, partner_ref), (mask_hbm, mask_ref), (src_hbm, src_ref),
        (weights_hbm, weights_ref),
    ]
    copies = [pltpu.make_async_copy(a, b, sems.at[i]) for i, (a, b) in enumerate(pairs)]
    for copy in copies:
        copy.start()
    for copy in copies[:5]:
        copy.wait()
    levels, rows, cols = theta_ref.shape
    t = theta_ref[...]
    u, v, d = coef_ref[0], coef_ref[1], coef_ref[2]
    tend = tendency(
        t, shifted(t, 2, True), shifted(t, 2, False), shifted(t, 1, True), shifted(t, 1, False), u, v, d
    )
    last = rows - 1
    tiles = levels // TILE
    each = KINDS * tiles
    for kind, (field, row) in enumerate(((t, 0), (t, 1), (tend, 1), (u, 0), (v, 0), (d, 0))):
        high, low = field[:, last - row, :], field[:, row, :]
        bulk_ref[pl.ds(kind * tiles, tiles)] = high.reshape(tiles, TILE, cols)
        bulk_ref[pl.ds(each + kind * tiles, tiles)] = low.reshape(tiles, TILE, cols)
    turned, across = turn(t), [turn(u), turn(v), turn(d)]
    lane = lax.broadcasted_iota(jnp.int32, (1, cols), 1)
    second = jnp.where(lane == 1, partner_ref[0, 0].astype(F32), turned[1:2])
    columns = [turned[0:1], second, turned[cols - 2 : cols - 1], turned[cols - 1 : cols]]
    atm = atm_ref[...].astype(F32)
    begin = jnp.concatenate(columns + [atm[: TILE - 4]], axis=0)
    used = atm.shape[0] - (TILE - 4) + 3
    rest = [jnp.zeros((TILE - used, cols), F32)]
    base = jnp.concatenate([atm[TILE - 4 :]] + [part[0:1] for part in across] + rest, axis=0)
    to_east = jnp.concatenate([atm[TILE - 4 :]] + [part[cols - 1 : cols] for part in across] + rest, axis=0)
    for target in range(here.devices):
        e, n = target // here.block_rows, target % here.block_rows
        order = (e % here.half) * (here.block_rows - 1) + n - (here.n < n).astype(jnp.int32)
        upward = here.even if e < here.half else jnp.logical_not(here.even)
        tile = bulk_ref[jnp.where(upward, 0, each) + jnp.minimum(order, each - 1)]
        own = jnp.where(e == here.east, to_east, base)
        out_ref[target] = jnp.concatenate([begin, jnp.where(here.n == n, own, tile)], axis=0).astype(BF16)
    for copy in copies[5:]:
        copy.wait()


def middle_kernel(
    mask_ref, partner_ref, src_ref, theta_ref, coef_ref, weights_ref, recv_ref,
    flux_ref, force_ref, next_ref, out_ref,
):
    here = Place()
    levels, rows, cols = theta_ref.shape
    fields = flux_ref.shape[0]
    last = rows - 1
    wet = mask_ref[0, 0].astype(F32)

    pairs, cells, points = weights_ref.shape
    chosen = [recv_ref[here.slot(src_ref[0, pair], here.n)][4 : 4 + fields] for pair in range(pairs)]
    weights = weights_ref[...].reshape(pairs * cells, points)
    total = jnp.dot(jnp.concatenate(chosen, axis=1), weights, preferred_element_type=F32)
    force = jnp.zeros((rows, cols), F32)
    for k in range(fields):
        grid = jnp.concatenate([total[k : k + 1, r * cols : (r + 1) * cols] for r in range(rows)], axis=0)
        flux_ref[k] = grid
        force = force + COEFS[k] * grid
    force = wet * (0.1 * force)
    force_ref[...] = force

    t = theta_ref[...]
    u, v, d = wet * coef_ref[0], wet * coef_ref[1], wet * coef_ref[2]
    lane = lax.broadcasted_iota(jnp.int32, t.shape, 2)
    line = lax.broadcasted_iota(jnp.int32, t.shape, 1)
    level = lax.broadcasted_iota(jnp.int32, t.shape, 0)

    def got(e, n):
        return recv_ref[here.slot(e, n)].astype(F32)

    sides = fill(cols, {0: got(here.west, here.n)[3:4], cols - 1: got(here.east, here.n)[0:1]}).T.reshape(t.shape)
    fold, over, under = got(partner_ref[0, 0], here.n), got(here.e, here.above), got(here.e, here.below)
    spots = (0, 1, cols - 2, cols - 1)
    beyond = {spot: jnp.where(here.is_top, fold[3 - i : 4 - i], over[i : i + 1]) for i, spot in enumerate(spots)}
    beyond.update({spot + (2 if i < 2 else -2): under[i : i + 1] for i, spot in enumerate(spots)})
    beyond = fill(cols, beyond).T.reshape(t.shape)
    flat = lax.broadcasted_iota(jnp.int32, (levels, cols), 1)
    above = jnp.where(here.is_top, beyond[:, last, :], beyond[:, 0, :])
    above = jnp.where((flat < 2) | (flat >= cols - 2), above, 0.0)
    below = beyond[:, last, :]
    below = jnp.where(
        flat < 2, pltpu.roll(below, cols - 2, 1), jnp.where(flat >= cols - 2, pltpu.roll(below, 2, 1), 0.0)
    )
    below = jnp.where(here.has_south, below, 0.0)
    east = jnp.where(lane == cols - 1, sides, shifted(t, 2, True))
    west = jnp.where(lane == 0, sides, shifted(t, 2, False))
    north = jnp.where(line == last, above[:, None, :], shifted(t, 1, True))
    south = jnp.where(line == 0, below[:, None, :], shifted(t, 1, False))
    t = stencil(t, east, west, north, south, u, v, d)
    t = t + jnp.where(level == 0, force[None], 0.0)
    next_ref[...] = t

    held = [got(m, here.top) for m in range(here.count)]
    size = -(-here.count * TILE // cols) * cols
    tiles = [block[TILE:] for block in held] + [jnp.zeros((size - here.count * TILE, cols), F32)] * (size > here.count * TILE)
    tiles = jnp.concatenate(tiles, axis=0).astype(BF16)
    partners = jnp.concatenate([jnp.broadcast_to(block[1:2, 1:2], (TILE, 1)) for block in held], axis=0)
    wanted = TILE * partners + lax.rem(lax.broadcasted_iota(jnp.int32, partners.shape, 0), TILE).astype(F32)
    pick = lax.broadcasted_iota(jnp.int32, (here.count * TILE, size), 1).astype(F32) == wanted
    folded = jnp.dot(pick.astype(F32).astype(BF16), tiles, preferred_element_type=F32)

    turned = turn(t)
    slot = lax.broadcasted_iota(jnp.int32, (rows, rows, cols), 1)
    marks = jnp.where(slot == WET_SLOT, wet, 0.0)
    marks = [jnp.where(slot == FORCE_SLOT, force[:, None, :], marks)] + [marks] * (levels // rows - 1)
    marks = jnp.concatenate(marks, axis=0).reshape(cols, cols).T
    ends = jnp.concatenate([turned[0:1], turned[cols - 1 : cols], jnp.zeros((6, cols), F32)], axis=0)
    slot = lax.rem(lax.broadcasted_iota(jnp.int32, (1, cols), 1), 8)

    def corners(shifts, mark):
        row = mark
        for index, shift in enumerate(shifts):
            moved = pltpu.roll(ends, shift % cols, 1) if shift else ends
            row = jnp.where(slot == index, moved[index // 2 : index // 2 + 1], row)
        return row

    up, down = (-last, 2 - last, 2 - last, 4 - last), (0, 0, 2, 2)
    low_mark, high_mark = marks[0:1], marks[cols - 1 : cols]
    rest = jnp.zeros((TILE - 5, cols), F32)
    high_force, low_force = [force[last : last + 1], force[last - 1 : last]], [force[0:1], force[1:2]]
    low, high = [turned[0:1], turned[1:2]], [turned[cols - 1 : cols], turned[cols - 2 : cols - 1]]
    base = jnp.concatenate([corners(up, low_mark)] + high_force + low + [rest], axis=0)
    to_east = jnp.concatenate([corners(up, high_mark)] + high_force + high + [rest], axis=0)
    to_below = jnp.concatenate([corners(down, low_mark)] + low_force + low + [rest], axis=0)
    first_half = here.e < here.half
    for target in range(here.devices):
        e, n = target // here.block_rows, target % here.block_rows
        begin = jnp.where(n == here.n - 1, to_below, jnp.where(e == here.east, to_east, base))
        pair = n + 1 if n % 2 == 0 else n - 1
        other = max(n - 1, 0) if n % 2 == 0 else min(n + 1, here.top)
        tile = got(e, jnp.where(first_half, pair, other))[TILE:]
        if n == here.top:
            tile = jnp.where(first_half, tile, folded[e * TILE : (e + 1) * TILE])
        out_ref[target] = jnp.concatenate([begin, tile], axis=0).astype(BF16)


def last_kernel(
    mask_ref, partner_ref, theta_ref, coef_ref, next_ref, force_ref, first_ref, second_ref, result_ref,
):
    here = Place()
    levels, rows, cols = theta_ref.shape
    last = rows - 1
    partner = partner_ref[0, 0]
    wet = mask_ref[0, 0].astype(F32)
    is_top, has_south = here.is_top, here.has_south

    def got(e, n):
        return second_ref[here.slot(e, n)].astype(F32)

    west, east = got(here.west, here.n), got(here.east, here.n)
    over, under = got(here.e, here.above), got(here.e, here.below)
    fold = got(partner, here.n)
    fold_east = got(lax.rem(partner + 1, here.count), here.n)[0:1]
    fold_west = got(lax.rem(partner + here.count - 1, here.count), here.n)[0:1]
    over_west, over_east = got(here.west, here.above)[0:1], got(here.east, here.above)[0:1]
    under_west, under_east = got(here.west, here.below)[0:1], got(here.east, here.below)[0:1]
    first_west = first_ref[here.slot(here.west, here.n)].astype(F32)
    first_east = first_ref[here.slot(here.east, here.n)].astype(F32)

    def mark(block):
        return block[0:1, WET_SLOT : WET_SLOT + 1]

    tiles = KINDS * levels // TILE

    def gather(begin, source):
        found = []
        for k in range(tiles):
            e, order = k // (here.block_rows - 1), k % (here.block_rows - 1)
            found.append(got(begin + e, order + (source <= order).astype(jnp.int32))[TILE:])
        return jnp.concatenate(found, axis=0)

    near, far = gather(0, here.pair), gather(here.half, here.other)
    south = jnp.where(has_south, jnp.where(here.even, far, near), 0.0)
    north = jnp.where(here.even, near, far)
    mirror = cols - 1 - lax.broadcasted_iota(jnp.int32, north.shape, 1)
    north = jnp.where(is_top, jnp.take_along_axis(north, mirror, axis=1), north)

    def kinds(bulk, wet, sign):
        t, inner, tend, u, v, d = [bulk[kind * levels : (kind + 1) * levels] for kind in range(KINDS)]
        return t, inner, inner + wet * tend, (sign * wet) * u, (sign * wet) * v, wet * d

    north = kinds(north, jnp.where(is_top, mark(fold), mark(over)), jnp.where(is_top, -1.0, 1.0))
    south = kinds(south, mark(under), 1.0)

    top_west, top_east = jnp.zeros((1, cols), F32), jnp.zeros((1, cols), F32)
    for s in range(here.count):
        row = got(s, here.n)[0:1]
        top_west = jnp.where(first_west[1:2, 1:2] == float(s), row, top_west)
        top_east = jnp.where(first_east[1:2, 1:2] == float(s), row, top_east)
    moved = [fold[0:1], over[0:1], under[0:1], fold_west, over_west, under_west, top_east]
    moved = jnp.concatenate(moved + [jnp.zeros((1, cols), F32)], axis=0)
    moved = pltpu.roll(moved, cols - 2, 1)
    ends = fill(
        cols,
        {
            0: jnp.where(is_top, moved[0:1], over[0:1]),
            1: under[0:1],
            2: jnp.where(is_top, fold_east, moved[4:5]),
            3: moved[5:6],
            cols - 4: under_east,
            cols - 3: jnp.where(is_top, moved[3:4], over_east),
            cols - 2: moved[2:3],
            cols - 1: jnp.where(is_top, fold[0:1], moved[1:2]),
        },
    ).T.reshape(theta_ref.shape)
    edges, inners = ends[:, 0, :], ends[:, 1, :]
    lane = lax.broadcasted_iota(jnp.int32, (levels, cols), 1)
    level = lax.broadcasted_iota(jnp.int32, (levels, cols), 0)

    def capped(row, values, lanes):
        low = pltpu.roll(values, cols - lanes, 1) if lanes else values
        high = pltpu.roll(values, lanes, 1) if lanes else values
        return jnp.where(lane == 0, low, jnp.where(lane == cols - 1, high, row))

    def forced(row, force):
        return row + jnp.where(level == 0, force, 0.0)

    flip = cols - 1 - lax.broadcasted_iota(jnp.int32, (8, cols), 1)
    flipped = jnp.take_along_axis(fold[:TILE], flip, axis=1)
    north_force = [jnp.where(is_top, flipped[k : k + 1], over[k : k + 1]) for k in (1, 2)]
    south_force = [under[1:2], under[2:3]]
    t0 = theta_ref[...]

    def rim(rows_of, inside, outward, force, at):
        edge_row = stencil(
            rows_of[0], shifted(rows_of[0], 1, True), shifted(rows_of[0], 1, False),
            rows_of[1] if outward else inside, inside if outward else rows_of[1], *rows_of[3:],
        )
        return capped(forced(edge_row, force[0]), edges, at), capped(forced(rows_of[2], force[1]), inners, at)

    north_one, north_two = rim(north, t0[:, last, :], True, north_force, 0)
    south_one, south_two = rim(south, t0[:, 0, :], False, south_force, 1)
    south_one, south_two = jnp.where(has_south, south_one, 0.0), jnp.where(has_south, south_two, 0.0)
    u, v, d = wet * coef_ref[0], wet * coef_ref[1], wet * coef_ref[2]
    shape = t0.shape
    wide = lax.broadcasted_iota(jnp.int32, shape, 2)
    line = lax.broadcasted_iota(jnp.int32, shape, 1)
    force = jnp.where(lax.broadcasted_iota(jnp.int32, shape, 0) == 0, force_ref[...][None], 0.0)
    inside = (wide >= 2) & (wide < cols - 2)
    t = next_ref[...]
    t = t + jnp.where((line == last) & inside, (d - 0.5 * v) * north[0][:, None, :], 0.0)
    t = t + jnp.where((line == 0) & inside, (d + 0.5 * v) * south[0][:, None, :], 0.0)

    def outer(row, beyond, inside, outward, rows_of, force_row, lanes):
        low, high = pltpu.roll(edges, cols - lanes, 1), pltpu.roll(edges, lanes, 1)
        result = stencil(
            row, jnp.where(lane == cols - 1, high, shifted(row, 1, True)),
            jnp.where(lane == 0, low, shifted(row, 1, False)),
            beyond if outward else inside, inside if outward else beyond, *rows_of[3:],
        )
        return forced(result, force_row)

    north_next = outer(north_one, north_two, t[:, last, :], True, north, north_force[0], 2)
    south_next = outer(south_one, south_two, t[:, 0, :], False, south, south_force[0], 3)
    south_next = jnp.where(has_south, south_next, 0.0)

    def pair(low, high):
        return jnp.concatenate([low, high, jnp.zeros((6, cols), F32)], axis=0)

    turned = turn(t)
    side = pair(west[3:4], east[3:4])
    along = lax.broadcasted_iota(jnp.int32, (8, cols), 1)
    place = lax.rem(along, rows)
    corner = pair(jnp.where(is_top, top_west, moved[4:5]), jnp.where(is_top, moved[6:7], over_east))
    side_north = jnp.where(place == last, pltpu.roll(corner, last, 1), shifted(side, 1, True))
    corner = jnp.where(has_south, pair(moved[5:6], under_east), 0.0)
    side_south = jnp.where(place == 0, corner, shifted(side, 1, False))
    side_force = jnp.take_along_axis(pair(west[0:1], east[0:1]), jnp.where(along < rows, 8 * along, 0) + FORCE_SLOT, axis=1)
    side_next = stencil(
        side, pair(turned[0:1], east[4:5]), pair(west[4:5], turned[cols - 1 : cols]), side_north, side_south,
        *[pair(mark(west) * first_west[k : k + 1], mark(east) * first_east[k : k + 1]) for k in range(10, 13)],
    ) + jnp.where(along < rows, side_force, 0.0)

    def advance(t, sides, above, below):
        return force + stencil(
            t,
            jnp.where(wide == cols - 1, sides, shifted(t, 2, True)),
            jnp.where(wide == 0, sides, shifted(t, 2, False)),
            jnp.where(line == last, above[:, None, :], shifted(t, 1, True)),
            jnp.where(line == 0, below[:, None, :], shifted(t, 1, False)),
            u, v, d,
        )

    def columns(low, high):
        return fill(cols, {0: low, cols - 1: high}).T.reshape(shape)

    t = advance(t, columns(west[3:4], east[3:4]), north_one, south_one)
    result_ref[...] = advance(t, columns(side_next[0:1], side_next[1:2]), north_next, south_next)


def exchange(blocks):
    return lax.all_to_all(blocks, ("ew", "ns"), split_axis=0, concat_axis=0, tiled=True)


def local(theta, velocity, diffusivity, land_mask, fold_partner, atm_flux, remap_src, remap_weights):
    levels, rows, cols = theta.shape
    fields = atm_flux.shape[2]
    shape = jax.ShapeDtypeStruct
    devices = lax.axis_size("ew") * lax.axis_size("ns")
    blocks = (devices, BLOCK, cols)
    room = 60 * 2**20 - 2 * max(0, 2 * devices * BLOCK * cols - 2**20)
    scalars = [land_mask, fold_partner.reshape(1, 1), remap_src[0]]
    weights = remap_weights[0, 0]
    out, field, coef, weights, *scalars = pl.pallas_call(
        first_kernel,
        out_shape=(
            pltpu.VMEM(blocks, BF16), pltpu.VMEM(theta.shape, F32), pltpu.VMEM((3,) + theta.shape, F32),
            pltpu.VMEM(weights.shape, BF16),
        ) + tuple(pltpu.SMEM(x.shape, x.dtype) for x in scalars),
        in_specs=[HBM] * 8,
        out_specs=(VMEM,) * 4 + (SMEM,) * 3,
        scratch_shapes=[
            pltpu.VMEM((fields, cols), BF16),
            pltpu.VMEM((2 * KINDS * levels // TILE, TILE, cols), F32),
            pltpu.SemaphoreType.DMA((8,)),
        ],
        compiler_params=pltpu.CompilerParams(vmem_limit_bytes=room),
        name="first",
    )(*scalars, theta, velocity, diffusivity, atm_flux[0, 0], weights)
    first = exchange(out)
    flux, force, after, out = pl.pallas_call(
        middle_kernel,
        out_shape=(
            shape((fields, rows, cols), F32), pltpu.VMEM((rows, cols), F32), pltpu.VMEM(theta.shape, F32),
            pltpu.VMEM(blocks, BF16),
        ),
        in_specs=[SMEM] * 3 + [VMEM] * 4,
        out_specs=(VMEM,) * 4,
        compiler_params=PARAMS,
        name="middle",
    )(*scalars, field, coef, weights, first)
    second = exchange(out)
    field = pl.pallas_call(
        last_kernel,
        out_shape=shape(theta.shape, F32),
        in_specs=[SMEM] * 2 + [VMEM] * 6,
        out_specs=VMEM,
        compiler_params=PARAMS,
        name="last",
    )(*scalars[:2], field, coef, after, force, first, second)
    return field, flux.reshape(1, 1, fields, rows * cols)


def solution(mesh):
    return jax.shard_map(
        local,
        mesh=mesh,
        in_specs=(
            P(None, "ns", "ew"),
            P(None, None, "ns", "ew"),
            P(None, "ns", "ew"),
            P("ns", "ew"),
            P("ew"),
            P("ns", "ew", None, None),
            P("ns", "ew", None),
            P("ns", "ew", None, None, None),
        ),
        out_specs=(P(None, "ns", "ew"), P("ns", "ew", None, None)),
        check_vma=False,
    )
```

time: 38 us -> 31 us (0.82)
  blocking collectives: 11.2 us -> 25.3 us
  starting transfers between devices: 8.27 us -> 0 us
  waiting for transfers between devices: 7.25 us -> 0 us
  local copies, waits for them, and re-layouts: 5.14 us -> 0 us
    all_to_all x1 -> x2, blocking collectives: 11.2 us -> 25.3 us  [exchange(): lax.all_to_all(blocks, ('ew', 'ns'), split_axis=0, concat_axis=0, tiled=T...]
    all_to_all x1 -> x0, starting transfers between devices: 7.3 us -> none  [exchange(): lax.all_to_all(blocks, ('ew', 'ns'), split_axis=0, concat_axis=0, tiled=T...]
    all_to_all x1 -> x0, waiting for transfers between devices: 6.93 us -> none  [exchange(): lax.all_to_all(blocks, ('ew', 'ns'), split_axis=0, concat_axis=0, tiled=T...]
    unnamed x12 -> x0, local copies, waits for them, and re-layouts: 5.14 us -> none
    ppermute x2 -> x0, starting transfers between devices: 0.97 us -> none  [swap(): return lax.ppermute(rows, 'ns', pairs + [(b, a) for a, b in pairs])]
    pallas_call x1, Pallas kernels: 1.41 us -> 0.87 us  [local(): pl.pallas_call(middle_kernel, out_shape=(shape((fields, rows, cols), F32)...]
  transfers between devices with their start and end apart: 3 -> 0, of which waited for: 2 -> 0; matrix products, arithmetic and copies ran while one was open for 0% -> 0% of each run, Pallas kernels for 0% -> 0%
where the time goes in v2:
time: 31 us; the launch traced here: 30.8 us
  blocking collectives  25.3 us (82%)
  Pallas kernels  3.5 us (11%)
  between operations  1.93 us (6%)
    all_to_all x2, blocking collectives, exchange(): lax.all_to_all(blocks, ('ew', 'ns'), split_axis=0, concat_axis=0, tiled=T...  25.3 us
    pallas_call x1, Pallas kernels, local(): pl.pallas_call(first_kernel, out_shape=(pltpu.VMEM(blocks, BF16), pltpu.V...  1.46 us
    pallas_call x1, Pallas kernels, local(): pl.pallas_call(last_kernel, out_shape=shape(theta.shape, F32), in_specs=[...  1.17 us
    pallas_call x1, Pallas kernels, local(): pl.pallas_call(middle_kernel, out_shape=(shape((fields, rows, cols), F32)...  0.87 us

profile of v2, /device:TPU:0, one launch (start us, length us, event | category | flops | bytes accessed | tf_op | source)
XLA Modules:
  0.0 30.8 jit_solution(3489032080750722775)
XLA Ops:
  1.9 1.5 %first.1 = (bf16[32,16,128]{2,1,0:T(8,128)(2,1)S(1)}, f32[16,8,128]{2,1,0:T(8,128)S(1)}, f32[3,16,8,128]{3,2,1,0:T(8,128)S(1)}, bf16[4,128,1024]{2,1,0:T(8,128)(...) custom-call(s32[1,1]{1,0:T(1,128)S(6)} %copy.12.mask_hbm, s32[1,1]{1,0:T(1,128)} %bitcast.5.partner_hbm, ...), custom_call_target="tpu_custom_call" | custom-call | tf_op jit(solution)/shard_map/first/pallas_call | solution.py:384
  3.4 15.3 %all_to_all.10.recv_ref.first_ref = bf16[32,16,128]{2,1,0:T(8,128)(2,1)S(1)} all-to-all(bf16[32,16,128]{2,1,0:T(8,128)(2,1)S(1)} %get-tuple-element.19), channel_id=1, replica_groups=mesh['ew'=8,'ns'=4] {'ew','ns'}, dimensions={0} | all-to-all | bytes 262144 | tf_op jit(solution)/shard_map/all_to_all | solution.py:372
  18.7 0.9 %middle.1 = (f32[6,8,128]{2,1,0:T(8,128)}, f32[8,128]{1,0:T(8,128)S(1)}, f32[16,8,128]{2,1,0:T(8,128)S(1)}, bf16[32,16,128]{2,1,0:T(8,128)(2,1)S(1)}) custom-call(s32[1,1]{1,0:T(1,128)S(4)} %get-tuple-element.13.mask_ref, s32[1,1]{1,0:T(1,128)S(4)} %get-tuple-element.14.partner_ref, s32[1,4]{1,0:T(1,128)S(4)} %get-tuple-element.17.src_ref, ...), custom_call_target="tpu_custom_call" | custom-call | tf_op jit(solution)/shard_map/middle/pallas_call | solution.py:401
  19.6 10.0 %all_to_all.11.second_ref = bf16[32,16,128]{2,1,0:T(8,128)(2,1)S(1)} all-to-all(bf16[32,16,128]{2,1,0:T(8,128)(2,1)S(1)} %get-tuple-element.22), channel_id=1, replica_groups=mesh['ew'=8,'ns'=4] {'ew','ns'}, dimensions={0} | all-to-all | bytes 262144 | tf_op jit(solution)/shard_map/all_to_all | solution.py:372
  29.6 1.2 %last.1 = f32[16,8,128]{2,1,0:T(8,128)} custom-call(s32[1,1]{1,0:T(1,128)S(4)} %get-tuple-element.13.mask_ref, s32[1,1]{1,0:T(1,128)S(4)} %get-tuple-element.14.partner_ref, f32[16,8,128]{2,1,0:T(8,128)S(1)} %get-tuple-element.15.theta_ref, f32[3,16,8,128]{3,2,1,0:T(8,128)S(1)} %get-tuple-element.16.coef_ref, f32[16,8,128]{2,1,0:T(8,128)S(1)} %get-tuple-element.20.next_ref, ...), custom_call_target="tpu_custom_call" | custom-call | tf_op jit(solution)/shard_map/last/pallas_call | solution.py:413

commit v3 on v2

v3 whole, which is shorter than its diff:
```python
import jax
import jax.numpy as jnp
from jax import lax
from jax.experimental import pallas as pl
from jax.experimental.pallas import tpu as pltpu
from jax.sharding import PartitionSpec as P

COEFS = (0.5, -0.3, 0.2, 0.4, -0.25, 0.35)
VMEM = pl.BlockSpec(memory_space=pltpu.VMEM)
SMEM = pl.BlockSpec(memory_space=pltpu.SMEM)
HBM = pl.BlockSpec(memory_space=pltpu.HBM)
PARAMS = pltpu.CompilerParams(vmem_limit_bytes=16 * 1024 * 1024)
F32 = jnp.float32
BF16 = jnp.bfloat16
KINDS = 6
BLOCK, TILE = 16, 8
FORCE_SLOT, WET_SLOT = 4, 5


def tendency(t, east, west, north, south, u, v, d):
    return d * (east + west + north + south - 4.0 * t) - 0.5 * (u * (east - west) + v * (north - south))


def stencil(t, *others):
    return t + tendency(t, *others)


class Place:
    def __init__(self):
        self.count, self.block_rows = lax.axis_size("ew"), lax.axis_size("ns")
        self.devices = self.count * self.block_rows
        self.e, self.n = lax.axis_index("ew"), lax.axis_index("ns")
        self.top = self.block_rows - 1
        self.is_top = self.n == self.top
        self.has_south = self.n > 0
        self.even = lax.rem(self.n, 2) == 0
        self.east = lax.rem(self.e + 1, self.count)
        self.west = lax.rem(self.e + self.count - 1, self.count)
        self.above = jnp.minimum(self.n + 1, self.top)
        self.below = jnp.maximum(self.n - 1, 0)
        self.pair = jnp.where(self.even, self.n + 1, self.n - 1)
        self.other = jnp.where(self.even, self.below, self.above)
        self.half = self.count // 2

    def slot(self, e, n):
        return e * self.block_rows + n


def fill(size, rows):
    parts, at = [], 0
    for index in sorted(rows):
        if index > at:
            parts.append(jnp.zeros((index - at, size), F32))
        parts.append(rows[index])
        at = index + 1
    if at < size:
        parts.append(jnp.zeros((size - at, size), F32))
    return jnp.concatenate(parts, axis=0)


def turn(field):
    return field.reshape(field.shape[0] * field.shape[1], field.shape[2]).T


def shifted(field, axis, back):
    size = field.shape[axis]
    return pltpu.roll(field, size - 1 if back else 1, axis)


def first_kernel(
    partner_ref, theta_hbm, vel_hbm, diff_hbm, atm_hbm,
    out_ref, theta_ref, coef_ref,
    atm_ref, bulk_ref, sems,
):
    here = Place()
    pairs = [
        (theta_hbm, theta_ref), (vel_hbm, coef_ref.at[pl.ds(0, 2)]), (diff_hbm, coef_ref.at[2]),
        (atm_hbm, atm_ref),
    ]
    copies = [pltpu.make_async_copy(a, b, sems.at[i]) for i, (a, b) in enumerate(pairs)]
    for copy in copies:
        copy.start()
    for copy in copies:
        copy.wait()
    levels, rows, cols = theta_ref.shape
    tiles = levels // TILE
    each = KINDS * tiles
    for side, step in enumerate((-1, 1)):
        edge = rows - 1 if step < 0 else 0
        outer, t, inner = [theta_ref[:, edge + k * step, :] for k in range(3)]
        north, south = (outer, inner) if step < 0 else (inner, outer)
        coef = [coef_ref[k, :, edge + step, :] for k in range(3)]
        tend = tendency(t, shifted(t, 1, True), shifted(t, 1, False), north, south, *coef)
        for kind, field in enumerate((outer, t, tend, *[coef_ref[k, :, edge, :] for k in range(3)])):
            bulk_ref[pl.ds(side * each + kind * tiles, tiles)] = field.reshape(tiles, TILE, cols)
    turned = turn(theta_ref[...])
    lane = lax.broadcasted_iota(jnp.int32, (1, cols), 1)
    second = jnp.where(lane == 1, partner_ref[0].astype(F32), turned[1:2])
    columns = [turned[0:1], second, turned[cols - 2 : cols - 1], turned[cols - 1 : cols]]
    atm = atm_ref[...].astype(F32)
    begin = jnp.concatenate(columns + [atm[: TILE - 4]], axis=0)
    own = jnp.concatenate([atm[TILE - 4 :], jnp.zeros((2 * TILE - 4 - atm.shape[0], cols), F32)], axis=0)
    for target in range(here.devices):
        e, n = target // here.block_rows, target % here.block_rows
        order = (e % here.half) * (here.block_rows - 1) + n - (here.n < n).astype(jnp.int32)
        upward = here.even if e < here.half else jnp.logical_not(here.even)
        tile = bulk_ref[jnp.where(upward, 0, each) + jnp.minimum(order, each - 1)]
        out_ref[target] = jnp.concatenate([begin, jnp.where(here.n == n, own, tile)], axis=0).astype(BF16)

def load_kernel(src_hbm, weights_hbm, src_ref, weights_ref, sems):
    copies = [
        pltpu.make_async_copy(weights_hbm, weights_ref, sems.at[0]), pltpu.make_async_copy(src_hbm, src_ref, sems.at[1])
    ]
    for copy in copies:
        copy.start()
    for copy in copies:
        copy.wait()


def side_kernel(
    mask_ref, theta_ref, coef_ref, points_ref, columns_ref, rims_ref, start_ref
):
    levels, rows, cols = theta_ref.shape
    last = rows - 1
    wet = mask_ref[0, 0].astype(F32)
    u, v, d = wet * coef_ref[0], wet * coef_ref[1], wet * coef_ref[2]
    turned = [turn(u), turn(v), turn(d)]
    for side, at in enumerate((0, cols - 1)):
        for k in range(3):
            columns_ref[side, k : k + 1, :] = turned[k][at : at + 1]
    center, east, west, north, south = 1.0 - 4.0 * d, d - 0.5 * u, d + 0.5 * u, d - 0.5 * v, d + 0.5 * v
    for k, field in enumerate((center, east, west, north, south)):
        points_ref[k] = field
    t = theta_ref[...]
    lane = lax.broadcasted_iota(jnp.int32, t.shape, 2)
    line = lax.broadcasted_iota(jnp.int32, t.shape, 1)
    rims_ref[0] = jnp.where(lane == cols - 1, east, jnp.where(lane == 0, west, 0.0))
    rims_ref[1] = jnp.where(line == last, north, jnp.where(line == 0, south, 0.0))
    inner = center * t
    inner = inner + east * jnp.where(lane == cols - 1, 0.0, shifted(t, 2, True))
    inner = inner + west * jnp.where(lane == 0, 0.0, shifted(t, 2, False))
    inner = inner + north * jnp.where(line == last, 0.0, shifted(t, 1, True))
    inner = inner + south * jnp.where(line == 0, 0.0, shifted(t, 1, False))
    start_ref[...] = inner


def middle_kernel(
    mask_ref, partner_ref, src_ref, columns_ref, rims_ref, start_ref, weights_ref, recv_ref,
    total_ref, force_ref, next_ref, ends_ref, out_ref,
):
    here = Place()
    levels, rows, cols = start_ref.shape
    fields = total_ref.shape[0]
    last = rows - 1
    wet = mask_ref[0, 0].astype(F32)

    pairs, cells, points = weights_ref.shape
    chosen = [recv_ref[here.slot(src_ref[0, pair], here.n)][4 : 4 + fields] for pair in range(pairs)]
    weights = weights_ref[...].reshape(pairs * cells, points)
    total = jnp.dot(jnp.concatenate(chosen, axis=1), weights, preferred_element_type=F32)
    total_ref[...] = total
    force = jnp.zeros((1, points), F32)
    for k in range(fields):
        force = force + COEFS[k] * total[k : k + 1]
    force = jnp.concatenate([force[:, r * cols : (r + 1) * cols] for r in range(rows)], axis=0)
    force = wet * (0.1 * force)
    force_ref[...] = force

    shape = start_ref.shape
    line = lax.broadcasted_iota(jnp.int32, shape, 1)
    level = lax.broadcasted_iota(jnp.int32, shape, 0)

    def got(e, n):
        return recv_ref[here.slot(e, n)].astype(F32)

    sides = fill(cols, {0: got(here.west, here.n)[3:4], cols - 1: got(here.east, here.n)[0:1]}).T.reshape(shape)
    fold, over, under = got(partner_ref[0], here.n), got(here.e, here.above), got(here.e, here.below)
    spots = (0, 1, cols - 2, cols - 1)
    beyond = {spot: jnp.where(here.is_top, fold[3 - i : 4 - i], over[i : i + 1]) for i, spot in enumerate(spots)}
    beyond.update({spot + (2 if i < 2 else -2): under[i : i + 1] for i, spot in enumerate(spots)})
    beyond = fill(cols, beyond).T.reshape(shape)
    flat = lax.broadcasted_iota(jnp.int32, (levels, cols), 1)
    above = jnp.where(here.is_top, beyond[:, last, :], beyond[:, 0, :])
    above = jnp.where((flat < 2) | (flat >= cols - 2), above, 0.0)
    below = beyond[:, last, :]
    below = jnp.where(
        flat < 2, pltpu.roll(below, cols - 2, 1), jnp.where(flat >= cols - 2, pltpu.roll(below, 2, 1), 0.0)
    )
    below = jnp.where(here.has_south, below, 0.0)
    across = jnp.where(line == last, above[:, None, :], below[:, None, :])
    t = start_ref[...] + rims_ref[0] * sides + rims_ref[1] * across
    next_ref[...] = t + jnp.where(level == 0, force[None], 0.0)

    held = [got(m, here.top) for m in range(here.count)]
    size = -(-here.count * TILE // cols) * cols
    tiles = [block[TILE:] for block in held] + [jnp.zeros((size - here.count * TILE, cols), F32)] * (size > here.count * TILE)
    tiles = jnp.concatenate(tiles, axis=0).astype(BF16)
    partners = jnp.concatenate([jnp.broadcast_to(block[1:2, 1:2], (TILE, 1)) for block in held], axis=0)
    wanted = TILE * partners + lax.rem(lax.broadcasted_iota(jnp.int32, partners.shape, 0), TILE).astype(F32)
    pick = lax.broadcasted_iota(jnp.int32, (here.count * TILE, size), 1).astype(F32) == wanted
    folded = jnp.dot(pick.astype(F32).astype(BF16), tiles, preferred_element_type=F32)

    turned = turn(t) + jnp.concatenate([force, jnp.zeros((cols - rows, cols), F32)], axis=0).T
    ends = jnp.concatenate([turned[0:1], turned[cols - 1 : cols], jnp.zeros((TILE - 2, cols), F32)], axis=0)
    lane = lax.broadcasted_iota(jnp.int32, (TILE, cols), 1)
    forces = jnp.concatenate([force, jnp.zeros((cols - rows, cols), F32)], axis=0).T
    forces = jnp.concatenate([forces[0:1], forces[cols - 1 : cols], jnp.zeros((TILE - 2, cols), F32)], axis=0)
    ends_ref[...] = ends
    marks = jnp.take_along_axis(forces, lane // 8, axis=1)
    slot = lax.rem(lane, 8)
    marks = jnp.where(slot == FORCE_SLOT, marks, jnp.where(slot == WET_SLOT, wet, 0.0))
    slot = slot[0:1]

    def corners(shifts, mark):
        row = mark
        for index, shift in enumerate(shifts):
            moved = pltpu.roll(ends, shift % cols, 1) if shift else ends
            row = jnp.where(slot == index, moved[index // 2 : index // 2 + 1], row)
        return row

    up, down = (-last, 2 - last, 2 - last, 4 - last), (0, 0, 2, 2)
    low_mark, high_mark = marks[0:1], marks[1:2]
    low_coef, high_coef = columns_ref[0], columns_ref[1]
    high_force, low_force = [force[last : last + 1], force[last - 1 : last]], [force[0:1], force[1:2]]
    low, high = [turned[0:1], turned[1:2]], [turned[cols - 1 : cols], turned[cols - 2 : cols - 1]]
    base = jnp.concatenate([corners(up, low_mark)] + high_force + low + [low_coef], axis=0)
    to_east = jnp.concatenate([corners(up, high_mark)] + high_force + high + [high_coef], axis=0)
    to_below = jnp.concatenate([corners(down, low_mark)] + low_force + low + [low_coef], axis=0)
    first_half = here.e < here.half
    for target in range(here.devices):
        e, n = target // here.block_rows, target % here.block_rows
        begin = jnp.where(n == here.n - 1, to_below, jnp.where(e == here.east, to_east, base))
        pair = n + 1 if n % 2 == 0 else n - 1
        other = max(n - 1, 0) if n % 2 == 0 else min(n + 1, here.top)
        tile = got(e, jnp.where(first_half, pair, other))[TILE:]
        if n == here.top:
            tile = jnp.where(first_half, tile, folded[e * TILE : (e + 1) * TILE])
        out_ref[target] = jnp.concatenate([begin, tile], axis=0).astype(BF16)


def last_kernel(
    partner_ref, theta_ref, points_ref, total_ref, next_ref, ends_ref, force_ref, first_ref, second_ref,
    result_hbm, flux_hbm, result_ref, flux_ref, rim_ref, sems,
):
    here = Place()
    levels, rows, cols = theta_ref.shape
    last = rows - 1
    for k in range(flux_ref.shape[0]):
        for r in range(rows):
            flux_ref[k, r : r + 1, :] = total_ref[k : k + 1, r * cols : (r + 1) * cols]
    copies = [
        pltpu.make_async_copy(flux_ref, flux_hbm, sems.at[0]), pltpu.make_async_copy(result_ref, result_hbm, sems.at[1])
    ]
    copies[0].start()
    partner = partner_ref[0]
    is_top, has_south = here.is_top, here.has_south

    def got(e, n):
        return second_ref[here.slot(e, n)].astype(F32)

    west, east = got(here.west, here.n), got(here.east, here.n)
    over, under = got(here.e, here.above), got(here.e, here.below)
    fold = got(partner, here.n)
    fold_east = got(lax.rem(partner + 1, here.count), here.n)[0:1]
    fold_west = got(lax.rem(partner + here.count - 1, here.count), here.n)[0:1]
    over_west, over_east = got(here.west, here.above)[0:1], got(here.east, here.above)[0:1]
    under_west, under_east = got(here.west, here.below)[0:1], got(here.east, here.below)[0:1]
    first_west = first_ref[here.slot(here.west, here.n)].astype(F32)
    first_east = first_ref[here.slot(here.east, here.n)].astype(F32)

    def mark(block):
        return block[0:1, WET_SLOT : WET_SLOT + 1]

    tiles = KINDS * levels // TILE

    def gather(begin, source):
        found = []
        for k in range(tiles):
            e, order = k // (here.block_rows - 1), k % (here.block_rows - 1)
            found.append(got(begin + e, order + (source <= order).astype(jnp.int32))[TILE:])
        return jnp.concatenate(found, axis=0)

    near, far = gather(0, here.pair), gather(here.half, here.other)
    south = jnp.where(has_south, jnp.where(here.even, far, near), 0.0)
    north = jnp.where(here.even, near, far)
    mirror = cols - 1 - lax.broadcasted_iota(jnp.int32, north.shape, 1)
    north = jnp.where(is_top, jnp.take_along_axis(north, mirror, axis=1), north)

    def kinds(bulk, wet, sign):
        t, inner, tend, u, v, d = [bulk[kind * levels : (kind + 1) * levels] for kind in range(KINDS)]
        return t, inner, inner + wet * tend, (sign * wet) * u, (sign * wet) * v, wet * d

    north = kinds(north, jnp.where(is_top, mark(fold), mark(over)), jnp.where(is_top, -1.0, 1.0))
    south = kinds(south, mark(under), 1.0)

    top_west, top_east = jnp.zeros((1, cols), F32), jnp.zeros((1, cols), F32)
    for s in range(here.count):
        row = got(s, here.n)[0:1]
        top_west = jnp.where(first_west[1:2, 1:2] == float(s), row, top_west)
        top_east = jnp.where(first_east[1:2, 1:2] == float(s), row, top_east)
    moved = [fold[0:1], over[0:1], under[0:1], fold_west, over_west, under_west, top_east]
    moved = jnp.concatenate(moved + [jnp.zeros((1, cols), F32)], axis=0)
    moved = pltpu.roll(moved, cols - 2, 1)
    def pair(low, high):
        return jnp.concatenate([low, high, jnp.zeros((TILE - 2, cols), F32)], axis=0)

    along = lax.broadcasted_iota(jnp.int32, (TILE, cols), 1)
    place = lax.rem(along, rows)
    side = pair(west[3:4], east[3:4])
    corner = pair(jnp.where(is_top, top_west, moved[4:5]), jnp.where(is_top, moved[6:7], over_east))
    side_north = jnp.where(place == last, pltpu.roll(corner, last, 1), shifted(side, 1, True))
    corner = jnp.where(has_south, pair(moved[5:6], under_east), 0.0)
    side_south = jnp.where(place == 0, corner, shifted(side, 1, False))
    side_force = jnp.take_along_axis(pair(west[0:1], east[0:1]), jnp.where(along < rows, 8 * along, 0) + FORCE_SLOT, axis=1)
    side_next = stencil(
        side, pair(ends_ref[0:1], east[4:5]), pair(west[4:5], ends_ref[1:2]), side_north, side_south,
        *[pair(west[k : k + 1], east[k : k + 1]) for k in (5, 6, 7)],
    ) + jnp.where(along < rows, side_force, 0.0)

    listed = [
        (west[3:4], east[3:4]),
        (side_next[0:1], side_next[1:2]),
        (jnp.where(is_top, moved[0:1], over[0:1]), jnp.where(is_top, fold[0:1], moved[1:2])),
        (under[0:1], moved[2:3]),
        (jnp.where(is_top, fold_east, moved[4:5]), jnp.where(is_top, moved[3:4], over_east)),
        (moved[5:6], under_east),
    ]
    lanes = {}
    for q, (low, high) in enumerate(listed):
        lanes[2 * q], lanes[(2 * q - 1) % cols] = low, high
    rim = fill(cols, lanes).T.reshape(theta_ref.shape)
    rim_ref[...] = rim

    def listing(q, field):
        return pltpu.roll(field, cols - 2 * q, field.ndim - 1) if q else field

    edges, inners = rim_ref[:, 0, :], rim_ref[:, 1, :]
    lane = lax.broadcasted_iota(jnp.int32, (levels, cols), 1)
    level = lax.broadcasted_iota(jnp.int32, (levels, cols), 0)
    ends = (lane == 0) | (lane == cols - 1)

    def forced(row, force):
        return row + jnp.where(level == 0, force, 0.0)

    flip = cols - 1 - lax.broadcasted_iota(jnp.int32, (8, cols), 1)
    flipped = jnp.take_along_axis(fold[:TILE], flip, axis=1)
    north_force = [jnp.where(is_top, flipped[k : k + 1], over[k : k + 1]) for k in (1, 2)]
    south_force = [under[1:2], under[2:3]]

    def beyond(rows_of, inside, outward, force, q):
        edge_row = stencil(
            rows_of[0], shifted(rows_of[0], 1, True), shifted(rows_of[0], 1, False),
            rows_of[1] if outward else inside, inside if outward else rows_of[1], *rows_of[3:],
        )
        edge_row = jnp.where(ends, listing(q, edges), forced(edge_row, force[0]))
        return edge_row, jnp.where(ends, listing(q, inners), forced(rows_of[2], force[1]))

    north_one, north_two = beyond(north, theta_ref[:, last, :], True, north_force, 2)
    south_one, south_two = beyond(south, theta_ref[:, 0, :], False, south_force, 3)
    south_one, south_two = jnp.where(has_south, south_one, 0.0), jnp.where(has_south, south_two, 0.0)
    shape = theta_ref.shape
    wide = lax.broadcasted_iota(jnp.int32, shape, 2)
    line = lax.broadcasted_iota(jnp.int32, shape, 1)
    force = jnp.where(lax.broadcasted_iota(jnp.int32, shape, 0) == 0, force_ref[...][None], 0.0)
    inside = (lane >= 2) & (lane < cols - 2)
    top_row = next_ref[:, last, :] + jnp.where(inside, points_ref[3, :, last, :] * north[0], 0.0)
    bottom_row = next_ref[:, 0, :] + jnp.where(inside, points_ref[4, :, 0, :] * south[0], 0.0)
    t = jnp.where(line == last, top_row[:, None, :], jnp.where(line == 0, bottom_row[:, None, :], next_ref[...]))

    def outer(row, further, inside, outward, rows_of, force_row, diagonal):
        result = stencil(
            row, jnp.where(lane == cols - 1, diagonal, shifted(row, 1, True)),
            jnp.where(lane == 0, diagonal, shifted(row, 1, False)),
            further if outward else inside, inside if outward else further, *rows_of[3:],
        )
        return forced(result, force_row)

    north_next = outer(north_one, north_two, top_row, True, north, north_force[0], listing(4, edges))
    south_next = outer(south_one, south_two, bottom_row, False, south, south_force[0], listing(5, edges))
    south_next = jnp.where(has_south, south_next, 0.0)

    def advance(t, sides, above, below):
        east = jnp.where(wide == cols - 1, sides, shifted(t, 2, True))
        west = jnp.where(wide == 0, sides, shifted(t, 2, False))
        north = jnp.where(line == last, above[:, None, :], shifted(t, 1, True))
        south = jnp.where(line == 0, below[:, None, :], shifted(t, 1, False))
        result = force
        for k, field in enumerate((t, east, west, north, south)):
            result = result + points_ref[k] * field
        return result

    t = advance(t, rim, north_one, south_one)
    result_ref[...] = advance(t, listing(1, rim), north_next, south_next)
    copies[1].start()
    for copy in copies:
        copy.wait()


def exchange(blocks):
    return lax.all_to_all(blocks, ("ew", "ns"), split_axis=0, concat_axis=0, tiled=True)


def local(theta, velocity, diffusivity, land_mask, fold_partner, atm_flux, remap_src, remap_weights):
    levels, rows, cols = theta.shape
    fields = atm_flux.shape[2]
    shape = jax.ShapeDtypeStruct
    devices = lax.axis_size("ew") * lax.axis_size("ns")
    blocks = (devices, BLOCK, cols)
    room = 60 * 2**20 - 2 * max(0, 2 * devices * BLOCK * cols - 2**20)
    weights = remap_weights[0, 0]
    out, field, coef = pl.pallas_call(
        first_kernel,
        out_shape=(
            pltpu.VMEM(blocks, BF16), pltpu.VMEM(theta.shape, F32), pltpu.VMEM((3,) + theta.shape, F32),
        ),
        in_specs=[SMEM] + [HBM] * 4,
        out_specs=(VMEM,) * 3,
        scratch_shapes=[
            pltpu.VMEM((fields, cols), BF16),
            pltpu.VMEM((2 * KINDS * levels // TILE, TILE, cols), F32),
            pltpu.SemaphoreType.DMA((4,)),
        ],
        compiler_params=pltpu.CompilerParams(vmem_limit_bytes=room),
        name="first",
    )(fold_partner, theta, velocity, diffusivity, atm_flux[0, 0])
    first = exchange(out)
    sources, weights = pl.pallas_call(
        load_kernel,
        out_shape=(pltpu.SMEM(remap_src.shape[1:], remap_src.dtype), pltpu.VMEM(weights.shape, BF16)),
        in_specs=[HBM] * 2,
        out_specs=(SMEM, VMEM),
        scratch_shapes=[pltpu.SemaphoreType.DMA((2,))],
        compiler_params=pltpu.CompilerParams(vmem_limit_bytes=room),
        cost_estimate=pl.CostEstimate(flops=2**20, bytes_accessed=2**22, transcendentals=0),
        name="load",
    )(remap_src[0], weights)
    points, columns, rims, start = pl.pallas_call(
        side_kernel,
        out_shape=(
            pltpu.VMEM((5,) + theta.shape, F32), pltpu.VMEM((2, 3, cols), F32), pltpu.VMEM((2,) + theta.shape, F32),
            pltpu.VMEM(theta.shape, F32),
        ),
        in_specs=[SMEM, VMEM, VMEM],
        out_specs=(VMEM,) * 4,
        compiler_params=PARAMS,
        cost_estimate=pl.CostEstimate(flops=2**20, bytes_accessed=2**20, transcendentals=0),
        name="side",
    )(land_mask, field, coef)
    total, force, after, ends, out = pl.pallas_call(
        middle_kernel,
        out_shape=(
            pltpu.VMEM((fields, rows * cols), F32), pltpu.VMEM((rows, cols), F32), pltpu.VMEM(theta.shape, F32),
            pltpu.VMEM((TILE, cols), F32), pltpu.VMEM(blocks, BF16),
        ),
        in_specs=[SMEM] * 3 + [VMEM] * 5,
        out_specs=(VMEM,) * 5,
        compiler_params=PARAMS,
        name="middle",
    )(land_mask, fold_partner, sources, columns, rims, start, weights, first)
    second = exchange(out)
    field, flux = pl.pallas_call(
        last_kernel,
        out_shape=(shape(theta.shape, F32), shape((fields, rows, cols), F32)),
        in_specs=[SMEM] + [VMEM] * 8,
        out_specs=(HBM, HBM),
        scratch_shapes=[
            pltpu.VMEM(theta.shape, F32), pltpu.VMEM((fields, rows, cols), F32), pltpu.VMEM(theta.shape, F32),
            pltpu.SemaphoreType.DMA((2,)),
        ],
        compiler_params=PARAMS,
        name="last",
    )(fold_partner, field, points, total, after, ends, force, first, second)
    return field, flux.reshape(1, 1, fields, rows * cols)


def solution(mesh):
    return jax.shard_map(
        local,
        mesh=mesh,
        in_specs=(
            P(None, "ns", "ew"),
            P(None, None, "ns", "ew"),
            P(None, "ns", "ew"),
            P("ns", "ew"),
            P("ew"),
            P("ns", "ew", None, None),
            P("ns", "ew", None),
            P("ns", "ew", None, None, None),
        ),
        out_specs=(P(None, "ns", "ew"), P("ns", "ew", None, None)),
        check_vma=False,
    )
```

time: 31 us -> 30.5 us (0.984)
  blocking collectives: 25.3 us -> 10 us
  starting transfers between devices: 0 us -> 7.3 us
  waiting for transfers between devices: 0 us -> 6.14 us
  Pallas kernels: 3.5 us -> 4.89 us
    all_to_all x2 -> x1, blocking collectives: 25.3 us -> 10 us  [exchange(): lax.all_to_all(blocks, ('ew', 'ns'), split_axis=0, concat_axis=0, tiled=T...]
    all_to_all x0 -> x1, starting transfers between devices: none -> 7.3 us  [exchange(): lax.all_to_all(blocks, ('ew', 'ns'), split_axis=0, concat_axis=0, tiled=T...]
    all_to_all x0 -> x1, waiting for transfers between devices: none -> 6.14 us  [exchange(): lax.all_to_all(blocks, ('ew', 'ns'), split_axis=0, concat_axis=0, tiled=T...]
    pallas_call x2 -> x4, Pallas kernels: 2.04 us -> 3.11 us  [the longest x1 1.25 us: local(): pl.pallas_call(load_kernel, out_shape=(pltpu.SMEM(remap_src.shape[1:], re...]
    pallas_call x1, Pallas kernels: 1.46 us -> 1.78 us  [local(): pl.pallas_call(first_kernel, out_shape=(pltpu.VMEM(blocks, BF16), pltpu.V...]
  transfers between devices with their start and end apart: 0 -> 1, of which waited for: 0 -> 1; matrix products, arithmetic and copies ran while one was open for 0% -> 0% of each run, Pallas kernels for 0% -> 5%
where the time goes in v3:
time: 30.5 us; the launch traced here: 30.3 us
  blocking collectives  10 us (33%)
  starting transfers between devices  7.3 us (24%)
  waiting for transfers between devices  6.14 us (20%)
  Pallas kernels  4.89 us (16%)
  between operations  1.96 us (6%)
    all_to_all x1, blocking collectives, exchange(): lax.all_to_all(blocks, ('ew', 'ns'), split_axis=0, concat_axis=0, tiled=T...  10 us
    all_to_all x1, starting transfers between devices, exchange(): lax.all_to_all(blocks, ('ew', 'ns'), split_axis=0, concat_axis=0, tiled=T...  7.3 us
    all_to_all x1, waiting for transfers between devices, exchange(): lax.all_to_all(blocks, ('ew', 'ns'), split_axis=0, concat_axis=0, tiled=T...  6.14 us
    pallas_call x1, Pallas kernels, local(): pl.pallas_call(first_kernel, out_shape=(pltpu.VMEM(blocks, BF16), pltpu.V...  1.78 us
    pallas_call x1, Pallas kernels, local(): pl.pallas_call(load_kernel, out_shape=(pltpu.SMEM(remap_src.shape[1:], re...  1.25 us
    pallas_call x1, Pallas kernels, local(): pl.pallas_call(last_kernel, out_shape=(shape(theta.shape, F32), shape((fi...  1.19 us
  transfers between devices with their start and end apart: 1, of which 1 were waited for; matrix products, arithmetic and copies ran while one was open for 0% of the time, Pallas kernels for 5%

profile of v3, /device:TPU:0, one launch (start us, length us, event | category | flops | bytes accessed | tf_op | source)
XLA Modules:
  0.0 30.3 jit_solution(5459360069911680857)
XLA Ops:
  1.3 1.8 %first.1 = (bf16[32,16,128]{2,1,0:T(8,128)(2,1)}, f32[16,8,128]{2,1,0:T(8,128)S(1)}, f32[3,16,8,128]{3,2,1,0:T(8,128)S(1)}) custom-call(s32[1]{0:T(128)S(6)} %copy.13.partner_ref, f32[16,8,128]{2,1,0:T(8,128)} %theta_hbm.1, f32[2,16,8,128]{3,2,1,0:T(8,128)} %vel_hbm.1, f32[16,8,128]{2,1,0:T(8,128)} %diff_hbm.1, bf16[6,128]{1,0:T(8,128)(2,1)} %bitcast.5), custom_call_target="tpu_custom_call" | custom-call | tf_op jit(solution)/shard_map/first/pallas_call | solution.py:411
  3.1 7.3 %all-to-all-start = ((bf16[32,16,128]{2,1,0:T(8,128)(2,1)}), bf16[32,16,128]{2,1,0:T(8,128)(2,1)S(1)}, u32[]{:S(2)}, u32[]{:S(2)}) async-start(bf16[32,16,128]{2,1,0:T(8,128)(2,1)} %get-tuple-element.26), calls=%async_computation | async-start | bytes 262144 | tf_op jit(solution)/shard_map/all_to_all | solution.py:400
  11.0 1.3 %load.1 = (s32[1,4]{1,0:T(1,128)S(4)}, bf16[4,128,1024]{2,1,0:T(8,128)(2,1)S(1)}) custom-call(s32[1,4]{1,0:T(1,128)} %bitcast.6, bf16[4,128,1024]{2,1,0:T(8,128)(2,1)} %bitcast.4), custom_call_target="tpu_custom_call" | custom-call | flops 1048576 | bytes 4194304 | tf_op jit(solution)/shard_map/load/pallas_call | solution.py:427
  12.3 0.2 side.1
  12.5 6.1 %all-to-all-done.recv_ref.first_ref = bf16[32,16,128]{2,1,0:T(8,128)(2,1)S(1)} async-done(((bf16[32,16,128]{2,1,0:T(8,128)(2,1)}), bf16[32,16,128]{2,1,0:T(8,128)(2,1)S(1)}, u32[]{:S(2)}, u32[]{:S(2)}) %all-to-all-start) | async-done | bytes 131104 | tf_op jit(solution)/shard_map/all_to_all | solution.py:400
  18.6 0.5 %middle.1 = (f32[6,1024]{1,0:T(8,128)S(1)}, f32[8,128]{1,0:T(8,128)S(1)}, f32[16,8,128]{2,1,0:T(8,128)S(1)}, f32[8,128]{1,0:T(8,128)S(1)}, bf16[32,16,128]{2,1,0:T(8,128)(2,1)S(1)}) custom-call(s32[1,1]{1,0:T(1,128)S(6)} %copy.12.mask_ref, s32[1]{0:T(128)S(6)} %copy.13.partner_ref, s32[1,4]{1,0:T(1,128)S(4)} %get-tuple-element.21.src_ref, ...), custom_call_target="tpu_custom_call" | custom-call | tf_op jit(solution)/shard_map/middle/pallas_call | solution.py:449
  19.1 10.0 %all_to_all.10.second_ref = bf16[32,16,128]{2,1,0:T(8,128)(2,1)S(1)} all-to-all(bf16[32,16,128]{2,1,0:T(8,128)(2,1)S(1)} %get-tuple-element.31), channel_id=1, replica_groups=mesh['ew'=8,'ns'=4] {'ew','ns'}, dimensions={0} | all-to-all | bytes 262144 | tf_op jit(solution)/shard_map/all_to_all | solution.py:400
  29.1 1.2 %last.1 = (f32[16,8,128]{2,1,0:T(8,128)}, f32[6,8,128]{2,1,0:T(8,128)}) custom-call(s32[1]{0:T(128)S(6)} %copy.13.partner_ref, f32[16,8,128]{2,1,0:T(8,128)S(1)} %get-tuple-element.18.theta_ref, f32[5,16,8,128]{3,2,1,0:T(8,128)S(1)} %get-tuple-element.20.points_ref, f32[6,1024]{1,0:T(8,128)S(1)} %get-tuple-element.27.total_ref, ...), custom_call_target="tpu_custom_call" | custom-call | tf_op jit(solution)/shard_map/last/pallas_call | solution.py:461
Async XLA Ops:
  3.1 15.5 %all-to-all-start = ((bf16[32,16,128]{2,1,0:T(8,128)(2,1)}), bf16[32,16,128]{2,1,0:T(8,128)(2,1)S(1)}, u32[]{:S(2)}, u32[]{:S(2)}) async-start(bf16[32,16,128]{2,1,0:T(8,128)(2,1)} %get-tuple-element.26), calls=%async_computation | async-start | bytes 262144 | tf_op jit(solution)/shard_map/all_to_all | solution.py:400

commit v4 on v3

--- a/solution.py
+++ b/solution.py
@@ -1,3 +1,5 @@
+import functools
+
 import jax
 import jax.numpy as jnp
 from jax import lax
@@ -43,7 +45,7 @@
         self.half = self.count // 2
 
     def slot(self, e, n):
-        return e * self.block_rows + n
+        return n * self.count + e
 
 
 def fill(size, rows):
@@ -67,32 +69,46 @@
     return pltpu.roll(field, size - 1 if back else 1, axis)
 
 
-def first_kernel(
-    partner_ref, theta_hbm, vel_hbm, diff_hbm, atm_hbm,
-    out_ref, theta_ref, coef_ref,
-    atm_ref, bulk_ref, sems,
-):
-    here = Place()
-    pairs = [
-        (theta_hbm, theta_ref), (vel_hbm, coef_ref.at[pl.ds(0, 2)]), (diff_hbm, coef_ref.at[2]),
-        (atm_hbm, atm_ref),
-    ]
-    copies = [pltpu.make_async_copy(a, b, sems.at[i]) for i, (a, b) in enumerate(pairs)]
+def bring_kernel(count, *refs):
+    copies = [pltpu.make_async_copy(refs[i], refs[count + i], refs[-1].at[i]) for i in range(count)]
     for copy in copies:
         copy.start()
     for copy in copies:
         copy.wait()
+
+
+def bring(arrays, memories, room, name):
+    return pl.pallas_call(
+        functools.partial(bring_kernel, len(arrays)),
+        out_shape=tuple(memory(x.shape, x.dtype) for x, memory in zip(arrays, memories)),
+        in_specs=[HBM] * len(arrays),
+        out_specs=tuple(VMEM if memory is pltpu.VMEM else SMEM for memory in memories),
+        scratch_shapes=[pltpu.SemaphoreType.DMA((len(arrays),))],
+        compiler_params=pltpu.CompilerParams(vmem_limit_bytes=room),
+        cost_estimate=pl.CostEstimate(flops=2**20, bytes_accessed=2**22, transcendentals=0),
+        name=name,
+    )(*arrays)
+
+
+def first_kernel(partner_ref, theta_ref, vel_ref, diff_ref, atm_ref, out_ref, bulk_ref):
+    here = Place()
     levels, rows, cols = theta_ref.shape
+    each = KINDS * levels // TILE
+    firsts = [
+        [jnp.where(upward, 0, each) - (here.n < n).astype(jnp.int32) for n in range(here.block_rows)]
+        for upward in (here.even, jnp.logical_not(here.even))
+    ]
+    coef_refs = [vel_ref.at[0], vel_ref.at[1], diff_ref]
     tiles = levels // TILE
-    each = KINDS * tiles
     for side, step in enumerate((-1, 1)):
         edge = rows - 1 if step < 0 else 0
         outer, t, inner = [theta_ref[:, edge + k * step, :] for k in range(3)]
         north, south = (outer, inner) if step < 0 else (inner, outer)
-        coef = [coef_ref[k, :, edge + step, :] for k in range(3)]
+        coef = [ref[:, edge + step, :] for ref in coef_refs]
         tend = tendency(t, shifted(t, 1, True), shifted(t, 1, False), north, south, *coef)
-        for kind, field in enumerate((outer, t, tend, *[coef_ref[k, :, edge, :] for k in range(3)])):
+        for kind, field in enumerate((outer, t, tend, *[ref[:, edge, :] for ref in coef_refs])):
             bulk_ref[pl.ds(side * each + kind * tiles, tiles)] = field.reshape(tiles, TILE, cols)
+    bulk_ref[2 * each] = jnp.zeros((TILE, cols), F32)
     turned = turn(theta_ref[...])
     lane = lax.broadcasted_iota(jnp.int32, (1, cols), 1)
     second = jnp.where(lane == 1, partner_ref[0].astype(F32), turned[1:2])
@@ -101,29 +117,20 @@
     begin = jnp.concatenate(columns + [atm[: TILE - 4]], axis=0)
     own = jnp.concatenate([atm[TILE - 4 :], jnp.zeros((2 * TILE - 4 - atm.shape[0], cols), F32)], axis=0)
     for target in range(here.devices):
-        e, n = target // here.block_rows, target % here.block_rows
-        order = (e % here.half) * (here.block_rows - 1) + n - (here.n < n).astype(jnp.int32)
-        upward = here.even if e < here.half else jnp.logical_not(here.even)
-        tile = bulk_ref[jnp.where(upward, 0, each) + jnp.minimum(order, each - 1)]
+        e, n = target % here.count, target // here.count
+        order = (e % here.half) * (here.block_rows - 1) + n
+        start = firsts[e // here.half][n]
+        tile = bulk_ref[start + min(order, each)]
         out_ref[target] = jnp.concatenate([begin, jnp.where(here.n == n, own, tile)], axis=0).astype(BF16)
 
-def load_kernel(src_hbm, weights_hbm, src_ref, weights_ref, sems):
-    copies = [
-        pltpu.make_async_copy(weights_hbm, weights_ref, sems.at[0]), pltpu.make_async_copy(src_hbm, src_ref, sems.at[1])
-    ]
-    for copy in copies:
-        copy.start()
-    for copy in copies:
-        copy.wait()
-
 
 def side_kernel(
-    mask_ref, theta_ref, coef_ref, points_ref, columns_ref, rims_ref, start_ref
+    mask_ref, theta_ref, vel_ref, diff_ref, points_ref, columns_ref, rims_ref, start_ref
 ):
     levels, rows, cols = theta_ref.shape
     last = rows - 1
     wet = mask_ref[0, 0].astype(F32)
-    u, v, d = wet * coef_ref[0], wet * coef_ref[1], wet * coef_ref[2]
+    u, v, d = wet * vel_ref[0], wet * vel_ref[1], wet * diff_ref[...]
     turned = [turn(u), turn(v), turn(d)]
     for side, at in enumerate((0, cols - 1)):
         for k in range(3):
@@ -228,7 +235,7 @@
     to_below = jnp.concatenate([corners(down, low_mark)] + low_force + low + [low_coef], axis=0)
     first_half = here.e < here.half
     for target in range(here.devices):
-        e, n = target // here.block_rows, target % here.block_rows
+        e, n = target % here.count, target // here.count
         begin = jnp.where(n == here.n - 1, to_below, jnp.where(e == here.east, to_east, base))
         pair = n + 1 if n % 2 == 0 else n - 1
         other = max(n - 1, 0) if n % 2 == 0 else min(n + 1, here.top)
@@ -397,7 +404,7 @@
 
 
 def exchange(blocks):
-    return lax.all_to_all(blocks, ("ew", "ns"), split_axis=0, concat_axis=0, tiled=True)
+    return lax.all_to_all(blocks, ("ns", "ew"), split_axis=0, concat_axis=0, tiled=True)
 
 
 def local(theta, velocity, diffusivity, land_mask, fold_partner, atm_flux, remap_src, remap_weights):
@@ -408,44 +415,32 @@
     blocks = (devices, BLOCK, cols)
     room = 60 * 2**20 - 2 * max(0, 2 * devices * BLOCK * cols - 2**20)
     weights = remap_weights[0, 0]
-    out, field, coef = pl.pallas_call(
+    field, velocity, diffusivity, flux = bring(
+        [theta, velocity, diffusivity, atm_flux[0, 0]], [pltpu.VMEM] * 4, room, "bring"
+    )
+    out = pl.pallas_call(
         first_kernel,
-        out_shape=(
-            pltpu.VMEM(blocks, BF16), pltpu.VMEM(theta.shape, F32), pltpu.VMEM((3,) + theta.shape, F32),
-        ),
-        in_specs=[SMEM] + [HBM] * 4,
-        out_specs=(VMEM,) * 3,
-        scratch_shapes=[
-            pltpu.VMEM((fields, cols), BF16),
-            pltpu.VMEM((2 * KINDS * levels // TILE, TILE, cols), F32),
-            pltpu.SemaphoreType.DMA((4,)),
-        ],
-        compiler_params=pltpu.CompilerParams(vmem_limit_bytes=room),
+        out_shape=pltpu.VMEM(blocks, BF16),
+        in_specs=[SMEM] + [VMEM] * 4,
+        out_specs=VMEM,
+        scratch_shapes=[pltpu.VMEM((2 * KINDS * levels // TILE + 1, TILE, cols), F32)],
+        compiler_params=PARAMS,
         name="first",
-    )(fold_partner, theta, velocity, diffusivity, atm_flux[0, 0])
+    )(fold_partner, field, velocity, diffusivity, flux)
     first = exchange(out)
-    sources, weights = pl.pallas_call(
-        load_kernel,
-        out_shape=(pltpu.SMEM(remap_src.shape[1:], remap_src.dtype), pltpu.VMEM(weights.shape, BF16)),
-        in_specs=[HBM] * 2,
-        out_specs=(SMEM, VMEM),
-        scratch_shapes=[pltpu.SemaphoreType.DMA((2,))],
-        compiler_params=pltpu.CompilerParams(vmem_limit_bytes=room),
-        cost_estimate=pl.CostEstimate(flops=2**20, bytes_accessed=2**22, transcendentals=0),
-        name="load",
-    )(remap_src[0], weights)
+    sources, weights = bring([remap_src[0], weights], [pltpu.SMEM, pltpu.VMEM], room, "load")
     points, columns, rims, start = pl.pallas_call(
         side_kernel,
         out_shape=(
             pltpu.VMEM((5,) + theta.shape, F32), pltpu.VMEM((2, 3, cols), F32), pltpu.VMEM((2,) + theta.shape, F32),
             pltpu.VMEM(theta.shape, F32),
         ),
-        in_specs=[SMEM, VMEM, VMEM],
+        in_specs=[SMEM] + [VMEM] * 3,
         out_specs=(VMEM,) * 4,
         compiler_params=PARAMS,
         cost_estimate=pl.CostEstimate(flops=2**20, bytes_accessed=2**20, transcendentals=0),
         name="side",
-    )(land_mask, field, coef)
+    )(land_mask, field, velocity, diffusivity)
     total, force, after, ends, out = pl.pallas_call(
         middle_kernel,
         out_shape=(

time: 30.5 us -> 30 us (0.984)
  waiting for transfers between devices: 6.14 us -> 5.66 us
    all_to_all x1, waiting for transfers between devices: 6.14 us -> 5.66 us  [exchange(): lax.all_to_all(blocks, ('ns', 'ew'), split_axis=0, concat_axis=0, tiled=T...]
    pallas_call x2 -> x3, Pallas kernels: 3.04 us -> 3.03 us  [the longest x2 2.23 us: bring(): pl.pallas_call(functools.partial(bring_kernel, len(arrays)), out_shape=tu...]
where the time goes in v4:
time: 30 us; the launch traced here: 29.8 us
  blocking collectives  10 us (33%)
  starting transfers between devices  7.3 us (24%)
  waiting for transfers between devices  5.66 us (19%)
  Pallas kernels  4.88 us (16%)
  between operations  1.96 us (7%)
    all_to_all x1, blocking collectives, exchange(): lax.all_to_all(blocks, ('ns', 'ew'), split_axis=0, concat_axis=0, tiled=T...  10 us
    all_to_all x1, starting transfers between devices, exchange(): lax.all_to_all(blocks, ('ns', 'ew'), split_axis=0, concat_axis=0, tiled=T...  7.3 us
    all_to_all x1, waiting for transfers between devices, exchange(): lax.all_to_all(blocks, ('ns', 'ew'), split_axis=0, concat_axis=0, tiled=T...  5.66 us
    pallas_call x2, Pallas kernels, bring(): pl.pallas_call(functools.partial(bring_kernel, len(arrays)), out_shape=tu...  2.23 us
    pallas_call x1, Pallas kernels, local(): pl.pallas_call(last_kernel, out_shape=(shape(theta.shape, F32), shape((fi...  1.19 us
    pallas_call x1, Pallas kernels, local(): pl.pallas_call(first_kernel, out_shape=pltpu.VMEM(blocks, BF16), in_specs...  0.8 us
  transfers between devices with their start and end apart: 1, of which 1 were waited for; matrix products, arithmetic and copies ran while one was open for 0% of the time, Pallas kernels for 5%

profile of v4, /device:TPU:0, one launch (start us, length us, event | category | flops | bytes accessed | tf_op | source)
XLA Modules:
  0.0 29.8 jit_solution(17966895857664090384)
XLA Ops:
  1.3 1.0 %bring.1 = (f32[16,8,128]{2,1,0:T(8,128)S(1)}, f32[2,16,8,128]{3,2,1,0:T(8,128)S(1)}, f32[16,8,128]{2,1,0:T(8,128)S(1)}, bf16[6,128]{1,0:T(8,128)(2,1)S(1)}) custom-call(f32[16,8,128]{2,1,0:T(8,128)} %refs_0_.1, f32[2,16,8,128]{3,2,1,0:T(8,128)} %refs_1_.1, f32[16,8,128]{2,1,0:T(8,128)} %refs_2_.1, bf16[6,128]{1,0:T(8,128)(2,1)} %bitcast.5), custom_call_target="tpu_custom_call" | custom-call | flops 1048576 | bytes 4194304 | tf_op jit(solution)/shard_map/bring/pallas_call | solution.py:81
  2.3 0.8 %first.1 = bf16[32,16,128]{2,1,0:T(8,128)(2,1)} custom-call(s32[1]{0:T(128)S(6)} %copy.13.partner_ref, f32[16,8,128]{2,1,0:T(8,128)S(1)} %get-tuple-element.19.theta_ref, f32[2,16,8,128]{3,2,1,0:T(8,128)S(1)} %get-tuple-element.20.vel_ref, f32[16,8,128]{2,1,0:T(8,128)S(1)} %get-tuple-element.21.diff_ref, bf16[6,128]{1,0:T(8,128)(2,1)S(1)} %get-tuple-element.28.atm_ref), custom_call_target="tpu_custom_call" | custom-call | tf_op jit(solution)/shard_map/first/pallas_call | solution.py:421
  3.1 7.3 %all-to-all-start = ((bf16[32,16,128]{2,1,0:T(8,128)(2,1)}), bf16[32,16,128]{2,1,0:T(8,128)(2,1)S(1)}, u32[]{:S(2)}, u32[]{:S(2)}) async-start(bf16[32,16,128]{2,1,0:T(8,128)(2,1)} %first.1), calls=%async_computation | async-start | bytes 262144 | tf_op jit(solution)/shard_map/all_to_all | solution.py:407
  11.0 0.2 side.1
  11.2 1.2 %load.1 = (s32[1,4]{1,0:T(1,128)S(4)}, bf16[4,128,1024]{2,1,0:T(8,128)(2,1)S(1)}) custom-call(s32[1,4]{1,0:T(1,128)} %bitcast.6, bf16[4,128,1024]{2,1,0:T(8,128)(2,1)} %bitcast.4), custom_call_target="tpu_custom_call" | custom-call | flops 1048576 | bytes 4194304 | tf_op jit(solution)/shard_map/load/pallas_call | solution.py:81
  12.5 5.7 %all-to-all-done.recv_ref.first_ref = bf16[32,16,128]{2,1,0:T(8,128)(2,1)S(1)} async-done(((bf16[32,16,128]{2,1,0:T(8,128)(2,1)}), bf16[32,16,128]{2,1,0:T(8,128)(2,1)S(1)}, u32[]{:S(2)}, u32[]{:S(2)}) %all-to-all-start) | async-done | bytes 131104 | tf_op jit(solution)/shard_map/all_to_all | solution.py:407
  18.1 0.5 %middle.1 = (f32[6,1024]{1,0:T(8,128)S(1)}, f32[8,128]{1,0:T(8,128)S(1)}, f32[16,8,128]{2,1,0:T(8,128)S(1)}, f32[8,128]{1,0:T(8,128)S(1)}, bf16[32,16,128]{2,1,0:T(8,128)(2,1)S(1)}) custom-call(s32[1,1]{1,0:T(1,128)S(6)} %copy.12.mask_ref, s32[1]{0:T(128)S(6)} %copy.13.partner_ref, s32[1,4]{1,0:T(1,128)S(4)} %get-tuple-element.23.src_ref, ...), custom_call_target="tpu_custom_call" | custom-call | tf_op jit(solution)/shard_map/middle/pallas_call | solution.py:444
  18.6 10.0 %all_to_all.10.second_ref = bf16[32,16,128]{2,1,0:T(8,128)(2,1)S(1)} all-to-all(bf16[32,16,128]{2,1,0:T(8,128)(2,1)S(1)} %get-tuple-element.33), channel_id=1, replica_groups=mesh['ew'=8,'ns'=4] {'ns','ew'}, dimensions={0} | all-to-all | bytes 262144 | tf_op jit(solution)/shard_map/all_to_all | solution.py:407
  28.6 1.2 %last.1 = (f32[16,8,128]{2,1,0:T(8,128)}, f32[6,8,128]{2,1,0:T(8,128)}) custom-call(s32[1]{0:T(128)S(6)} %copy.13.partner_ref, f32[16,8,128]{2,1,0:T(8,128)S(1)} %get-tuple-element.19.theta_ref, f32[5,16,8,128]{3,2,1,0:T(8,128)S(1)} %get-tuple-element.22.points_ref, f32[6,1024]{1,0:T(8,128)S(1)} %get-tuple-element.29.total_ref, ...), custom_call_target="tpu_custom_call" | custom-call | tf_op jit(solution)/shard_map/last/pallas_call | solution.py:456
Async XLA Ops:
  3.1 15.0 %all-to-all-start = ((bf16[32,16,128]{2,1,0:T(8,128)(2,1)}), bf16[32,16,128]{2,1,0:T(8,128)(2,1)S(1)}, u32[]{:S(2)}, u32[]{:S(2)}) async-start(bf16[32,16,128]{2,1,0:T(8,128)(2,1)} %first.1), calls=%async_computation | async-start | bytes 262144 | tf_op jit(solution)/shard_map/all_to_all | solution.py:407

commit v5 on v4

--- a/solution.py
+++ b/solution.py
@@ -15,8 +15,8 @@
 F32 = jnp.float32
 BF16 = jnp.bfloat16
 KINDS = 6
-BLOCK, TILE = 16, 8
-FORCE_SLOT, WET_SLOT = 4, 5
+TILE = 8
+FORCE_SLOT, WET_SLOT, PARTNER_SLOT = 4, 5, 4
 
 
 def tendency(t, east, west, north, south, u, v, d):
@@ -42,10 +42,15 @@
         self.below = jnp.maximum(self.n - 1, 0)
         self.pair = jnp.where(self.even, self.n + 1, self.n - 1)
         self.other = jnp.where(self.even, self.below, self.above)
-        self.half = self.count // 2
 
     def slot(self, e, n):
         return n * self.count + e
+
+
+def relays(row, block_rows):
+    is_top = row == block_rows - 1
+    first = jnp.where((row % 2 == 0) | is_top, jnp.maximum(row - 2, 0), row + 2)
+    return first, jnp.where(is_top, jnp.maximum(row - 3, 0), row + 1 - 2 * (row % 2)), jnp.where(is_top, 0, 2)
 
 
 def fill(size, rows):
@@ -62,6 +67,21 @@
 
 def turn(field):
     return field.reshape(field.shape[0] * field.shape[1], field.shape[2]).T
+
+
+def row_of(ref, row):
+    levels, rows, cols = ref.shape
+    return ref.reshape(levels * rows, cols), pl.ds(row, levels, stride=rows)
+
+
+def read_row(ref, row):
+    flat, at = row_of(ref, row)
+    return flat[at, :]
+
+
+def write_row(ref, row, values):
+    flat, at = row_of(ref, row)
+    flat[at, :] = values
 
 
 def shifted(field, axis, back):
@@ -90,42 +110,60 @@
     )(*arrays)
 
 
-def first_kernel(partner_ref, theta_ref, vel_ref, diff_ref, atm_ref, out_ref, bulk_ref):
+def first_kernel(partner_ref, theta_ref, vel_ref, diff_ref, atm_ref, out_ref, near_ref, bulk_ref):
     here = Place()
     levels, rows, cols = theta_ref.shape
-    each = KINDS * levels // TILE
-    firsts = [
-        [jnp.where(upward, 0, each) - (here.n < n).astype(jnp.int32) for n in range(here.block_rows)]
-        for upward in (here.even, jnp.logical_not(here.even))
-    ]
+    tiles = levels // TILE
+    each = KINDS * tiles
     coef_refs = [vel_ref.at[0], vel_ref.at[1], diff_ref]
-    tiles = levels // TILE
-    for side, step in enumerate((-1, 1)):
+    strips = []
+    for step in (1, -1):
         edge = rows - 1 if step < 0 else 0
-        outer, t, inner = [theta_ref[:, edge + k * step, :] for k in range(3)]
+        outer, t, inner = [read_row(theta_ref, edge + k * step) for k in range(3)]
         north, south = (outer, inner) if step < 0 else (inner, outer)
-        coef = [ref[:, edge + step, :] for ref in coef_refs]
+        coef = [read_row(ref, edge + step) for ref in coef_refs]
         tend = tendency(t, shifted(t, 1, True), shifted(t, 1, False), north, south, *coef)
-        for kind, field in enumerate((outer, t, tend, *[ref[:, edge, :] for ref in coef_refs])):
-            bulk_ref[pl.ds(side * each + kind * tiles, tiles)] = field.reshape(tiles, TILE, cols)
-    bulk_ref[2 * each] = jnp.zeros((TILE, cols), F32)
+        strips.append([outer, t, tend] + [read_row(ref, edge) for ref in coef_refs])
+    for kind, (low, high) in enumerate(zip(*strips)):
+        near_ref[kind] = jnp.where(here.even, high, low)
+        far = jnp.where(here.even, low, high)
+        bulk_ref[pl.ds(kind * tiles, tiles)] = far.reshape(tiles, TILE, cols)
+    partner = partner_ref[0].astype(F32)
+
+    @pl.when(here.is_top)
+    def _():
+        for kind in range(KINDS):
+            write_row(bulk_ref, kind, strips[1][kind])
+        write_row(bulk_ref, KINDS, jnp.full((levels, cols), partner))
+        write_row(bulk_ref, KINDS + 1, jnp.zeros((levels, cols), F32))
+
     turned = turn(theta_ref[...])
-    lane = lax.broadcasted_iota(jnp.int32, (1, cols), 1)
-    second = jnp.where(lane == 1, partner_ref[0].astype(F32), turned[1:2])
-    columns = [turned[0:1], second, turned[cols - 2 : cols - 1], turned[cols - 1 : cols]]
+    lane = lax.broadcasted_iota(jnp.int32, (TILE, cols), 1)
+    slot = lax.rem(lane, 8)
+    spots = [turned[0:1], turned[1:2], turned[cols - 2 : cols - 1], turned[cols - 1 : cols]]
+    spots = jnp.concatenate(spots + [jnp.zeros((TILE - 4, cols), F32)], axis=0)
+    spots = jnp.where(here.even, spots, pltpu.roll(spots, cols - rows + 1, 1))
+    corner = jnp.where(slot[0:1] == PARTNER_SLOT, partner, 0.0)
+    for k in range(4):
+        moved = pltpu.roll(spots, k, 1) if k else spots
+        corner = jnp.where(slot[0:1] == k, moved[k : k + 1], corner)
     atm = atm_ref[...].astype(F32)
-    begin = jnp.concatenate(columns + [atm[: TILE - 4]], axis=0)
-    own = jnp.concatenate([atm[TILE - 4 :], jnp.zeros((2 * TILE - 4 - atm.shape[0], cols), F32)], axis=0)
-    for target in range(here.devices):
-        e, n = target % here.count, target // here.count
-        order = (e % here.half) * (here.block_rows - 1) + n
-        start = firsts[e // here.half][n]
-        tile = bulk_ref[start + min(order, each)]
-        out_ref[target] = jnp.concatenate([begin, jnp.where(here.n == n, own, tile)], axis=0).astype(BF16)
+    to_west = jnp.concatenate([corner, turned[0:1], atm], axis=0)
+    to_east = jnp.concatenate([corner, turned[cols - 1 : cols], atm], axis=0)
+    column = jnp.where(here.is_top, partner_ref[0], here.e)
+    first, _, skip = relays(jnp.where(here.is_top, here.top, here.other), here.block_rows)
+    for e in range(here.count):
+        ahead = lax.rem(e - column + here.count, here.count)
+        whole, some = jnp.minimum(ahead, TILE - 1), jnp.clip(ahead + TILE - skip, 0, levels - 1)
+        own = jnp.where(e == here.east, to_east, to_west)
+        for n in range(here.block_rows):
+            tile = bulk_ref[jnp.where(first == n, whole, some)]
+            owed = (here.n == n) | ((here.other == n) & (here.e == e))
+            out_ref[n * here.count + e] = jnp.where(owed, own, tile).astype(BF16)
 
 
 def side_kernel(
-    mask_ref, theta_ref, vel_ref, diff_ref, points_ref, columns_ref, rims_ref, start_ref
+    mask_ref, theta_ref, vel_ref, diff_ref, points_ref, columns_ref, start_ref
 ):
     levels, rows, cols = theta_ref.shape
     last = rows - 1
@@ -141,8 +179,6 @@
     t = theta_ref[...]
     lane = lax.broadcasted_iota(jnp.int32, t.shape, 2)
     line = lax.broadcasted_iota(jnp.int32, t.shape, 1)
-    rims_ref[0] = jnp.where(lane == cols - 1, east, jnp.where(lane == 0, west, 0.0))
-    rims_ref[1] = jnp.where(line == last, north, jnp.where(line == 0, south, 0.0))
     inner = center * t
     inner = inner + east * jnp.where(lane == cols - 1, 0.0, shifted(t, 2, True))
     inner = inner + west * jnp.where(lane == 0, 0.0, shifted(t, 2, False))
@@ -152,8 +188,8 @@
 
 
 def middle_kernel(
-    mask_ref, partner_ref, src_ref, columns_ref, rims_ref, start_ref, weights_ref, recv_ref,
-    total_ref, force_ref, next_ref, ends_ref, out_ref,
+    mask_ref, partner_ref, src_ref, columns_ref, points_ref, start_ref, weights_ref, recv_ref, near_ref,
+    total_ref, force_ref, next_ref, ends_ref, out_ref, beyond_ref, plain_ref,
 ):
     here = Place()
     levels, rows, cols = start_ref.shape
@@ -162,7 +198,7 @@
     wet = mask_ref[0, 0].astype(F32)
 
     pairs, cells, points = weights_ref.shape
-    chosen = [recv_ref[here.slot(src_ref[0, pair], here.n)][4 : 4 + fields] for pair in range(pairs)]
+    chosen = [recv_ref[here.slot(src_ref[0, pair], here.n)][TILE - fields :] for pair in range(pairs)]
     weights = weights_ref[...].reshape(pairs * cells, points)
     total = jnp.dot(jnp.concatenate(chosen, axis=1), weights, preferred_element_type=F32)
     total_ref[...] = total
@@ -174,35 +210,35 @@
     force_ref[...] = force
 
     shape = start_ref.shape
-    line = lax.broadcasted_iota(jnp.int32, shape, 1)
     level = lax.broadcasted_iota(jnp.int32, shape, 0)
 
     def got(e, n):
         return recv_ref[here.slot(e, n)].astype(F32)
 
-    sides = fill(cols, {0: got(here.west, here.n)[3:4], cols - 1: got(here.east, here.n)[0:1]}).T.reshape(shape)
-    fold, over, under = got(partner_ref[0], here.n), got(here.e, here.above), got(here.e, here.below)
+    sides = fill(cols, {0: got(here.west, here.n)[1:2], cols - 1: got(here.east, here.n)[1:2]}).T.reshape(shape)
+    from_fold, over, under = got(partner_ref[0], here.n)[0:1], got(here.e, here.above)[0:1], got(here.e, here.below)[0:1]
+    facing = jnp.where(here.is_top, from_fold, jnp.where(here.even, under, over))
+    facing = jnp.broadcast_to(facing, (TILE, cols))
+    facing = [facing[0:1]] + [pltpu.roll(facing, cols - k, 1)[0:1] for k in range(1, 4)]
+    facing = [jnp.where(here.is_top, facing[3 - k], facing[k]) for k in range(4)]
     spots = (0, 1, cols - 2, cols - 1)
-    beyond = {spot: jnp.where(here.is_top, fold[3 - i : 4 - i], over[i : i + 1]) for i, spot in enumerate(spots)}
-    beyond.update({spot + (2 if i < 2 else -2): under[i : i + 1] for i, spot in enumerate(spots)})
-    beyond = fill(cols, beyond).T.reshape(shape)
-    flat = lax.broadcasted_iota(jnp.int32, (levels, cols), 1)
-    above = jnp.where(here.is_top, beyond[:, last, :], beyond[:, 0, :])
-    above = jnp.where((flat < 2) | (flat >= cols - 2), above, 0.0)
-    below = beyond[:, last, :]
-    below = jnp.where(
-        flat < 2, pltpu.roll(below, cols - 2, 1), jnp.where(flat >= cols - 2, pltpu.roll(below, 2, 1), 0.0)
-    )
-    below = jnp.where(here.has_south, below, 0.0)
-    across = jnp.where(line == last, above[:, None, :], below[:, None, :])
-    t = start_ref[...] + rims_ref[0] * sides + rims_ref[1] * across
+    beyond_ref[...] = fill(cols, dict(zip(spots, facing))).T.reshape(shape)
+    far = read_row(beyond_ref, 0)
+    above = jnp.where(here.even, near_ref[0], far)
+    below = jnp.where(here.has_south, jnp.where(here.even, far, near_ref[0]), 0.0)
+    lane = lax.broadcasted_iota(jnp.int32, shape, 2)
+    rim = jnp.where(lane == cols - 1, points_ref[1], jnp.where(lane == 0, points_ref[2], 0.0))
+    plain_ref[...] = start_ref[...] + rim * sides
+    write_row(plain_ref, last, read_row(plain_ref, last) + read_row(points_ref.at[3], last) * above)
+    write_row(plain_ref, 0, read_row(plain_ref, 0) + read_row(points_ref.at[4], 0) * below)
+    t = plain_ref[...]
     next_ref[...] = t + jnp.where(level == 0, force[None], 0.0)
 
     held = [got(m, here.top) for m in range(here.count)]
     size = -(-here.count * TILE // cols) * cols
-    tiles = [block[TILE:] for block in held] + [jnp.zeros((size - here.count * TILE, cols), F32)] * (size > here.count * TILE)
+    tiles = held + [jnp.zeros((size - here.count * TILE, cols), F32)] * (size > here.count * TILE)
     tiles = jnp.concatenate(tiles, axis=0).astype(BF16)
-    partners = jnp.concatenate([jnp.broadcast_to(block[1:2, 1:2], (TILE, 1)) for block in held], axis=0)
+    partners = jnp.concatenate([jnp.broadcast_to(block[KINDS : KINDS + 1, 0:1], (TILE, 1)) for block in held], axis=0)
     wanted = TILE * partners + lax.rem(lax.broadcasted_iota(jnp.int32, partners.shape, 0), TILE).astype(F32)
     pick = lax.broadcasted_iota(jnp.int32, (here.count * TILE, size), 1).astype(F32) == wanted
     folded = jnp.dot(pick.astype(F32).astype(BF16), tiles, preferred_element_type=F32)
@@ -233,21 +269,22 @@
     base = jnp.concatenate([corners(up, low_mark)] + high_force + low + [low_coef], axis=0)
     to_east = jnp.concatenate([corners(up, high_mark)] + high_force + high + [high_coef], axis=0)
     to_below = jnp.concatenate([corners(down, low_mark)] + low_force + low + [low_coef], axis=0)
-    first_half = here.e < here.half
-    for target in range(here.devices):
-        e, n = target % here.count, target // here.count
-        begin = jnp.where(n == here.n - 1, to_below, jnp.where(e == here.east, to_east, base))
-        pair = n + 1 if n % 2 == 0 else n - 1
-        other = max(n - 1, 0) if n % 2 == 0 else min(n + 1, here.top)
-        tile = got(e, jnp.where(first_half, pair, other))[TILE:]
-        if n == here.top:
-            tile = jnp.where(first_half, tile, folded[e * TILE : (e + 1) * TILE])
-        out_ref[target] = jnp.concatenate([begin, tile], axis=0).astype(BF16)
+    for e in range(here.count):
+        ahead = lax.rem(e - here.e + here.count, here.count)
+        close = (ahead <= 1) | (ahead == here.count - 1)
+        for n in range(here.block_rows):
+            begin = jnp.where(n == here.n - 1, to_below, jnp.where(e == here.east, to_east, base))
+            owed = (n == here.n) | (close & ((n == here.n - 1) | (n == here.n + 1)))
+            if n == here.top:
+                tile = folded[e * TILE : (e + 1) * TILE]
+            else:
+                tile = got(e, max(n - 1, 0) if n % 2 == 0 else n + 1)
+            out_ref[n * here.count + e] = jnp.where(owed, begin, tile).astype(BF16)
 
 
 def last_kernel(
-    partner_ref, theta_ref, points_ref, total_ref, next_ref, ends_ref, force_ref, first_ref, second_ref,
-    result_hbm, flux_hbm, result_ref, flux_ref, rim_ref, sems,
+    partner_ref, theta_ref, points_ref, total_ref, next_ref, ends_ref, force_ref, first_ref, second_ref, near_ref,
+    result_hbm, flux_hbm, result_ref, flux_ref, rim_ref, tall_ref, tile_ref, sems,
 ):
     here = Place()
     levels, rows, cols = theta_ref.shape
@@ -278,23 +315,23 @@
     def mark(block):
         return block[0:1, WET_SLOT : WET_SLOT + 1]
 
-    tiles = KINDS * levels // TILE
-
-    def gather(begin, source):
-        found = []
-        for k in range(tiles):
-            e, order = k // (here.block_rows - 1), k % (here.block_rows - 1)
-            found.append(got(begin + e, order + (source <= order).astype(jnp.int32))[TILE:])
-        return jnp.concatenate(found, axis=0)
-
-    near, far = gather(0, here.pair), gather(here.half, here.other)
-    south = jnp.where(has_south, jnp.where(here.even, far, near), 0.0)
-    north = jnp.where(here.even, near, far)
-    mirror = cols - 1 - lax.broadcasted_iota(jnp.int32, north.shape, 1)
-    north = jnp.where(is_top, jnp.take_along_axis(north, mirror, axis=1), north)
-
-    def kinds(bulk, wet, sign):
-        t, inner, tend, u, v, d = [bulk[kind * levels : (kind + 1) * levels] for kind in range(KINDS)]
+    first, second, skip = relays(here.n, here.block_rows)
+    for k in range(levels):
+        ahead, row = (k, first) if k < TILE else (k - TILE + skip, second)
+        tile_ref[k] = got(lax.rem(here.e + ahead, here.count), row)
+    tiles = levels // TILE
+    far = [tile_ref[pl.ds(kind * tiles, tiles)].reshape(levels, cols) for kind in range(KINDS)]
+    far = jnp.concatenate(far, axis=0)
+    mirrored = jnp.concatenate([read_row(tile_ref, kind) for kind in range(KINDS)], axis=0)
+    mirror = cols - 1 - lax.broadcasted_iota(jnp.int32, far.shape, 1)
+    far = jnp.where(is_top, jnp.take_along_axis(mirrored, mirror, axis=1), far)
+    far = [far[kind * levels : (kind + 1) * levels] for kind in range(KINDS)]
+    near = [near_ref[kind] for kind in range(KINDS)]
+    north = [jnp.where(here.even, a, b) for a, b in zip(near, far)]
+    south = [jnp.where(has_south, jnp.where(here.even, b, a), 0.0) for a, b in zip(near, far)]
+
+    def kinds(strip, wet, sign):
+        t, inner, tend, u, v, d = strip
         return t, inner, inner + wet * tend, (sign * wet) * u, (sign * wet) * v, wet * d
 
     north = kinds(north, jnp.where(is_top, mark(fold), mark(over)), jnp.where(is_top, -1.0, 1.0))
@@ -303,8 +340,8 @@
     top_west, top_east = jnp.zeros((1, cols), F32), jnp.zeros((1, cols), F32)
     for s in range(here.count):
         row = got(s, here.n)[0:1]
-        top_west = jnp.where(first_west[1:2, 1:2] == float(s), row, top_west)
-        top_east = jnp.where(first_east[1:2, 1:2] == float(s), row, top_east)
+        top_west = jnp.where(first_west[0:1, PARTNER_SLOT : PARTNER_SLOT + 1] == float(s), row, top_west)
+        top_east = jnp.where(first_east[0:1, PARTNER_SLOT : PARTNER_SLOT + 1] == float(s), row, top_east)
     moved = [fold[0:1], over[0:1], under[0:1], fold_west, over_west, under_west, top_east]
     moved = jnp.concatenate(moved + [jnp.zeros((1, cols), F32)], axis=0)
     moved = pltpu.roll(moved, cols - 2, 1)
@@ -341,7 +378,7 @@
     def listing(q, field):
         return pltpu.roll(field, cols - 2 * q, field.ndim - 1) if q else field
 
-    edges, inners = rim_ref[:, 0, :], rim_ref[:, 1, :]
+    edges, inners = read_row(rim_ref, 0), read_row(rim_ref, 1)
     lane = lax.broadcasted_iota(jnp.int32, (levels, cols), 1)
     level = lax.broadcasted_iota(jnp.int32, (levels, cols), 0)
     ends = (lane == 0) | (lane == cols - 1)
@@ -362,17 +399,19 @@
         edge_row = jnp.where(ends, listing(q, edges), forced(edge_row, force[0]))
         return edge_row, jnp.where(ends, listing(q, inners), forced(rows_of[2], force[1]))
 
-    north_one, north_two = beyond(north, theta_ref[:, last, :], True, north_force, 2)
-    south_one, south_two = beyond(south, theta_ref[:, 0, :], False, south_force, 3)
+    north_one, north_two = beyond(north, read_row(theta_ref, last), True, north_force, 2)
+    south_one, south_two = beyond(south, read_row(theta_ref, 0), False, south_force, 3)
     south_one, south_two = jnp.where(has_south, south_one, 0.0), jnp.where(has_south, south_two, 0.0)
     shape = theta_ref.shape
     wide = lax.broadcasted_iota(jnp.int32, shape, 2)
-    line = lax.broadcasted_iota(jnp.int32, shape, 1)
     force = jnp.where(lax.broadcasted_iota(jnp.int32, shape, 0) == 0, force_ref[...][None], 0.0)
     inside = (lane >= 2) & (lane < cols - 2)
-    top_row = next_ref[:, last, :] + jnp.where(inside, points_ref[3, :, last, :] * north[0], 0.0)
-    bottom_row = next_ref[:, 0, :] + jnp.where(inside, points_ref[4, :, 0, :] * south[0], 0.0)
-    t = jnp.where(line == last, top_row[:, None, :], jnp.where(line == 0, bottom_row[:, None, :], next_ref[...]))
+    more_north, more_south = inside & jnp.logical_not(here.even), inside & here.even
+    top_row = read_row(next_ref, last) + jnp.where(more_north, read_row(points_ref.at[3], last) * north[0], 0.0)
+    bottom_row = read_row(next_ref, 0) + jnp.where(more_south, read_row(points_ref.at[4], 0) * south[0], 0.0)
+    tall_ref[:, TILE : 2 * TILE, :] = next_ref[...]
+    write_row(tall_ref, TILE + last, top_row)
+    write_row(tall_ref, TILE, bottom_row)
 
     def outer(row, further, inside, outward, rows_of, force_row, diagonal):
         result = stencil(
@@ -386,18 +425,20 @@
     south_next = outer(south_one, south_two, bottom_row, False, south, south_force[0], listing(5, edges))
     south_next = jnp.where(has_south, south_next, 0.0)
 
-    def advance(t, sides, above, below):
+    def advance(sides, above, below):
+        write_row(tall_ref, 2 * TILE, above)
+        write_row(tall_ref, TILE - 1, below)
+        t = tall_ref[:, TILE : 2 * TILE, :]
         east = jnp.where(wide == cols - 1, sides, shifted(t, 2, True))
         west = jnp.where(wide == 0, sides, shifted(t, 2, False))
-        north = jnp.where(line == last, above[:, None, :], shifted(t, 1, True))
-        south = jnp.where(line == 0, below[:, None, :], shifted(t, 1, False))
+        north, south = tall_ref[:, TILE + 1 : 2 * TILE + 1, :], tall_ref[:, TILE - 1 : 2 * TILE - 1, :]
         result = force
         for k, field in enumerate((t, east, west, north, south)):
             result = result + points_ref[k] * field
         return result
 
-    t = advance(t, rim, north_one, south_one)
-    result_ref[...] = advance(t, listing(1, rim), north_next, south_next)
+    tall_ref[:, TILE : 2 * TILE, :] = advance(rim, north_one, south_one)
+    result_ref[...] = advance(listing(1, rim), north_next, south_next)
     copies[1].start()
     for copy in copies:
         copy.wait()
@@ -405,6 +446,11 @@
 
 def exchange(blocks):
     return lax.all_to_all(blocks, ("ns", "ew"), split_axis=0, concat_axis=0, tiled=True)
+
+
+def swap(rows):
+    pairs = [(i, i + 1) for i in range(0, lax.axis_size("ns"), 2)]
+    return lax.ppermute(rows, "ns", pairs + [(b, a) for a, b in pairs])
 
 
 def local(theta, velocity, diffusivity, land_mask, fold_partner, atm_flux, remap_src, remap_weights):
@@ -412,31 +458,30 @@
     fields = atm_flux.shape[2]
     shape = jax.ShapeDtypeStruct
     devices = lax.axis_size("ew") * lax.axis_size("ns")
-    blocks = (devices, BLOCK, cols)
-    room = 60 * 2**20 - 2 * max(0, 2 * devices * BLOCK * cols - 2**20)
+    blocks = (devices, TILE, cols)
+    room = 60 * 2**20 - 2 * max(0, 4 * devices * TILE * cols - 2**20)
     weights = remap_weights[0, 0]
     field, velocity, diffusivity, flux = bring(
         [theta, velocity, diffusivity, atm_flux[0, 0]], [pltpu.VMEM] * 4, room, "bring"
     )
-    out = pl.pallas_call(
+    out, near = pl.pallas_call(
         first_kernel,
-        out_shape=pltpu.VMEM(blocks, BF16),
+        out_shape=(pltpu.VMEM(blocks, BF16), pltpu.VMEM((KINDS, levels, cols), F32)),
         in_specs=[SMEM] + [VMEM] * 4,
-        out_specs=VMEM,
-        scratch_shapes=[pltpu.VMEM((2 * KINDS * levels // TILE + 1, TILE, cols), F32)],
+        out_specs=(VMEM,) * 2,
+        scratch_shapes=[pltpu.VMEM((levels, TILE, cols), F32)],
         compiler_params=PARAMS,
         name="first",
     )(fold_partner, field, velocity, diffusivity, flux)
-    first = exchange(out)
+    first, near = exchange(out), swap(near)
     sources, weights = bring([remap_src[0], weights], [pltpu.SMEM, pltpu.VMEM], room, "load")
-    points, columns, rims, start = pl.pallas_call(
+    points, columns, start = pl.pallas_call(
         side_kernel,
         out_shape=(
-            pltpu.VMEM((5,) + theta.shape, F32), pltpu.VMEM((2, 3, cols), F32), pltpu.VMEM((2,) + theta.shape, F32),
-            pltpu.VMEM(theta.shape, F32),
+            pltpu.VMEM((5,) + theta.shape, F32), pltpu.VMEM((2, 3, cols), F32), pltpu.VMEM(theta.shape, F32),
         ),
         in_specs=[SMEM] + [VMEM] * 3,
-        out_specs=(VMEM,) * 4,
+        out_specs=(VMEM,) * 3,
         compiler_params=PARAMS,
         cost_estimate=pl.CostEstimate(flops=2**20, bytes_accessed=2**20, transcendentals=0),
         name="side",
@@ -447,24 +492,26 @@
             pltpu.VMEM((fields, rows * cols), F32), pltpu.VMEM((rows, cols), F32), pltpu.VMEM(theta.shape, F32),
             pltpu.VMEM((TILE, cols), F32), pltpu.VMEM(blocks, BF16),
         ),
-        in_specs=[SMEM] * 3 + [VMEM] * 5,
+        in_specs=[SMEM] * 3 + [VMEM] * 6,
         out_specs=(VMEM,) * 5,
+        scratch_shapes=[pltpu.VMEM(theta.shape, F32)] * 2,
         compiler_params=PARAMS,
         name="middle",
-    )(land_mask, fold_partner, sources, columns, rims, start, weights, first)
+    )(land_mask, fold_partner, sources, columns, points, start, weights, first, near)
     second = exchange(out)
     field, flux = pl.pallas_call(
         last_kernel,
         out_shape=(shape(theta.shape, F32), shape((fields, rows, cols), F32)),
-        in_specs=[SMEM] + [VMEM] * 8,
+        in_specs=[SMEM] + [VMEM] * 9,
         out_specs=(HBM, HBM),
         scratch_shapes=[
             pltpu.VMEM(theta.shape, F32), pltpu.VMEM((fields, rows, cols), F32), pltpu.VMEM(theta.shape, F32),
+            pltpu.VMEM((levels, 3 * TILE, cols), F32), pltpu.VMEM((levels, TILE, cols), F32),
             pltpu.SemaphoreType.DMA((2,)),
         ],
         compiler_params=PARAMS,
         name="last",
-    )(fold_partner, field, points, total, after, ends, force, first, second)
+    )(fold_partner, field, points, total, after, ends, force, first, second, near)
     return field, flux.reshape(1, 1, fields, rows * cols)
 
 

time: 30 us -> 28.8 us (0.960)
  blocking collectives: 10 us -> 8.97 us
  waiting for transfers between devices: 5.66 us -> 4.87 us
  starting transfers between devices: 7.3 us -> 7.61 us
    all_to_all x1, blocking collectives: 10 us -> 8.97 us  [exchange(): lax.all_to_all(blocks, ('ns', 'ew'), split_axis=0, concat_axis=0, tiled=T...]
    all_to_all x1, waiting for transfers between devices: 5.66 us -> 4.86 us  [exchange(): lax.all_to_all(blocks, ('ns', 'ew'), split_axis=0, concat_axis=0, tiled=T...]
    ppermute x0 -> x1, starting transfers between devices: none -> 0.32 us  [swap(): return lax.ppermute(rows, 'ns', pairs + [(b, a) for a, b in pairs])]
  transfers between devices with their start and end apart: 1 -> 2, of which waited for: 1 -> 1; matrix products, arithmetic and copies ran while one was open for 0% -> 0% of each run, Pallas kernels for 5% -> 5%
where the time goes in v5:
time: 28.8 us; the launch traced here: 28.5 us
  blocking collectives  8.97 us (31%)
  starting transfers between devices  7.61 us (26%)
  Pallas kernels  5.12 us (18%)
  waiting for transfers between devices  4.87 us (17%)
  between operations  1.97 us (7%)
    all_to_all x1, blocking collectives, exchange(): lax.all_to_all(blocks, ('ns', 'ew'), split_axis=0, concat_axis=0, tiled=T...  8.97 us
    all_to_all x1, starting transfers between devices, exchange(): lax.all_to_all(blocks, ('ns', 'ew'), split_axis=0, concat_axis=0, tiled=T...  7.3 us
    all_to_all x1, waiting for transfers between devices, exchange(): lax.all_to_all(blocks, ('ns', 'ew'), split_axis=0, concat_axis=0, tiled=T...  4.86 us
    pallas_call x2, Pallas kernels, bring(): pl.pallas_call(functools.partial(bring_kernel, len(arrays)), out_shape=tu...  2.23 us
    pallas_call x1, Pallas kernels, local(): pl.pallas_call(last_kernel, out_shape=(shape(theta.shape, F32), shape((fi...  1.18 us
    pallas_call x1, Pallas kernels, local(): pl.pallas_call(first_kernel, out_shape=(pltpu.VMEM(blocks, BF16), pltpu.V...  1.02 us
  transfers between devices with their start and end apart: 2, of which 1 were waited for; matrix products, arithmetic and copies ran while one was open for 0% of the time, Pallas kernels for 5%

profile of v5, /device:TPU:0, one launch (start us, length us, event | category | flops | bytes accessed | tf_op | source)
XLA Modules:
  0.0 28.5 jit_solution(16346273552221245168)
XLA Ops:
  1.3 1.0 %bring.1 = (f32[16,8,128]{2,1,0:T(8,128)S(1)}, f32[2,16,8,128]{3,2,1,0:T(8,128)S(1)}, f32[16,8,128]{2,1,0:T(8,128)S(1)}, bf16[6,128]{1,0:T(8,128)(2,1)S(1)}) custom-call(f32[16,8,128]{2,1,0:T(8,128)} %refs_0_.1, f32[2,16,8,128]{3,2,1,0:T(8,128)} %refs_1_.1, f32[16,8,128]{2,1,0:T(8,128)} %refs_2_.1, bf16[6,128]{1,0:T(8,128)(2,1)} %bitcast.5), custom_call_target="tpu_custom_call" | custom-call | flops 1048576 | bytes 4194304 | tf_op jit(solution)/shard_map/bring/pallas_call | solution.py:101
  2.3 1.0 %first.1 = (bf16[32,8,128]{2,1,0:T(8,128)(2,1)}, f32[6,16,128]{2,1,0:T(8,128)S(1)}) custom-call(s32[1]{0:T(128)S(6)} %copy.13.partner_ref, f32[16,8,128]{2,1,0:T(8,128)S(1)} %get-tuple-element.20.theta_ref, f32[2,16,8,128]{3,2,1,0:T(8,128)S(1)} %get-tuple-element.21.vel_ref, f32[16,8,128]{2,1,0:T(8,128)S(1)} %get-tuple-element.22.diff_ref, ...), custom_call_target="tpu_custom_call" | custom-call | tf_op jit(solution)/shard_map/first/pallas_call | solution.py:467
  3.3 7.3 %all-to-all-start = ((bf16[32,8,128]{2,1,0:T(8,128)(2,1)}), bf16[32,8,128]{2,1,0:T(8,128)(2,1)S(1)}, u32[]{:S(2)}, u32[]{:S(2)}) async-start(bf16[32,8,128]{2,1,0:T(8,128)(2,1)} %get-tuple-element.29), calls=%async_computation | async-start | bytes 131072 | tf_op jit(solution)/shard_map/all_to_all | solution.py:448
  10.6 0.3 %collective-permute-start = (f32[6,16,128]{2,1,0:T(8,128)S(1)}, f32[6,16,128]{2,1,0:T(8,128)S(1)}, u32[]{:S(2)}, u32[]{:S(2)}) collective-permute-start(f32[6,16,128]{2,1,0:T(8,128)S(1)} %get-tuple-element.30), channel_id=1, source_target_pairs={{0,1},{2,3},{1,0},{3,2},{4,5},{6,7},{5,4},{7,6},{8,9},{10,11},{9,8... | collective-permute-start | bytes 147464 | tf_op jit(solution)/shard_map/ppermute | solution.py:453
  11.6 0.2 side.1
  11.7 1.2 %load.1 = (s32[1,4]{1,0:T(1,128)S(4)}, bf16[4,128,1024]{2,1,0:T(8,128)(2,1)S(1)}) custom-call(s32[1,4]{1,0:T(1,128)} %bitcast.6, bf16[4,128,1024]{2,1,0:T(8,128)(2,1)} %bitcast.4), custom_call_target="tpu_custom_call" | custom-call | flops 1048576 | bytes 4194304 | tf_op jit(solution)/shard_map/load/pallas_call | solution.py:101
  13.0 0.0 collective-permute-done.near_ref
  13.0 4.9 %all-to-all-done.recv_ref.first_ref = bf16[32,8,128]{2,1,0:T(8,128)(2,1)S(1)} async-done(((bf16[32,8,128]{2,1,0:T(8,128)(2,1)}), bf16[32,8,128]{2,1,0:T(8,128)(2,1)S(1)}, u32[]{:S(2)}, u32[]{:S(2)}) %all-to-all-start) | async-done | bytes 65568 | tf_op jit(solution)/shard_map/all_to_all | solution.py:448
  17.9 0.5 %middle.1 = (f32[6,1024]{1,0:T(8,128)S(1)}, f32[8,128]{1,0:T(8,128)S(1)}, f32[16,8,128]{2,1,0:T(8,128)S(1)}, f32[8,128]{1,0:T(8,128)S(1)}, bf16[32,8,128]{2,1,0:T(8,128)(2,1)S(1)}) custom-call(s32[1,1]{1,0:T(1,128)S(6)} %copy.12.mask_ref, s32[1]{0:T(128)S(6)} %copy.13.partner_ref, s32[1,4]{1,0:T(1,128)S(4)} %get-tuple-element.24.src_ref, ...), custom_call_target="tpu_custom_call" | custom-call | tf_op jit(solution)/shard_map/middle/pallas_call | solution.py:489
  18.4 9.0 %all_to_all.10.second_ref = bf16[32,8,128]{2,1,0:T(8,128)(2,1)S(1)} all-to-all(bf16[32,8,128]{2,1,0:T(8,128)(2,1)S(1)} %get-tuple-element.35), channel_id=1, replica_groups=mesh['ew'=8,'ns'=4] {'ns','ew'}, dimensions={0} | all-to-all | bytes 131072 | tf_op jit(solution)/shard_map/all_to_all | solution.py:448
  27.4 1.2 %last.1 = (f32[16,8,128]{2,1,0:T(8,128)}, f32[6,8,128]{2,1,0:T(8,128)}) custom-call(s32[1]{0:T(128)S(6)} %copy.13.partner_ref, f32[16,8,128]{2,1,0:T(8,128)S(1)} %get-tuple-element.20.theta_ref, f32[5,16,8,128]{3,2,1,0:T(8,128)S(1)} %get-tuple-element.23.points_ref, f32[6,1024]{1,0:T(8,128)S(1)} %get-tuple-element.31.total_ref, ...), custom_call_target="tpu_custom_call" | custom-call | tf_op jit(solution)/shard_map/last/pallas_call | solution.py:502
Async XLA Ops:
  3.3 14.6 %all-to-all-start = ((bf16[32,8,128]{2,1,0:T(8,128)(2,1)}), bf16[32,8,128]{2,1,0:T(8,128)(2,1)S(1)}, u32[]{:S(2)}, u32[]{:S(2)}) async-start(bf16[32,8,128]{2,1,0:T(8,128)(2,1)} %get-tuple-element.29), calls=%async_computation | async-start | bytes 131072 | tf_op jit(solution)/shard_map/all_to_all | solution.py:448
  10.6 2.4 %collective-permute-start = (f32[6,16,128]{2,1,0:T(8,128)S(1)}, f32[6,16,128]{2,1,0:T(8,128)S(1)}, u32[]{:S(2)}, u32[]{:S(2)}) collective-permute-start(f32[6,16,128]{2,1,0:T(8,128)S(1)} %get-tuple-element.30), channel_id=1, source_target_pairs={{0,1},{2,3},{1,0},{3,2},{4,5},{6,7},{5,4},{7,6},{8,9},{10,11},{9,8... | collective-permute-start | bytes 147464 | tf_op jit(solution)/shard_map/ppermute | solution.py:453

commit v6 on v5

--- a/solution.py
+++ b/solution.py
@@ -116,6 +116,7 @@
     tiles = levels // TILE
     each = KINDS * tiles
     coef_refs = [vel_ref.at[0], vel_ref.at[1], diff_ref]
+    turned = turn(theta_ref[...])
     strips = []
     for step in (1, -1):
         edge = rows - 1 if step < 0 else 0
@@ -129,15 +130,11 @@
         far = jnp.where(here.even, low, high)
         bulk_ref[pl.ds(kind * tiles, tiles)] = far.reshape(tiles, TILE, cols)
     partner = partner_ref[0].astype(F32)
-
-    @pl.when(here.is_top)
-    def _():
-        for kind in range(KINDS):
-            write_row(bulk_ref, kind, strips[1][kind])
-        write_row(bulk_ref, KINDS, jnp.full((levels, cols), partner))
-        write_row(bulk_ref, KINDS + 1, jnp.zeros((levels, cols), F32))
-
-    turned = turn(theta_ref[...])
+    fold_ref = bulk_ref.at[pl.ds(levels, levels)]
+    for kind in range(KINDS):
+        write_row(fold_ref, kind, strips[1][kind])
+    write_row(fold_ref, KINDS, jnp.full((levels, cols), partner))
+    write_row(fold_ref, KINDS + 1, jnp.zeros((levels, cols), F32))
     lane = lax.broadcasted_iota(jnp.int32, (TILE, cols), 1)
     slot = lax.rem(lane, 8)
     spots = [turned[0:1], turned[1:2], turned[cols - 2 : cols - 1], turned[cols - 1 : cols]]
@@ -152,9 +149,11 @@
     to_east = jnp.concatenate([corner, turned[cols - 1 : cols], atm], axis=0)
     column = jnp.where(here.is_top, partner_ref[0], here.e)
     first, _, skip = relays(jnp.where(here.is_top, here.top, here.other), here.block_rows)
+    begin = jnp.where(here.is_top, levels, 0)
     for e in range(here.count):
         ahead = lax.rem(e - column + here.count, here.count)
-        whole, some = jnp.minimum(ahead, TILE - 1), jnp.clip(ahead + TILE - skip, 0, levels - 1)
+        whole = begin + jnp.minimum(ahead, TILE - 1)
+        some = begin + jnp.clip(ahead + TILE - skip, 0, levels - 1)
         own = jnp.where(e == here.east, to_east, to_west)
         for n in range(here.block_rows):
             tile = bulk_ref[jnp.where(first == n, whole, some)]
@@ -469,7 +468,7 @@
         out_shape=(pltpu.VMEM(blocks, BF16), pltpu.VMEM((KINDS, levels, cols), F32)),
         in_specs=[SMEM] + [VMEM] * 4,
         out_specs=(VMEM,) * 2,
-        scratch_shapes=[pltpu.VMEM((levels, TILE, cols), F32)],
+        scratch_shapes=[pltpu.VMEM((2 * levels, TILE, cols), F32)],
         compiler_params=PARAMS,
         name="first",
     )(fold_partner, field, velocity, diffusivity, flux)

time: 28.8 us -> 28.7 us (level)
  no operation moved by 1% of the time
where the time goes in v6:
time: 28.7 us; the launch traced here: 28.5 us
  blocking collectives  8.97 us (31%)
  starting transfers between devices  7.61 us (27%)
  Pallas kernels  5.04 us (18%)
  waiting for transfers between devices  4.87 us (17%)
  between operations  1.97 us (7%)
    all_to_all x1, blocking collectives, exchange(): lax.all_to_all(blocks, ('ns', 'ew'), split_axis=0, concat_axis=0, tiled=T...  8.97 us
    all_to_all x1, starting transfers between devices, exchange(): lax.all_to_all(blocks, ('ns', 'ew'), split_axis=0, concat_axis=0, tiled=T...  7.3 us
    all_to_all x1, waiting for transfers between devices, exchange(): lax.all_to_all(blocks, ('ns', 'ew'), split_axis=0, concat_axis=0, tiled=T...  4.86 us
    pallas_call x2, Pallas kernels, bring(): pl.pallas_call(functools.partial(bring_kernel, len(arrays)), out_shape=tu...  2.23 us
    pallas_call x1, Pallas kernels, local(): pl.pallas_call(last_kernel, out_shape=(shape(theta.shape, F32), shape((fi...  1.18 us
    pallas_call x1, Pallas kernels, local(): pl.pallas_call(first_kernel, out_shape=(pltpu.VMEM(blocks, BF16), pltpu.V...  0.95 us
  transfers between devices with their start and end apart: 2, of which 1 were waited for; matrix products, arithmetic and copies ran while one was open for 0% of the time, Pallas kernels for 5%

profile of v6, /device:TPU:0, one launch (start us, length us, event | category | flops | bytes accessed | tf_op | source)
XLA Modules:
  0.0 28.5 jit_solution(14178174460966877070)
XLA Ops:
  1.3 1.0 %bring.1 = (f32[16,8,128]{2,1,0:T(8,128)S(1)}, f32[2,16,8,128]{3,2,1,0:T(8,128)S(1)}, f32[16,8,128]{2,1,0:T(8,128)S(1)}, bf16[6,128]{1,0:T(8,128)(2,1)S(1)}) custom-call(f32[16,8,128]{2,1,0:T(8,128)} %refs_0_.1, f32[2,16,8,128]{3,2,1,0:T(8,128)} %refs_1_.1, f32[16,8,128]{2,1,0:T(8,128)} %refs_2_.1, bf16[6,128]{1,0:T(8,128)(2,1)} %bitcast.5), custom_call_target="tpu_custom_call" | custom-call | flops 1048576 | bytes 4194304 | tf_op jit(solution)/shard_map/bring/pallas_call | solution.py:101
  2.3 0.9 %first.1 = (bf16[32,8,128]{2,1,0:T(8,128)(2,1)}, f32[6,16,128]{2,1,0:T(8,128)S(1)}) custom-call(s32[1]{0:T(128)S(6)} %copy.13.partner_ref, f32[16,8,128]{2,1,0:T(8,128)S(1)} %get-tuple-element.20.theta_ref, f32[2,16,8,128]{3,2,1,0:T(8,128)S(1)} %get-tuple-element.21.vel_ref, f32[16,8,128]{2,1,0:T(8,128)S(1)} %get-tuple-element.22.diff_ref, ...), custom_call_target="tpu_custom_call" | custom-call | tf_op jit(solution)/shard_map/first/pallas_call | solution.py:466
  3.2 7.3 %all-to-all-start = ((bf16[32,8,128]{2,1,0:T(8,128)(2,1)}), bf16[32,8,128]{2,1,0:T(8,128)(2,1)S(1)}, u32[]{:S(2)}, u32[]{:S(2)}) async-start(bf16[32,8,128]{2,1,0:T(8,128)(2,1)} %get-tuple-element.29), calls=%async_computation | async-start | bytes 131072 | tf_op jit(solution)/shard_map/all_to_all | solution.py:447
  10.5 0.3 %collective-permute-start = (f32[6,16,128]{2,1,0:T(8,128)S(1)}, f32[6,16,128]{2,1,0:T(8,128)S(1)}, u32[]{:S(2)}, u32[]{:S(2)}) collective-permute-start(f32[6,16,128]{2,1,0:T(8,128)S(1)} %get-tuple-element.30), channel_id=1, source_target_pairs={{0,1},{2,3},{1,0},{3,2},{4,5},{6,7},{5,4},{7,6},{8,9},{10,11},{9,8... | collective-permute-start | bytes 147464 | tf_op jit(solution)/shard_map/ppermute | solution.py:452
  11.5 0.2 side.1
  11.7 1.2 %load.1 = (s32[1,4]{1,0:T(1,128)S(4)}, bf16[4,128,1024]{2,1,0:T(8,128)(2,1)S(1)}) custom-call(s32[1,4]{1,0:T(1,128)} %bitcast.6, bf16[4,128,1024]{2,1,0:T(8,128)(2,1)} %bitcast.4), custom_call_target="tpu_custom_call" | custom-call | flops 1048576 | bytes 4194304 | tf_op jit(solution)/shard_map/load/pallas_call | solution.py:101
  12.9 0.0 collective-permute-done.near_ref
  12.9 4.9 %all-to-all-done.recv_ref.first_ref = bf16[32,8,128]{2,1,0:T(8,128)(2,1)S(1)} async-done(((bf16[32,8,128]{2,1,0:T(8,128)(2,1)}), bf16[32,8,128]{2,1,0:T(8,128)(2,1)S(1)}, u32[]{:S(2)}, u32[]{:S(2)}) %all-to-all-start) | async-done | bytes 65568 | tf_op jit(solution)/shard_map/all_to_all | solution.py:447
  17.8 0.5 %middle.1 = (f32[6,1024]{1,0:T(8,128)S(1)}, f32[8,128]{1,0:T(8,128)S(1)}, f32[16,8,128]{2,1,0:T(8,128)S(1)}, f32[8,128]{1,0:T(8,128)S(1)}, bf16[32,8,128]{2,1,0:T(8,128)(2,1)S(1)}) custom-call(s32[1,1]{1,0:T(1,128)S(6)} %copy.12.mask_ref, s32[1]{0:T(128)S(6)} %copy.13.partner_ref, s32[1,4]{1,0:T(1,128)S(4)} %get-tuple-element.24.src_ref, ...), custom_call_target="tpu_custom_call" | custom-call | tf_op jit(solution)/shard_map/middle/pallas_call | solution.py:488
  18.3 9.0 %all_to_all.10.second_ref = bf16[32,8,128]{2,1,0:T(8,128)(2,1)S(1)} all-to-all(bf16[32,8,128]{2,1,0:T(8,128)(2,1)S(1)} %get-tuple-element.35), channel_id=1, replica_groups=mesh['ew'=8,'ns'=4] {'ns','ew'}, dimensions={0} | all-to-all | bytes 131072 | tf_op jit(solution)/shard_map/all_to_all | solution.py:447
  27.3 1.2 %last.1 = (f32[16,8,128]{2,1,0:T(8,128)}, f32[6,8,128]{2,1,0:T(8,128)}) custom-call(s32[1]{0:T(128)S(6)} %copy.13.partner_ref, f32[16,8,128]{2,1,0:T(8,128)S(1)} %get-tuple-element.20.theta_ref, f32[5,16,8,128]{3,2,1,0:T(8,128)S(1)} %get-tuple-element.23.points_ref, f32[6,1024]{1,0:T(8,128)S(1)} %get-tuple-element.31.total_ref, ...), custom_call_target="tpu_custom_call" | custom-call | tf_op jit(solution)/shard_map/last/pallas_call | solution.py:501
Async XLA Ops:
  3.2 14.6 %all-to-all-start = ((bf16[32,8,128]{2,1,0:T(8,128)(2,1)}), bf16[32,8,128]{2,1,0:T(8,128)(2,1)S(1)}, u32[]{:S(2)}, u32[]{:S(2)}) async-start(bf16[32,8,128]{2,1,0:T(8,128)(2,1)} %get-tuple-element.29), calls=%async_computation | async-start | bytes 131072 | tf_op jit(solution)/shard_map/all_to_all | solution.py:447
  10.5 2.4 %collective-permute-start = (f32[6,16,128]{2,1,0:T(8,128)S(1)}, f32[6,16,128]{2,1,0:T(8,128)S(1)}, u32[]{:S(2)}, u32[]{:S(2)}) collective-permute-start(f32[6,16,128]{2,1,0:T(8,128)S(1)} %get-tuple-element.30), channel_id=1, source_target_pairs={{0,1},{2,3},{1,0},{3,2},{4,5},{6,7},{5,4},{7,6},{8,9},{10,11},{9,8... | collective-permute-start | bytes 147464 | tf_op jit(solution)/shard_map/ppermute | solution.py:452

commit v7 on v6

--- a/solution.py
+++ b/solution.py
@@ -35,22 +35,25 @@
         self.top = self.block_rows - 1
         self.is_top = self.n == self.top
         self.has_south = self.n > 0
-        self.even = lax.rem(self.n, 2) == 0
-        self.east = lax.rem(self.e + 1, self.count)
-        self.west = lax.rem(self.e + self.count - 1, self.count)
+        self.even = (self.n & 1) == 0
+        self.east, self.west = self.wrap(self.e + 1), self.wrap(self.e + self.count - 1)
         self.above = jnp.minimum(self.n + 1, self.top)
         self.below = jnp.maximum(self.n - 1, 0)
         self.pair = jnp.where(self.even, self.n + 1, self.n - 1)
         self.other = jnp.where(self.even, self.below, self.above)
 
+    def wrap(self, e):
+        return jnp.where(e >= self.count, e - self.count, e)
+
     def slot(self, e, n):
         return n * self.count + e
 
 
 def relays(row, block_rows):
     is_top = row == block_rows - 1
-    first = jnp.where((row % 2 == 0) | is_top, jnp.maximum(row - 2, 0), row + 2)
-    return first, jnp.where(is_top, jnp.maximum(row - 3, 0), row + 1 - 2 * (row % 2)), jnp.where(is_top, 0, 2)
+    odd = row & 1
+    first = jnp.where((odd == 0) | is_top, jnp.maximum(row - 2, 0), row + 2)
+    return first, jnp.where(is_top, jnp.maximum(row - 3, 0), row + 1 - 2 * odd), jnp.where(is_top, 0, 2)
 
 
 def fill(size, rows):
@@ -136,7 +139,7 @@
     write_row(fold_ref, KINDS, jnp.full((levels, cols), partner))
     write_row(fold_ref, KINDS + 1, jnp.zeros((levels, cols), F32))
     lane = lax.broadcasted_iota(jnp.int32, (TILE, cols), 1)
-    slot = lax.rem(lane, 8)
+    slot = lane & 7
     spots = [turned[0:1], turned[1:2], turned[cols - 2 : cols - 1], turned[cols - 1 : cols]]
     spots = jnp.concatenate(spots + [jnp.zeros((TILE - 4, cols), F32)], axis=0)
     spots = jnp.where(here.even, spots, pltpu.roll(spots, cols - rows + 1, 1))
@@ -148,17 +151,17 @@
     to_west = jnp.concatenate([corner, turned[0:1], atm], axis=0)
     to_east = jnp.concatenate([corner, turned[cols - 1 : cols], atm], axis=0)
     column = jnp.where(here.is_top, partner_ref[0], here.e)
-    first, _, skip = relays(jnp.where(here.is_top, here.top, here.other), here.block_rows)
+    first, second, skip = relays(jnp.where(here.is_top, here.top, here.other), here.block_rows)
     begin = jnp.where(here.is_top, levels, 0)
     for e in range(here.count):
-        ahead = lax.rem(e - column + here.count, here.count)
-        whole = begin + jnp.minimum(ahead, TILE - 1)
-        some = begin + jnp.clip(ahead + TILE - skip, 0, levels - 1)
-        own = jnp.where(e == here.east, to_east, to_west)
-        for n in range(here.block_rows):
-            tile = bulk_ref[jnp.where(first == n, whole, some)]
-            owed = (here.n == n) | ((here.other == n) & (here.e == e))
-            out_ref[n * here.count + e] = jnp.where(owed, own, tile).astype(BF16)
+        ahead = here.wrap(e - column + here.count)
+        out_ref[here.slot(e, first)] = bulk_ref[begin + jnp.minimum(ahead, TILE - 1)].astype(BF16)
+        out_ref[here.slot(e, second)] = bulk_ref[begin + jnp.minimum(ahead + TILE - skip, levels - 1)].astype(BF16)
+    to_west, to_east = to_west.astype(BF16), to_east.astype(BF16)
+    out_ref[here.slot(here.e, here.other)] = to_west
+    for e in range(here.count):
+        out_ref[here.slot(e, here.n)] = to_west
+    out_ref[here.slot(here.east, here.n)] = to_east
 
 
 def side_kernel(
@@ -238,7 +241,7 @@
     tiles = held + [jnp.zeros((size - here.count * TILE, cols), F32)] * (size > here.count * TILE)
     tiles = jnp.concatenate(tiles, axis=0).astype(BF16)
     partners = jnp.concatenate([jnp.broadcast_to(block[KINDS : KINDS + 1, 0:1], (TILE, 1)) for block in held], axis=0)
-    wanted = TILE * partners + lax.rem(lax.broadcasted_iota(jnp.int32, partners.shape, 0), TILE).astype(F32)
+    wanted = TILE * partners + (lax.broadcasted_iota(jnp.int32, partners.shape, 0) & (TILE - 1)).astype(F32)
     pick = lax.broadcasted_iota(jnp.int32, (here.count * TILE, size), 1).astype(F32) == wanted
     folded = jnp.dot(pick.astype(F32).astype(BF16), tiles, preferred_element_type=F32)
 
@@ -248,8 +251,8 @@
     forces = jnp.concatenate([force, jnp.zeros((cols - rows, cols), F32)], axis=0).T
     forces = jnp.concatenate([forces[0:1], forces[cols - 1 : cols], jnp.zeros((TILE - 2, cols), F32)], axis=0)
     ends_ref[...] = ends
-    marks = jnp.take_along_axis(forces, lane // 8, axis=1)
-    slot = lax.rem(lane, 8)
+    marks = jnp.take_along_axis(forces, lane >> 3, axis=1)
+    slot = lane & 7
     marks = jnp.where(slot == FORCE_SLOT, marks, jnp.where(slot == WET_SLOT, wet, 0.0))
     slot = slot[0:1]
 
@@ -269,8 +272,7 @@
     to_east = jnp.concatenate([corners(up, high_mark)] + high_force + high + [high_coef], axis=0)
     to_below = jnp.concatenate([corners(down, low_mark)] + low_force + low + [low_coef], axis=0)
     for e in range(here.count):
-        ahead = lax.rem(e - here.e + here.count, here.count)
-        close = (ahead <= 1) | (ahead == here.count - 1)
+        close = (e == here.e) | (e == here.east) | (e == here.west)
         for n in range(here.block_rows):
             begin = jnp.where(n == here.n - 1, to_below, jnp.where(e == here.east, to_east, base))
             owed = (n == here.n) | (close & ((n == here.n - 1) | (n == here.n + 1)))
@@ -304,8 +306,8 @@
     west, east = got(here.west, here.n), got(here.east, here.n)
     over, under = got(here.e, here.above), got(here.e, here.below)
     fold = got(partner, here.n)
-    fold_east = got(lax.rem(partner + 1, here.count), here.n)[0:1]
-    fold_west = got(lax.rem(partner + here.count - 1, here.count), here.n)[0:1]
+    fold_east = got(here.wrap(partner + 1), here.n)[0:1]
+    fold_west = got(here.wrap(partner + here.count - 1), here.n)[0:1]
     over_west, over_east = got(here.west, here.above)[0:1], got(here.east, here.above)[0:1]
     under_west, under_east = got(here.west, here.below)[0:1], got(here.east, here.below)[0:1]
     first_west = first_ref[here.slot(here.west, here.n)].astype(F32)
@@ -317,7 +319,7 @@
     first, second, skip = relays(here.n, here.block_rows)
     for k in range(levels):
         ahead, row = (k, first) if k < TILE else (k - TILE + skip, second)
-        tile_ref[k] = got(lax.rem(here.e + ahead, here.count), row)
+        tile_ref[k] = got(here.wrap(here.e + jnp.minimum(ahead, here.count - 1)), row)
     tiles = levels // TILE
     far = [tile_ref[pl.ds(kind * tiles, tiles)].reshape(levels, cols) for kind in range(KINDS)]
     far = jnp.concatenate(far, axis=0)
@@ -348,7 +350,7 @@
         return jnp.concatenate([low, high, jnp.zeros((TILE - 2, cols), F32)], axis=0)
 
     along = lax.broadcasted_iota(jnp.int32, (TILE, cols), 1)
-    place = lax.rem(along, rows)
+    place = along & 7
     side = pair(west[3:4], east[3:4])
     corner = pair(jnp.where(is_top, top_west, moved[4:5]), jnp.where(is_top, moved[6:7], over_east))
     side_north = jnp.where(place == last, pltpu.roll(corner, last, 1), shifted(side, 1, True))

time: 28.7 us -> 28.6 us (level)
  no operation moved by 1% of the time
where the time goes in v7:
time: 28.6 us; the launch traced here: 28.4 us
  blocking collectives  8.97 us (31%)
  starting transfers between devices  7.61 us (27%)
  Pallas kernels  4.98 us (17%)
  waiting for transfers between devices  4.87 us (17%)
  between operations  1.97 us (7%)
    all_to_all x1, blocking collectives, exchange(): lax.all_to_all(blocks, ('ns', 'ew'), split_axis=0, concat_axis=0, tiled=T...  8.97 us
    all_to_all x1, starting transfers between devices, exchange(): lax.all_to_all(blocks, ('ns', 'ew'), split_axis=0, concat_axis=0, tiled=T...  7.3 us
    all_to_all x1, waiting for transfers between devices, exchange(): lax.all_to_all(blocks, ('ns', 'ew'), split_axis=0, concat_axis=0, tiled=T...  4.86 us
    pallas_call x2, Pallas kernels, bring(): pl.pallas_call(functools.partial(bring_kernel, len(arrays)), out_shape=tu...  2.23 us
    pallas_call x1, Pallas kernels, local(): pl.pallas_call(last_kernel, out_shape=(shape(theta.shape, F32), shape((fi...  1.19 us
    pallas_call x1, Pallas kernels, local(): pl.pallas_call(first_kernel, out_shape=(pltpu.VMEM(blocks, BF16), pltpu.V...  0.88 us
  transfers between devices with their start and end apart: 2, of which 1 were waited for; matrix products, arithmetic and copies ran while one was open for 0% of the time, Pallas kernels for 5%

profile of v7, /device:TPU:0, one launch (start us, length us, event | category | flops | bytes accessed | tf_op | source)
XLA Modules:
  0.0 28.4 jit_solution(15362473720708731451)
XLA Ops:
  1.3 1.0 %bring.1 = (f32[16,8,128]{2,1,0:T(8,128)S(1)}, f32[2,16,8,128]{3,2,1,0:T(8,128)S(1)}, f32[16,8,128]{2,1,0:T(8,128)S(1)}, bf16[6,128]{1,0:T(8,128)(2,1)S(1)}) custom-call(f32[16,8,128]{2,1,0:T(8,128)} %refs_0_.1, f32[2,16,8,128]{3,2,1,0:T(8,128)} %refs_1_.1, f32[16,8,128]{2,1,0:T(8,128)} %refs_2_.1, bf16[6,128]{1,0:T(8,128)(2,1)} %bitcast.5), custom_call_target="tpu_custom_call" | custom-call | flops 1048576 | bytes 4194304 | tf_op jit(solution)/shard_map/bring/pallas_call | solution.py:104
  2.3 0.9 %first.1 = (bf16[32,8,128]{2,1,0:T(8,128)(2,1)}, f32[6,16,128]{2,1,0:T(8,128)S(1)}) custom-call(s32[1]{0:T(128)S(6)} %copy.13.partner_ref, f32[16,8,128]{2,1,0:T(8,128)S(1)} %get-tuple-element.20.theta_ref, f32[2,16,8,128]{3,2,1,0:T(8,128)S(1)} %get-tuple-element.21.vel_ref, f32[16,8,128]{2,1,0:T(8,128)S(1)} %get-tuple-element.22.diff_ref, ...), custom_call_target="tpu_custom_call" | custom-call | tf_op jit(solution)/shard_map/first/pallas_call | solution.py:468
  3.1 7.3 %all-to-all-start = ((bf16[32,8,128]{2,1,0:T(8,128)(2,1)}), bf16[32,8,128]{2,1,0:T(8,128)(2,1)S(1)}, u32[]{:S(2)}, u32[]{:S(2)}) async-start(bf16[32,8,128]{2,1,0:T(8,128)(2,1)} %get-tuple-element.29), calls=%async_computation | async-start | bytes 131072 | tf_op jit(solution)/shard_map/all_to_all | solution.py:449
  10.5 0.3 %collective-permute-start = (f32[6,16,128]{2,1,0:T(8,128)S(1)}, f32[6,16,128]{2,1,0:T(8,128)S(1)}, u32[]{:S(2)}, u32[]{:S(2)}) collective-permute-start(f32[6,16,128]{2,1,0:T(8,128)S(1)} %get-tuple-element.30), channel_id=1, source_target_pairs={{0,1},{2,3},{1,0},{3,2},{4,5},{6,7},{5,4},{7,6},{8,9},{10,11},{9,8... | collective-permute-start | bytes 147464 | tf_op jit(solution)/shard_map/ppermute | solution.py:454
  11.4 0.2 side.1
  11.6 1.2 %load.1 = (s32[1,4]{1,0:T(1,128)S(4)}, bf16[4,128,1024]{2,1,0:T(8,128)(2,1)S(1)}) custom-call(s32[1,4]{1,0:T(1,128)} %bitcast.6, bf16[4,128,1024]{2,1,0:T(8,128)(2,1)} %bitcast.4), custom_call_target="tpu_custom_call" | custom-call | flops 1048576 | bytes 4194304 | tf_op jit(solution)/shard_map/load/pallas_call | solution.py:104
  12.9 0.0 collective-permute-done.near_ref
  12.9 4.9 %all-to-all-done.recv_ref.first_ref = bf16[32,8,128]{2,1,0:T(8,128)(2,1)S(1)} async-done(((bf16[32,8,128]{2,1,0:T(8,128)(2,1)}), bf16[32,8,128]{2,1,0:T(8,128)(2,1)S(1)}, u32[]{:S(2)}, u32[]{:S(2)}) %all-to-all-start) | async-done | bytes 65568 | tf_op jit(solution)/shard_map/all_to_all | solution.py:449
  17.7 0.5 %middle.1 = (f32[6,1024]{1,0:T(8,128)S(1)}, f32[8,128]{1,0:T(8,128)S(1)}, f32[16,8,128]{2,1,0:T(8,128)S(1)}, f32[8,128]{1,0:T(8,128)S(1)}, bf16[32,8,128]{2,1,0:T(8,128)(2,1)S(1)}) custom-call(s32[1,1]{1,0:T(1,128)S(6)} %copy.12.mask_ref, s32[1]{0:T(128)S(6)} %copy.13.partner_ref, s32[1,4]{1,0:T(1,128)S(4)} %get-tuple-element.24.src_ref, ...), custom_call_target="tpu_custom_call" | custom-call | tf_op jit(solution)/shard_map/middle/pallas_call | solution.py:490
  18.2 9.0 %all_to_all.10.second_ref = bf16[32,8,128]{2,1,0:T(8,128)(2,1)S(1)} all-to-all(bf16[32,8,128]{2,1,0:T(8,128)(2,1)S(1)} %get-tuple-element.35), channel_id=1, replica_groups=mesh['ew'=8,'ns'=4] {'ns','ew'}, dimensions={0} | all-to-all | bytes 131072 | tf_op jit(solution)/shard_map/all_to_all | solution.py:449
  27.2 1.2 %last.1 = (f32[16,8,128]{2,1,0:T(8,128)}, f32[6,8,128]{2,1,0:T(8,128)}) custom-call(s32[1]{0:T(128)S(6)} %copy.13.partner_ref, f32[16,8,128]{2,1,0:T(8,128)S(1)} %get-tuple-element.20.theta_ref, f32[5,16,8,128]{3,2,1,0:T(8,128)S(1)} %get-tuple-element.23.points_ref, f32[6,1024]{1,0:T(8,128)S(1)} %get-tuple-element.31.total_ref, ...), custom_call_target="tpu_custom_call" | custom-call | tf_op jit(solution)/shard_map/last/pallas_call | solution.py:503
Async XLA Ops:
  3.1 14.6 %all-to-all-start = ((bf16[32,8,128]{2,1,0:T(8,128)(2,1)}), bf16[32,8,128]{2,1,0:T(8,128)(2,1)S(1)}, u32[]{:S(2)}, u32[]{:S(2)}) async-start(bf16[32,8,128]{2,1,0:T(8,128)(2,1)} %get-tuple-element.29), calls=%async_computation | async-start | bytes 131072 | tf_op jit(solution)/shard_map/all_to_all | solution.py:449
  10.5 2.4 %collective-permute-start = (f32[6,16,128]{2,1,0:T(8,128)S(1)}, f32[6,16,128]{2,1,0:T(8,128)S(1)}, u32[]{:S(2)}, u32[]{:S(2)}) collective-permute-start(f32[6,16,128]{2,1,0:T(8,128)S(1)} %get-tuple-element.30), channel_id=1, source_target_pairs={{0,1},{2,3},{1,0},{3,2},{4,5},{6,7},{5,4},{7,6},{8,9},{10,11},{9,8... | collective-permute-start | bytes 147464 | tf_op jit(solution)/shard_map/ppermute | solution.py:454

commit v8 on v7

--- a/solution.py
+++ b/solution.py
@@ -92,29 +92,35 @@
     return pltpu.roll(field, size - 1 if back else 1, axis)
 
 
-def bring_kernel(count, *refs):
-    copies = [pltpu.make_async_copy(refs[i], refs[count + i], refs[-1].at[i]) for i in range(count)]
+def bring_kernel(count, skip, *refs):
+    copies = [pltpu.make_async_copy(refs[i], refs[count + skip + i], refs[-1].at[i]) for i in range(count)]
     for copy in copies:
         copy.start()
     for copy in copies:
         copy.wait()
 
 
-def bring(arrays, memories, room, name):
+def bring(arrays, memories, room, name, after=()):
     return pl.pallas_call(
-        functools.partial(bring_kernel, len(arrays)),
+        functools.partial(bring_kernel, len(arrays), len(after)),
         out_shape=tuple(memory(x.shape, x.dtype) for x, memory in zip(arrays, memories)),
-        in_specs=[HBM] * len(arrays),
+        in_specs=[HBM] * len(arrays) + [pl.BlockSpec(memory_space=pl.ANY)] * len(after),
         out_specs=tuple(VMEM if memory is pltpu.VMEM else SMEM for memory in memories),
         scratch_shapes=[pltpu.SemaphoreType.DMA((len(arrays),))],
         compiler_params=pltpu.CompilerParams(vmem_limit_bytes=room),
         cost_estimate=pl.CostEstimate(flops=2**20, bytes_accessed=2**22, transcendentals=0),
         name=name,
-    )(*arrays)
-
-
-def first_kernel(partner_ref, theta_ref, vel_ref, diff_ref, atm_ref, out_ref, near_ref, bulk_ref):
+    )(*arrays, *after)
+
+
+def first_kernel(
+    partner_ref, theta_ref, vel_ref, diff_ref, atm_ref, out_ref, near_ref, number_ref, token_ref, bulk_ref
+):
     here = Place()
+    partner = jnp.max(partner_ref[...].astype(F32))
+    partner_column = partner.astype(jnp.int32)
+    number_ref[0] = partner_column
+    token_ref[...] = jnp.zeros(token_ref.shape, F32)
     levels, rows, cols = theta_ref.shape
     tiles = levels // TILE
     each = KINDS * tiles
@@ -132,7 +138,6 @@
         near_ref[kind] = jnp.where(here.even, high, low)
         far = jnp.where(here.even, low, high)
         bulk_ref[pl.ds(kind * tiles, tiles)] = far.reshape(tiles, TILE, cols)
-    partner = partner_ref[0].astype(F32)
     fold_ref = bulk_ref.at[pl.ds(levels, levels)]
     for kind in range(KINDS):
         write_row(fold_ref, kind, strips[1][kind])
@@ -150,7 +155,7 @@
     atm = atm_ref[...].astype(F32)
     to_west = jnp.concatenate([corner, turned[0:1], atm], axis=0)
     to_east = jnp.concatenate([corner, turned[cols - 1 : cols], atm], axis=0)
-    column = jnp.where(here.is_top, partner_ref[0], here.e)
+    column = jnp.where(here.is_top, partner_column, here.e)
     first, second, skip = relays(jnp.where(here.is_top, here.top, here.other), here.block_rows)
     begin = jnp.where(here.is_top, levels, 0)
     for e in range(here.count):
@@ -165,7 +170,7 @@
 
 
 def side_kernel(
-    mask_ref, theta_ref, vel_ref, diff_ref, points_ref, columns_ref, start_ref
+    mask_ref, theta_ref, vel_ref, diff_ref, _, points_ref, columns_ref, start_ref
 ):
     levels, rows, cols = theta_ref.shape
     last = rows - 1
@@ -462,31 +467,35 @@
     blocks = (devices, TILE, cols)
     room = 60 * 2**20 - 2 * max(0, 4 * devices * TILE * cols - 2**20)
     weights = remap_weights[0, 0]
+    near_partner = swap(fold_partner).reshape(1, 1)
     field, velocity, diffusivity, flux = bring(
         [theta, velocity, diffusivity, atm_flux[0, 0]], [pltpu.VMEM] * 4, room, "bring"
     )
-    out, near = pl.pallas_call(
+    out, near, partner, token = pl.pallas_call(
         first_kernel,
-        out_shape=(pltpu.VMEM(blocks, BF16), pltpu.VMEM((KINDS, levels, cols), F32)),
-        in_specs=[SMEM] + [VMEM] * 4,
-        out_specs=(VMEM,) * 2,
+        out_shape=(
+            pltpu.VMEM(blocks, BF16), pltpu.VMEM((KINDS, levels, cols), F32), pltpu.SMEM((1,), jnp.int32),
+            pltpu.HBM((TILE, cols), F32),
+        ),
+        in_specs=[VMEM] * 5,
+        out_specs=(VMEM, VMEM, SMEM, VMEM),
         scratch_shapes=[pltpu.VMEM((2 * levels, TILE, cols), F32)],
         compiler_params=PARAMS,
         name="first",
-    )(fold_partner, field, velocity, diffusivity, flux)
+    )(near_partner, field, velocity, diffusivity, flux)
     first, near = exchange(out), swap(near)
-    sources, weights = bring([remap_src[0], weights], [pltpu.SMEM, pltpu.VMEM], room, "load")
+    sources, weights = bring([remap_src[0], weights], [pltpu.SMEM, pltpu.VMEM], room, "load", (token,))
     points, columns, start = pl.pallas_call(
         side_kernel,
         out_shape=(
             pltpu.VMEM((5,) + theta.shape, F32), pltpu.VMEM((2, 3, cols), F32), pltpu.VMEM(theta.shape, F32),
         ),
-        in_specs=[SMEM] + [VMEM] * 3,
+        in_specs=[SMEM] + [VMEM] * 3 + [pl.BlockSpec(memory_space=pl.ANY)],
         out_specs=(VMEM,) * 3,
         compiler_params=PARAMS,
         cost_estimate=pl.CostEstimate(flops=2**20, bytes_accessed=2**20, transcendentals=0),
         name="side",
-    )(land_mask, field, velocity, diffusivity)
+    )(land_mask, field, velocity, diffusivity, token)
     total, force, after, ends, out = pl.pallas_call(
         middle_kernel,
         out_shape=(
@@ -498,7 +507,7 @@
         scratch_shapes=[pltpu.VMEM(theta.shape, F32)] * 2,
         compiler_params=PARAMS,
         name="middle",
-    )(land_mask, fold_partner, sources, columns, points, start, weights, first, near)
+    )(land_mask, partner, sources, columns, points, start, weights, first, near)
     second = exchange(out)
     field, flux = pl.pallas_call(
         last_kernel,
@@ -512,7 +521,7 @@
         ],
         compiler_params=PARAMS,
         name="last",
-    )(fold_partner, field, points, total, after, ends, force, first, second, near)
+    )(partner, field, points, total, after, ends, force, first, second, near)
     return field, flux.reshape(1, 1, fields, rows * cols)
 
 

time: 28.6 us -> 29.1 us (1.017)
  Pallas kernels: 4.98 us -> 5.61 us
  between operations: 1.97 us -> 1.34 us
  starting transfers between devices: 7.61 us -> 7.98 us
    pallas_call x1, Pallas kernels: 0.88 us -> 1.52 us  [local(): pl.pallas_call(first_kernel, out_shape=(pltpu.VMEM(blocks, BF16), pltpu.V...]
    ppermute x1 -> x2, starting transfers between devices: 0.32 us -> 0.83 us  [swap(): return lax.ppermute(rows, 'ns', pairs + [(b, a) for a, b in pairs])]
  transfers between devices with their start and end apart: 2 -> 3, of which waited for: 1 -> 2; matrix products, arithmetic and copies ran while one was open for 0% -> 0% of each run, Pallas kernels for 5% -> 8%
where the time goes in v8:
time: 29.1 us; the launch traced here: 28.9 us
  blocking collectives  8.97 us (31%)
  starting transfers between devices  7.98 us (27%)
  Pallas kernels  5.61 us (19%)
  waiting for transfers between devices  4.94 us (17%)
  between operations  1.34 us (5%)
    all_to_all x1, blocking collectives, exchange(): lax.all_to_all(blocks, ('ns', 'ew'), split_axis=0, concat_axis=0, tiled=T...  8.97 us
    all_to_all x1, starting transfers between devices, exchange(): lax.all_to_all(blocks, ('ns', 'ew'), split_axis=0, concat_axis=0, tiled=T...  7.15 us
    all_to_all x1, waiting for transfers between devices, exchange(): lax.all_to_all(blocks, ('ns', 'ew'), split_axis=0, concat_axis=0, tiled=T...  4.84 us
    pallas_call x2, Pallas kernels, bring(): pl.pallas_call(functools.partial(bring_kernel, len(arrays), len(after)),...  2.23 us
    pallas_call x1, Pallas kernels, local(): pl.pallas_call(first_kernel, out_shape=(pltpu.VMEM(blocks, BF16), pltpu.V...  1.52 us
    pallas_call x1, Pallas kernels, local(): pl.pallas_call(last_kernel, out_shape=(shape(theta.shape, F32), shape((fi...  1.19 us
    ppermute x2, starting transfers between devices, swap(): return lax.ppermute(rows, 'ns', pairs + [(b, a) for a, b in pairs])  0.83 us
  transfers between devices with their start and end apart: 3, of which 2 were waited for; matrix products, arithmetic and copies ran while one was open for 0% of the time, Pallas kernels for 8%

profile of v8, /device:TPU:0, one launch (start us, length us, event | category | flops | bytes accessed | tf_op | source)
XLA Modules:
  0.0 28.9 jit_solution(6138104259783013447)
XLA Ops:
  0.6 0.5 %collective-permute-start = (s32[1]{0:T(128)}, s32[1]{0:T(128)}, u32[]{:S(2)}, u32[]{:S(2)}) collective-permute-start(s32[1]{0:T(128)} %param.12), channel_id=1, source_target_pairs={{0,1},{2,3},{1,0},{3,2},{4,5},{6,7},{5,4},{7,6},{8,9},{10,11},{9,8... | collective-permute-start | bytes 20 | tf_op jit(solution)/shard_map/ppermute | solution.py:459
  1.1 1.0 %bring.1 = (f32[16,8,128]{2,1,0:T(8,128)S(1)}, f32[2,16,8,128]{3,2,1,0:T(8,128)S(1)}, f32[16,8,128]{2,1,0:T(8,128)S(1)}, bf16[6,128]{1,0:T(8,128)(2,1)S(1)}) custom-call(f32[16,8,128]{2,1,0:T(8,128)} %refs_0_.1, f32[2,16,8,128]{3,2,1,0:T(8,128)} %refs_1_.1, f32[16,8,128]{2,1,0:T(8,128)} %refs_2_.1, bf16[6,128]{1,0:T(8,128)(2,1)} %bitcast.6), custom_call_target="tpu_custom_call" | custom-call | flops 1048576 | bytes 4194304 | tf_op jit(solution)/shard_map/bring/pallas_call | solution.py:104
  2.1 0.1 collective-permute-done
  2.2 1.5 %first.1 = (bf16[32,8,128]{2,1,0:T(8,128)(2,1)}, f32[6,16,128]{2,1,0:T(8,128)S(1)}, s32[1]{0:T(128)S(4)}, f32[8,128]{1,0:T(8,128)}) custom-call(s32[1,1]{1,0:T(1,128)} %bitcast.partner_ref, f32[16,8,128]{2,1,0:T(8,128)S(1)} %get-tuple-element.22.theta_ref, f32[2,16,8,128]{3,2,1,0:T(8,128)S(1)} %get-tuple-element.23.vel_ref, ...), custom_call_target="tpu_custom_call" | custom-call | tf_op jit(solution)/shard_map/first/pallas_call | solution.py:474
  3.8 7.1 %all-to-all-start = ((bf16[32,8,128]{2,1,0:T(8,128)(2,1)}), bf16[32,8,128]{2,1,0:T(8,128)(2,1)S(1)}, u32[]{:S(2)}, u32[]{:S(2)}) async-start(bf16[32,8,128]{2,1,0:T(8,128)(2,1)} %get-tuple-element.33), calls=%async_computation | async-start | bytes 131072 | tf_op jit(solution)/shard_map/all_to_all | solution.py:454
  10.9 0.0 copy-start
  10.9 0.3 %collective-permute-start.1 = (f32[6,16,128]{2,1,0:T(8,128)S(1)}, f32[6,16,128]{2,1,0:T(8,128)S(1)}, u32[]{:S(2)}, u32[]{:S(2)}) collective-permute-start(f32[6,16,128]{2,1,0:T(8,128)S(1)} %get-tuple-element.34), channel_id=1, source_target_pairs={{0,1},{2,3},{1,0},{3,2},{4,5},{6,7},{5,4},{7,6},{8,9},{10,11},{9,8... | collective-permute-start | bytes 147464 | tf_op jit(solution)/shard_map/ppermute | solution.py:459
  11.9 0.0 copy-done
  11.9 0.2 side.1
  12.1 1.2 %load.1 = (s32[1,4]{1,0:T(1,128)S(4)}, bf16[4,128,1024]{2,1,0:T(8,128)(2,1)S(1)}) custom-call(s32[1,4]{1,0:T(1,128)} %bitcast.7, bf16[4,128,1024]{2,1,0:T(8,128)(2,1)} %bitcast.5, f32[8,128]{1,0:T(8,128)} %get-tuple-element.27._.refs_2_), custom_call_target="tpu_custom_call" | custom-call | flops 1048576 | bytes 4194304 | tf_op jit(solution)/shard_map/load/pallas_call | solution.py:104
  13.3 0.0 collective-permute-done.1.near_ref
  13.3 4.8 %all-to-all-done.recv_ref.first_ref = bf16[32,8,128]{2,1,0:T(8,128)(2,1)S(1)} async-done(((bf16[32,8,128]{2,1,0:T(8,128)(2,1)}), bf16[32,8,128]{2,1,0:T(8,128)(2,1)S(1)}, u32[]{:S(2)}, u32[]{:S(2)}) %all-to-all-start) | async-done | bytes 65568 | tf_op jit(solution)/shard_map/all_to_all | solution.py:454
  18.2 0.5 %middle.1 = (f32[6,1024]{1,0:T(8,128)S(1)}, f32[8,128]{1,0:T(8,128)S(1)}, f32[16,8,128]{2,1,0:T(8,128)S(1)}, f32[8,128]{1,0:T(8,128)S(1)}, bf16[32,8,128]{2,1,0:T(8,128)(2,1)S(1)}) custom-call(s32[1,1]{1,0:T(1,128)S(6)} %copy.12.mask_ref, s32[1]{0:T(128)S(4)} %get-tuple-element.26.partner_ref, s32[1,4]{1,0:T(1,128)S(4)} %get-tuple-element.29.src_ref, ...), custom_call_target="tpu_custom_call" | custom-call | tf_op jit(solution)/shard_map/middle/pallas_call | solution.py:499
  18.7 9.0 %all_to_all.10.second_ref = bf16[32,8,128]{2,1,0:T(8,128)(2,1)S(1)} all-to-all(bf16[32,8,128]{2,1,0:T(8,128)(2,1)S(1)} %get-tuple-element.39), channel_id=1, replica_groups=mesh['ew'=8,'ns'=4] {'ns','ew'}, dimensions={0} | all-to-all | bytes 131072 | tf_op jit(solution)/shard_map/all_to_all | solution.py:454
  27.7 1.2 %last.1 = (f32[16,8,128]{2,1,0:T(8,128)}, f32[6,8,128]{2,1,0:T(8,128)}) custom-call(s32[1]{0:T(128)S(4)} %get-tuple-element.26.partner_ref, f32[16,8,128]{2,1,0:T(8,128)S(1)} %get-tuple-element.22.theta_ref, f32[5,16,8,128]{3,2,1,0:T(8,128)S(1)} %get-tuple-element.28.points_ref, f32[6,1024]{1,0:T(8,128)S(1)} %get-tuple-element.35.total_ref, ...), custom_call_target="tpu_custom_call" | custom-call | tf_op jit(solution)/shard_map/last/pallas_call | solution.py:512
Async XLA Ops:
  0.6 1.6 %collective-permute-start = (s32[1]{0:T(128)}, s32[1]{0:T(128)}, u32[]{:S(2)}, u32[]{:S(2)}) collective-permute-start(s32[1]{0:T(128)} %param.12), channel_id=1, source_target_pairs={{0,1},{2,3},{1,0},{3,2},{4,5},{6,7},{5,4},{7,6},{8,9},{10,11},{9,8... | collective-permute-start | bytes 20 | tf_op jit(solution)/shard_map/ppermute | solution.py:459
  3.8 14.4 %all-to-all-start = ((bf16[32,8,128]{2,1,0:T(8,128)(2,1)}), bf16[32,8,128]{2,1,0:T(8,128)(2,1)S(1)}, u32[]{:S(2)}, u32[]{:S(2)}) async-start(bf16[32,8,128]{2,1,0:T(8,128)(2,1)} %get-tuple-element.33), calls=%async_computation | async-start | bytes 131072 | tf_op jit(solution)/shard_map/all_to_all | solution.py:454
  10.9 1.0 %copy-start = (f32[8,128]{1,0:T(8,128)S(1)}, f32[8,128]{1,0:T(8,128)}, u32[]{:S(2)}) copy-start(f32[8,128]{1,0:T(8,128)} %get-tuple-element.27._.refs_2_) | copy-start | bytes 12292
  10.9 2.4 %collective-permute-start.1 = (f32[6,16,128]{2,1,0:T(8,128)S(1)}, f32[6,16,128]{2,1,0:T(8,128)S(1)}, u32[]{:S(2)}, u32[]{:S(2)}) collective-permute-start(f32[6,16,128]{2,1,0:T(8,128)S(1)} %get-tuple-element.34), channel_id=1, source_target_pairs={{0,1},{2,3},{1,0},{3,2},{4,5},{6,7},{5,4},{7,6},{8,9},{10,11},{9,8... | collective-permute-start | bytes 147464 | tf_op jit(solution)/shard_map/ppermute | solution.py:459

commit v9 on v7

--- a/solution.py
+++ b/solution.py
@@ -290,13 +290,6 @@
     here = Place()
     levels, rows, cols = theta_ref.shape
     last = rows - 1
-    for k in range(flux_ref.shape[0]):
-        for r in range(rows):
-            flux_ref[k, r : r + 1, :] = total_ref[k : k + 1, r * cols : (r + 1) * cols]
-    copies = [
-        pltpu.make_async_copy(flux_ref, flux_hbm, sems.at[0]), pltpu.make_async_copy(result_ref, result_hbm, sems.at[1])
-    ]
-    copies[0].start()
     partner = partner_ref[0]
     is_top, has_south = here.is_top, here.has_south
 
@@ -440,7 +433,14 @@
 
     tall_ref[:, TILE : 2 * TILE, :] = advance(rim, north_one, south_one)
     result_ref[...] = advance(listing(1, rim), north_next, south_next)
-    copies[1].start()
+    for k in range(flux_ref.shape[0]):
+        for r in range(rows):
+            flux_ref[k, r : r + 1, :] = total_ref[k : k + 1, r * cols : (r + 1) * cols]
+    copies = [
+        pltpu.make_async_copy(flux_ref, flux_hbm, sems.at[0]), pltpu.make_async_copy(result_ref, result_hbm, sems.at[1])
+    ]
+    for copy in copies:
+        copy.start()
     for copy in copies:
         copy.wait()
 

time: 28.6 us -> 28.6 us (level)
  no operation moved by 1% of the time
where the time goes in v9:
time: 28.6 us; the launch traced here: 28.4 us
  blocking collectives  8.97 us (31%)
  starting transfers between devices  7.61 us (27%)
  Pallas kernels  4.98 us (17%)
  waiting for transfers between devices  4.87 us (17%)
  between operations  1.97 us (7%)
    all_to_all x1, blocking collectives, exchange(): lax.all_to_all(blocks, ('ns', 'ew'), split_axis=0, concat_axis=0, tiled=T...  8.97 us
    all_to_all x1, starting transfers between devices, exchange(): lax.all_to_all(blocks, ('ns', 'ew'), split_axis=0, concat_axis=0, tiled=T...  7.3 us
    all_to_all x1, waiting for transfers between devices, exchange(): lax.all_to_all(blocks, ('ns', 'ew'), split_axis=0, concat_axis=0, tiled=T...  4.86 us
    pallas_call x2, Pallas kernels, bring(): pl.pallas_call(functools.partial(bring_kernel, len(arrays)), out_shape=tu...  2.23 us
    pallas_call x1, Pallas kernels, local(): pl.pallas_call(last_kernel, out_shape=(shape(theta.shape, F32), shape((fi...  1.19 us
    pallas_call x1, Pallas kernels, local(): pl.pallas_call(first_kernel, out_shape=(pltpu.VMEM(blocks, BF16), pltpu.V...  0.88 us
  transfers between devices with their start and end apart: 2, of which 1 were waited for; matrix products, arithmetic and copies ran while one was open for 0% of the time, Pallas kernels for 5%

profile of v9, /device:TPU:0, one launch (start us, length us, event | category | flops | bytes accessed | tf_op | source)
XLA Modules:
  0.0 28.4 jit_solution(15362473720708731451)
XLA Ops:
  1.3 1.0 %bring.1 = (f32[16,8,128]{2,1,0:T(8,128)S(1)}, f32[2,16,8,128]{3,2,1,0:T(8,128)S(1)}, f32[16,8,128]{2,1,0:T(8,128)S(1)}, bf16[6,128]{1,0:T(8,128)(2,1)S(1)}) custom-call(f32[16,8,128]{2,1,0:T(8,128)} %refs_0_.1, f32[2,16,8,128]{3,2,1,0:T(8,128)} %refs_1_.1, f32[16,8,128]{2,1,0:T(8,128)} %refs_2_.1, bf16[6,128]{1,0:T(8,128)(2,1)} %bitcast.5), custom_call_target="tpu_custom_call" | custom-call | flops 1048576 | bytes 4194304 | tf_op jit(solution)/shard_map/bring/pallas_call | solution.py:104
  2.3 0.9 %first.1 = (bf16[32,8,128]{2,1,0:T(8,128)(2,1)}, f32[6,16,128]{2,1,0:T(8,128)S(1)}) custom-call(s32[1]{0:T(128)S(6)} %copy.13.partner_ref, f32[16,8,128]{2,1,0:T(8,128)S(1)} %get-tuple-element.20.theta_ref, f32[2,16,8,128]{3,2,1,0:T(8,128)S(1)} %get-tuple-element.21.vel_ref, f32[16,8,128]{2,1,0:T(8,128)S(1)} %get-tuple-element.22.diff_ref, ...), custom_call_target="tpu_custom_call" | custom-call | tf_op jit(solution)/shard_map/first/pallas_call | solution.py:468
  3.1 7.3 %all-to-all-start = ((bf16[32,8,128]{2,1,0:T(8,128)(2,1)}), bf16[32,8,128]{2,1,0:T(8,128)(2,1)S(1)}, u32[]{:S(2)}, u32[]{:S(2)}) async-start(bf16[32,8,128]{2,1,0:T(8,128)(2,1)} %get-tuple-element.29), calls=%async_computation | async-start | bytes 131072 | tf_op jit(solution)/shard_map/all_to_all | solution.py:449
  10.5 0.3 %collective-permute-start = (f32[6,16,128]{2,1,0:T(8,128)S(1)}, f32[6,16,128]{2,1,0:T(8,128)S(1)}, u32[]{:S(2)}, u32[]{:S(2)}) collective-permute-start(f32[6,16,128]{2,1,0:T(8,128)S(1)} %get-tuple-element.30), channel_id=1, source_target_pairs={{0,1},{2,3},{1,0},{3,2},{4,5},{6,7},{5,4},{7,6},{8,9},{10,11},{9,8... | collective-permute-start | bytes 147464 | tf_op jit(solution)/shard_map/ppermute | solution.py:454
  11.4 0.2 side.1
  11.6 1.2 %load.1 = (s32[1,4]{1,0:T(1,128)S(4)}, bf16[4,128,1024]{2,1,0:T(8,128)(2,1)S(1)}) custom-call(s32[1,4]{1,0:T(1,128)} %bitcast.6, bf16[4,128,1024]{2,1,0:T(8,128)(2,1)} %bitcast.4), custom_call_target="tpu_custom_call" | custom-call | flops 1048576 | bytes 4194304 | tf_op jit(solution)/shard_map/load/pallas_call | solution.py:104
  12.9 0.0 collective-permute-done.near_ref
  12.9 4.9 %all-to-all-done.recv_ref.first_ref = bf16[32,8,128]{2,1,0:T(8,128)(2,1)S(1)} async-done(((bf16[32,8,128]{2,1,0:T(8,128)(2,1)}), bf16[32,8,128]{2,1,0:T(8,128)(2,1)S(1)}, u32[]{:S(2)}, u32[]{:S(2)}) %all-to-all-start) | async-done | bytes 65568 | tf_op jit(solution)/shard_map/all_to_all | solution.py:449
  17.7 0.5 %middle.1 = (f32[6,1024]{1,0:T(8,128)S(1)}, f32[8,128]{1,0:T(8,128)S(1)}, f32[16,8,128]{2,1,0:T(8,128)S(1)}, f32[8,128]{1,0:T(8,128)S(1)}, bf16[32,8,128]{2,1,0:T(8,128)(2,1)S(1)}) custom-call(s32[1,1]{1,0:T(1,128)S(6)} %copy.12.mask_ref, s32[1]{0:T(128)S(6)} %copy.13.partner_ref, s32[1,4]{1,0:T(1,128)S(4)} %get-tuple-element.24.src_ref, ...), custom_call_target="tpu_custom_call" | custom-call | tf_op jit(solution)/shard_map/middle/pallas_call | solution.py:490
  18.2 9.0 %all_to_all.10.second_ref = bf16[32,8,128]{2,1,0:T(8,128)(2,1)S(1)} all-to-all(bf16[32,8,128]{2,1,0:T(8,128)(2,1)S(1)} %get-tuple-element.35), channel_id=1, replica_groups=mesh['ew'=8,'ns'=4] {'ns','ew'}, dimensions={0} | all-to-all | bytes 131072 | tf_op jit(solution)/shard_map/all_to_all | solution.py:449
  27.2 1.2 %last.1 = (f32[16,8,128]{2,1,0:T(8,128)}, f32[6,8,128]{2,1,0:T(8,128)}) custom-call(s32[1]{0:T(128)S(6)} %copy.13.partner_ref, f32[16,8,128]{2,1,0:T(8,128)S(1)} %get-tuple-element.20.theta_ref, f32[5,16,8,128]{3,2,1,0:T(8,128)S(1)} %get-tuple-element.23.points_ref, f32[6,1024]{1,0:T(8,128)S(1)} %get-tuple-element.31.total_ref, ...), custom_call_target="tpu_custom_call" | custom-call | tf_op jit(solution)/shard_map/last/pallas_call | solution.py:503
Async XLA Ops:
  3.1 14.6 %all-to-all-start = ((bf16[32,8,128]{2,1,0:T(8,128)(2,1)}), bf16[32,8,128]{2,1,0:T(8,128)(2,1)S(1)}, u32[]{:S(2)}, u32[]{:S(2)}) async-start(bf16[32,8,128]{2,1,0:T(8,128)(2,1)} %get-tuple-element.29), calls=%async_computation | async-start | bytes 131072 | tf_op jit(solution)/shard_map/all_to_all | solution.py:449
  10.5 2.4 %collective-permute-start = (f32[6,16,128]{2,1,0:T(8,128)S(1)}, f32[6,16,128]{2,1,0:T(8,128)S(1)}, u32[]{:S(2)}, u32[]{:S(2)}) collective-permute-start(f32[6,16,128]{2,1,0:T(8,128)S(1)} %get-tuple-element.30), channel_id=1, source_target_pairs={{0,1},{2,3},{1,0},{3,2},{4,5},{6,7},{5,4},{7,6},{8,9},{10,11},{9,8... | collective-permute-start | bytes 147464 | tf_op jit(solution)/shard_map/ppermute | solution.py:454

commit v10 on v9

--- a/solution.py
+++ b/solution.py
@@ -47,6 +47,9 @@
 
     def slot(self, e, n):
         return n * self.count + e
+
+    def second_slot(self, e, n):
+        return e * self.block_rows + n
 
 
 def relays(row, block_rows):
@@ -280,7 +283,7 @@
                 tile = folded[e * TILE : (e + 1) * TILE]
             else:
                 tile = got(e, max(n - 1, 0) if n % 2 == 0 else n + 1)
-            out_ref[n * here.count + e] = jnp.where(owed, begin, tile).astype(BF16)
+            out_ref[here.second_slot(e, n)] = jnp.where(owed, begin, tile).astype(BF16)
 
 
 def last_kernel(
@@ -294,7 +297,7 @@
     is_top, has_south = here.is_top, here.has_south
 
     def got(e, n):
-        return second_ref[here.slot(e, n)].astype(F32)
+        return second_ref[here.second_slot(e, n)].astype(F32)
 
     west, east = got(here.west, here.n), got(here.east, here.n)
     over, under = got(here.e, here.above), got(here.e, here.below)
@@ -445,8 +448,8 @@
         copy.wait()
 
 
-def exchange(blocks):
-    return lax.all_to_all(blocks, ("ns", "ew"), split_axis=0, concat_axis=0, tiled=True)
+def exchange(blocks, axes):
+    return lax.all_to_all(blocks, axes, split_axis=0, concat_axis=0, tiled=True)
 
 
 def swap(rows):
@@ -474,7 +477,7 @@
         compiler_params=PARAMS,
         name="first",
     )(fold_partner, field, velocity, diffusivity, flux)
-    first, near = exchange(out), swap(near)
+    first, near = exchange(out, ("ns", "ew")), swap(near)
     sources, weights = bring([remap_src[0], weights], [pltpu.SMEM, pltpu.VMEM], room, "load")
     points, columns, start = pl.pallas_call(
         side_kernel,
@@ -499,7 +502,7 @@
         compiler_params=PARAMS,
         name="middle",
     )(land_mask, fold_partner, sources, columns, points, start, weights, first, near)
-    second = exchange(out)
+    second = exchange(out, ("ew", "ns"))
     field, flux = pl.pallas_call(
         last_kernel,
         out_shape=(shape(theta.shape, F32), shape((fields, rows, cols), F32)),

time: 28.6 us -> 28.8 us (level)
  no operation moved by 1% of the time
where the time goes in v10:
time: 28.8 us; the launch traced here: 28.5 us
  blocking collectives  9.1 us (32%)
  starting transfers between devices  7.61 us (26%)
  Pallas kernels  4.98 us (17%)
  waiting for transfers between devices  4.87 us (17%)
  between operations  1.97 us (7%)
    all_to_all x1, blocking collectives, exchange(): return lax.all_to_all(blocks, axes, split_axis=0, concat_axis=0, tiled=True)  9.1 us
    all_to_all x1, starting transfers between devices, exchange(): return lax.all_to_all(blocks, axes, split_axis=0, concat_axis=0, tiled=True)  7.3 us
    all_to_all x1, waiting for transfers between devices, exchange(): return lax.all_to_all(blocks, axes, split_axis=0, concat_axis=0, tiled=True)  4.86 us
    pallas_call x2, Pallas kernels, bring(): pl.pallas_call(functools.partial(bring_kernel, len(arrays)), out_shape=tu...  2.23 us
    pallas_call x1, Pallas kernels, local(): pl.pallas_call(last_kernel, out_shape=(shape(theta.shape, F32), shape((fi...  1.18 us
    pallas_call x1, Pallas kernels, local(): pl.pallas_call(first_kernel, out_shape=(pltpu.VMEM(blocks, BF16), pltpu.V...  0.88 us
  transfers between devices with their start and end apart: 2, of which 1 were waited for; matrix products, arithmetic and copies ran while one was open for 0% of the time, Pallas kernels for 5%

profile of v10, /device:TPU:0, one launch (start us, length us, event | category | flops | bytes accessed | tf_op | source)
XLA Modules:
  0.0 28.5 jit_solution(12140726104326840601)
XLA Ops:
  1.3 1.0 %bring.1 = (f32[16,8,128]{2,1,0:T(8,128)S(1)}, f32[2,16,8,128]{3,2,1,0:T(8,128)S(1)}, f32[16,8,128]{2,1,0:T(8,128)S(1)}, bf16[6,128]{1,0:T(8,128)(2,1)S(1)}) custom-call(f32[16,8,128]{2,1,0:T(8,128)} %refs_0_.1, f32[2,16,8,128]{3,2,1,0:T(8,128)} %refs_1_.1, f32[16,8,128]{2,1,0:T(8,128)} %refs_2_.1, bf16[6,128]{1,0:T(8,128)(2,1)} %bitcast.5), custom_call_target="tpu_custom_call" | custom-call | flops 1048576 | bytes 4194304 | tf_op jit(solution)/shard_map/bring/pallas_call | solution.py:107
  2.3 0.9 %first.1 = (bf16[32,8,128]{2,1,0:T(8,128)(2,1)}, f32[6,16,128]{2,1,0:T(8,128)S(1)}) custom-call(s32[1]{0:T(128)S(6)} %copy.13.partner_ref, f32[16,8,128]{2,1,0:T(8,128)S(1)} %get-tuple-element.20.theta_ref, f32[2,16,8,128]{3,2,1,0:T(8,128)S(1)} %get-tuple-element.21.vel_ref, f32[16,8,128]{2,1,0:T(8,128)S(1)} %get-tuple-element.22.diff_ref, ...), custom_call_target="tpu_custom_call" | custom-call | tf_op jit(solution)/shard_map/first/pallas_call | solution.py:471
  3.1 7.3 %all-to-all-start = ((bf16[32,8,128]{2,1,0:T(8,128)(2,1)}), bf16[32,8,128]{2,1,0:T(8,128)(2,1)S(1)}, u32[]{:S(2)}, u32[]{:S(2)}) async-start(bf16[32,8,128]{2,1,0:T(8,128)(2,1)} %get-tuple-element.29), calls=%async_computation | async-start | bytes 131072 | tf_op jit(solution)/shard_map/all_to_all | solution.py:452
  10.5 0.3 %collective-permute-start = (f32[6,16,128]{2,1,0:T(8,128)S(1)}, f32[6,16,128]{2,1,0:T(8,128)S(1)}, u32[]{:S(2)}, u32[]{:S(2)}) collective-permute-start(f32[6,16,128]{2,1,0:T(8,128)S(1)} %get-tuple-element.30), channel_id=1, source_target_pairs={{0,1},{2,3},{1,0},{3,2},{4,5},{6,7},{5,4},{7,6},{8,9},{10,11},{9,8... | collective-permute-start | bytes 147464 | tf_op jit(solution)/shard_map/ppermute | solution.py:457
  11.4 0.2 side.1
  11.6 1.2 %load.1 = (s32[1,4]{1,0:T(1,128)S(4)}, bf16[4,128,1024]{2,1,0:T(8,128)(2,1)S(1)}) custom-call(s32[1,4]{1,0:T(1,128)} %bitcast.6, bf16[4,128,1024]{2,1,0:T(8,128)(2,1)} %bitcast.4), custom_call_target="tpu_custom_call" | custom-call | flops 1048576 | bytes 4194304 | tf_op jit(solution)/shard_map/load/pallas_call | solution.py:107
  12.9 0.0 collective-permute-done.near_ref
  12.9 4.9 %all-to-all-done.recv_ref.first_ref = bf16[32,8,128]{2,1,0:T(8,128)(2,1)S(1)} async-done(((bf16[32,8,128]{2,1,0:T(8,128)(2,1)}), bf16[32,8,128]{2,1,0:T(8,128)(2,1)S(1)}, u32[]{:S(2)}, u32[]{:S(2)}) %all-to-all-start) | async-done | bytes 65568 | tf_op jit(solution)/shard_map/all_to_all | solution.py:452
  17.7 0.5 %middle.1 = (f32[6,1024]{1,0:T(8,128)S(1)}, f32[8,128]{1,0:T(8,128)S(1)}, f32[16,8,128]{2,1,0:T(8,128)S(1)}, f32[8,128]{1,0:T(8,128)S(1)}, bf16[32,8,128]{2,1,0:T(8,128)(2,1)S(1)}) custom-call(s32[1,1]{1,0:T(1,128)S(6)} %copy.12.mask_ref, s32[1]{0:T(128)S(6)} %copy.13.partner_ref, s32[1,4]{1,0:T(1,128)S(4)} %get-tuple-element.24.src_ref, ...), custom_call_target="tpu_custom_call" | custom-call | tf_op jit(solution)/shard_map/middle/pallas_call | solution.py:493
  18.2 9.1 %all_to_all.10.second_ref = bf16[32,8,128]{2,1,0:T(8,128)(2,1)S(1)} all-to-all(bf16[32,8,128]{2,1,0:T(8,128)(2,1)S(1)} %get-tuple-element.35), channel_id=1, replica_groups=mesh['ew'=8,'ns'=4] {'ew','ns'}, dimensions={0} | all-to-all | bytes 131072 | tf_op jit(solution)/shard_map/all_to_all | solution.py:452
  27.4 1.2 %last.1 = (f32[16,8,128]{2,1,0:T(8,128)}, f32[6,8,128]{2,1,0:T(8,128)}) custom-call(s32[1]{0:T(128)S(6)} %copy.13.partner_ref, f32[16,8,128]{2,1,0:T(8,128)S(1)} %get-tuple-element.20.theta_ref, f32[5,16,8,128]{3,2,1,0:T(8,128)S(1)} %get-tuple-element.23.points_ref, f32[6,1024]{1,0:T(8,128)S(1)} %get-tuple-element.31.total_ref, ...), custom_call_target="tpu_custom_call" | custom-call | tf_op jit(solution)/shard_map/last/pallas_call | solution.py:506
Async XLA Ops:
  3.1 14.6 %all-to-all-start = ((bf16[32,8,128]{2,1,0:T(8,128)(2,1)}), bf16[32,8,128]{2,1,0:T(8,128)(2,1)S(1)}, u32[]{:S(2)}, u32[]{:S(2)}) async-start(bf16[32,8,128]{2,1,0:T(8,128)(2,1)} %get-tuple-element.29), calls=%async_computation | async-start | bytes 131072 | tf_op jit(solution)/shard_map/all_to_all | solution.py:452
  10.5 2.4 %collective-permute-start = (f32[6,16,128]{2,1,0:T(8,128)S(1)}, f32[6,16,128]{2,1,0:T(8,128)S(1)}, u32[]{:S(2)}, u32[]{:S(2)}) collective-permute-start(f32[6,16,128]{2,1,0:T(8,128)S(1)} %get-tuple-element.30), channel_id=1, source_target_pairs={{0,1},{2,3},{1,0},{3,2},{4,5},{6,7},{5,4},{7,6},{8,9},{10,11},{9,8... | collective-permute-start | bytes 147464 | tf_op jit(solution)/shard_map/ppermute | solution.py:457

commit v11 on v9

--- a/solution.py
+++ b/solution.py
@@ -432,15 +432,17 @@
         return result
 
     tall_ref[:, TILE : 2 * TILE, :] = advance(rim, north_one, south_one)
-    result_ref[...] = advance(listing(1, rim), north_next, south_next)
     for k in range(flux_ref.shape[0]):
         for r in range(rows):
             flux_ref[k, r : r + 1, :] = total_ref[k : k + 1, r * cols : (r + 1) * cols]
-    copies = [
-        pltpu.make_async_copy(flux_ref, flux_hbm, sems.at[0]), pltpu.make_async_copy(result_ref, result_hbm, sems.at[1])
-    ]
-    for copy in copies:
-        copy.start()
+    copies = [pltpu.make_async_copy(flux_ref, flux_hbm, sems.at[0])]
+    copies[0].start()
+    t = advance(listing(1, rim), north_next, south_next)
+    for half in range(2):
+        part = pl.ds(half * (levels // 2), levels // 2)
+        result_ref[part] = t[half * (levels // 2) : (half + 1) * (levels // 2)]
+        copies.append(pltpu.make_async_copy(result_ref.at[part], result_hbm.at[part], sems.at[1 + half]))
+        copies[-1].start()
     for copy in copies:
         copy.wait()
 
@@ -508,7 +510,7 @@
         scratch_shapes=[
             pltpu.VMEM(theta.shape, F32), pltpu.VMEM((fields, rows, cols), F32), pltpu.VMEM(theta.shape, F32),
             pltpu.VMEM((levels, 3 * TILE, cols), F32), pltpu.VMEM((levels, TILE, cols), F32),
-            pltpu.SemaphoreType.DMA((2,)),
+            pltpu.SemaphoreType.DMA((3,)),
         ],
         compiler_params=PARAMS,
         name="last",

time: 28.6 us -> 28.6 us (level)
  no operation moved by 1% of the time
where the time goes in v11:
time: 28.6 us; the launch traced here: 28.4 us
  blocking collectives  8.97 us (31%)
  starting transfers between devices  7.61 us (27%)
  Pallas kernels  4.98 us (17%)
  waiting for transfers between devices  4.87 us (17%)
  between operations  1.97 us (7%)
    all_to_all x1, blocking collectives, exchange(): lax.all_to_all(blocks, ('ns', 'ew'), split_axis=0, concat_axis=0, tiled=T...  8.97 us
    all_to_all x1, starting transfers between devices, exchange(): lax.all_to_all(blocks, ('ns', 'ew'), split_axis=0, concat_axis=0, tiled=T...  7.3 us
    all_to_all x1, waiting for transfers between devices, exchange(): lax.all_to_all(blocks, ('ns', 'ew'), split_axis=0, concat_axis=0, tiled=T...  4.86 us
    pallas_call x2, Pallas kernels, bring(): pl.pallas_call(functools.partial(bring_kernel, len(arrays)), out_shape=tu...  2.23 us
    pallas_call x1, Pallas kernels, local(): pl.pallas_call(last_kernel, out_shape=(shape(theta.shape, F32), shape((fi...  1.18 us
    pallas_call x1, Pallas kernels, local(): pl.pallas_call(first_kernel, out_shape=(pltpu.VMEM(blocks, BF16), pltpu.V...  0.88 us
  transfers between devices with their start and end apart: 2, of which 1 were waited for; matrix products, arithmetic and copies ran while one was open for 0% of the time, Pallas kernels for 5%

profile of v11, /device:TPU:0, one launch (start us, length us, event | category | flops | bytes accessed | tf_op | source)
XLA Modules:
  0.0 28.4 jit_solution(15868654548919463064)
XLA Ops:
  1.3 1.0 %bring.1 = (f32[16,8,128]{2,1,0:T(8,128)S(1)}, f32[2,16,8,128]{3,2,1,0:T(8,128)S(1)}, f32[16,8,128]{2,1,0:T(8,128)S(1)}, bf16[6,128]{1,0:T(8,128)(2,1)S(1)}) custom-call(f32[16,8,128]{2,1,0:T(8,128)} %refs_0_.1, f32[2,16,8,128]{3,2,1,0:T(8,128)} %refs_1_.1, f32[16,8,128]{2,1,0:T(8,128)} %refs_2_.1, bf16[6,128]{1,0:T(8,128)(2,1)} %bitcast.5), custom_call_target="tpu_custom_call" | custom-call | flops 1048576 | bytes 4194304 | tf_op jit(solution)/shard_map/bring/pallas_call | solution.py:104
  2.3 0.9 %first.1 = (bf16[32,8,128]{2,1,0:T(8,128)(2,1)}, f32[6,16,128]{2,1,0:T(8,128)S(1)}) custom-call(s32[1]{0:T(128)S(6)} %copy.13.partner_ref, f32[16,8,128]{2,1,0:T(8,128)S(1)} %get-tuple-element.20.theta_ref, f32[2,16,8,128]{3,2,1,0:T(8,128)S(1)} %get-tuple-element.21.vel_ref, f32[16,8,128]{2,1,0:T(8,128)S(1)} %get-tuple-element.22.diff_ref, ...), custom_call_target="tpu_custom_call" | custom-call | tf_op jit(solution)/shard_map/first/pallas_call | solution.py:470
  3.1 7.3 %all-to-all-start = ((bf16[32,8,128]{2,1,0:T(8,128)(2,1)}), bf16[32,8,128]{2,1,0:T(8,128)(2,1)S(1)}, u32[]{:S(2)}, u32[]{:S(2)}) async-start(bf16[32,8,128]{2,1,0:T(8,128)(2,1)} %get-tuple-element.29), calls=%async_computation | async-start | bytes 131072 | tf_op jit(solution)/shard_map/all_to_all | solution.py:451
  10.5 0.3 %collective-permute-start = (f32[6,16,128]{2,1,0:T(8,128)S(1)}, f32[6,16,128]{2,1,0:T(8,128)S(1)}, u32[]{:S(2)}, u32[]{:S(2)}) collective-permute-start(f32[6,16,128]{2,1,0:T(8,128)S(1)} %get-tuple-element.30), channel_id=1, source_target_pairs={{0,1},{2,3},{1,0},{3,2},{4,5},{6,7},{5,4},{7,6},{8,9},{10,11},{9,8... | collective-permute-start | bytes 147464 | tf_op jit(solution)/shard_map/ppermute | solution.py:456
  11.4 0.2 side.1
  11.6 1.2 %load.1 = (s32[1,4]{1,0:T(1,128)S(4)}, bf16[4,128,1024]{2,1,0:T(8,128)(2,1)S(1)}) custom-call(s32[1,4]{1,0:T(1,128)} %bitcast.6, bf16[4,128,1024]{2,1,0:T(8,128)(2,1)} %bitcast.4), custom_call_target="tpu_custom_call" | custom-call | flops 1048576 | bytes 4194304 | tf_op jit(solution)/shard_map/load/pallas_call | solution.py:104
  12.9 0.0 collective-permute-done.near_ref
  12.9 4.9 %all-to-all-done.recv_ref.first_ref = bf16[32,8,128]{2,1,0:T(8,128)(2,1)S(1)} async-done(((bf16[32,8,128]{2,1,0:T(8,128)(2,1)}), bf16[32,8,128]{2,1,0:T(8,128)(2,1)S(1)}, u32[]{:S(2)}, u32[]{:S(2)}) %all-to-all-start) | async-done | bytes 65568 | tf_op jit(solution)/shard_map/all_to_all | solution.py:451
  17.7 0.5 %middle.1 = (f32[6,1024]{1,0:T(8,128)S(1)}, f32[8,128]{1,0:T(8,128)S(1)}, f32[16,8,128]{2,1,0:T(8,128)S(1)}, f32[8,128]{1,0:T(8,128)S(1)}, bf16[32,8,128]{2,1,0:T(8,128)(2,1)S(1)}) custom-call(s32[1,1]{1,0:T(1,128)S(6)} %copy.12.mask_ref, s32[1]{0:T(128)S(6)} %copy.13.partner_ref, s32[1,4]{1,0:T(1,128)S(4)} %get-tuple-element.24.src_ref, ...), custom_call_target="tpu_custom_call" | custom-call | tf_op jit(solution)/shard_map/middle/pallas_call | solution.py:492
  18.2 9.0 %all_to_all.10.second_ref = bf16[32,8,128]{2,1,0:T(8,128)(2,1)S(1)} all-to-all(bf16[32,8,128]{2,1,0:T(8,128)(2,1)S(1)} %get-tuple-element.35), channel_id=1, replica_groups=mesh['ew'=8,'ns'=4] {'ns','ew'}, dimensions={0} | all-to-all | bytes 131072 | tf_op jit(solution)/shard_map/all_to_all | solution.py:451
  27.2 1.2 %last.1 = (f32[16,8,128]{2,1,0:T(8,128)}, f32[6,8,128]{2,1,0:T(8,128)}) custom-call(s32[1]{0:T(128)S(6)} %copy.13.partner_ref, f32[16,8,128]{2,1,0:T(8,128)S(1)} %get-tuple-element.20.theta_ref, f32[5,16,8,128]{3,2,1,0:T(8,128)S(1)} %get-tuple-element.23.points_ref, f32[6,1024]{1,0:T(8,128)S(1)} %get-tuple-element.31.total_ref, ...), custom_call_target="tpu_custom_call" | custom-call | tf_op jit(solution)/shard_map/last/pallas_call | solution.py:505
Async XLA Ops:
  3.1 14.6 %all-to-all-start = ((bf16[32,8,128]{2,1,0:T(8,128)(2,1)}), bf16[32,8,128]{2,1,0:T(8,128)(2,1)S(1)}, u32[]{:S(2)}, u32[]{:S(2)}) async-start(bf16[32,8,128]{2,1,0:T(8,128)(2,1)} %get-tuple-element.29), calls=%async_computation | async-start | bytes 131072 | tf_op jit(solution)/shard_map/all_to_all | solution.py:451
  10.5 2.4 %collective-permute-start = (f32[6,16,128]{2,1,0:T(8,128)S(1)}, f32[6,16,128]{2,1,0:T(8,128)S(1)}, u32[]{:S(2)}, u32[]{:S(2)}) collective-permute-start(f32[6,16,128]{2,1,0:T(8,128)S(1)} %get-tuple-element.30), channel_id=1, source_target_pairs={{0,1},{2,3},{1,0},{3,2},{4,5},{6,7},{5,4},{7,6},{8,9},{10,11},{9,8... | collective-permute-start | bytes 147464 | tf_op jit(solution)/shard_map/ppermute | solution.py:456

commit v12 on v11

--- a/solution.py
+++ b/solution.py
@@ -464,8 +464,8 @@
     blocks = (devices, TILE, cols)
     room = 60 * 2**20 - 2 * max(0, 4 * devices * TILE * cols - 2**20)
     weights = remap_weights[0, 0]
-    field, velocity, diffusivity, flux = bring(
-        [theta, velocity, diffusivity, atm_flux[0, 0]], [pltpu.VMEM] * 4, room, "bring"
+    velocity, field, diffusivity, flux = bring(
+        [velocity, theta, diffusivity, atm_flux[0, 0]], [pltpu.VMEM] * 4, room, "bring"
     )
     out, near = pl.pallas_call(
         first_kernel,

time: 28.6 us -> 28.6 us (level)
  no operation moved by 1% of the time
where the time goes in v12:
time: 28.6 us; the launch traced here: 28.4 us
  blocking collectives  8.97 us (31%)
  starting transfers between devices  7.61 us (27%)
  Pallas kernels  4.96 us (17%)
  waiting for transfers between devices  4.87 us (17%)
  between operations  1.97 us (7%)
    all_to_all x1, blocking collectives, exchange(): lax.all_to_all(blocks, ('ns', 'ew'), split_axis=0, concat_axis=0, tiled=T...  8.97 us
    all_to_all x1, starting transfers between devices, exchange(): lax.all_to_all(blocks, ('ns', 'ew'), split_axis=0, concat_axis=0, tiled=T...  7.3 us
    all_to_all x1, waiting for transfers between devices, exchange(): lax.all_to_all(blocks, ('ns', 'ew'), split_axis=0, concat_axis=0, tiled=T...  4.86 us
    pallas_call x2, Pallas kernels, bring(): pl.pallas_call(functools.partial(bring_kernel, len(arrays)), out_shape=tu...  2.22 us
    pallas_call x1, Pallas kernels, local(): pl.pallas_call(last_kernel, out_shape=(shape(theta.shape, F32), shape((fi...  1.18 us
    pallas_call x1, Pallas kernels, local(): pl.pallas_call(first_kernel, out_shape=(pltpu.VMEM(blocks, BF16), pltpu.V...  0.88 us
  transfers between devices with their start and end apart: 2, of which 1 were waited for; matrix products, arithmetic and copies ran while one was open for 0% of the time, Pallas kernels for 5%

profile of v12, /device:TPU:0, one launch (start us, length us, event | category | flops | bytes accessed | tf_op | source)
XLA Modules:
  0.0 28.4 jit_solution(7691016153097177885)
XLA Ops:
  1.3 1.0 %bring.1 = (f32[2,16,8,128]{3,2,1,0:T(8,128)S(1)}, f32[16,8,128]{2,1,0:T(8,128)S(1)}, f32[16,8,128]{2,1,0:T(8,128)S(1)}, bf16[6,128]{1,0:T(8,128)(2,1)S(1)}) custom-call(f32[2,16,8,128]{3,2,1,0:T(8,128)} %refs_0_.1, f32[16,8,128]{2,1,0:T(8,128)} %refs_1_.1, f32[16,8,128]{2,1,0:T(8,128)} %refs_2_.1, bf16[6,128]{1,0:T(8,128)(2,1)} %bitcast.5), custom_call_target="tpu_custom_call" | custom-call | flops 1048576 | bytes 4194304 | tf_op jit(solution)/shard_map/bring/pallas_call | solution.py:104
  2.3 0.9 %first.1 = (bf16[32,8,128]{2,1,0:T(8,128)(2,1)}, f32[6,16,128]{2,1,0:T(8,128)S(1)}) custom-call(s32[1]{0:T(128)S(6)} %copy.13.partner_ref, f32[16,8,128]{2,1,0:T(8,128)S(1)} %get-tuple-element.20.theta_ref, f32[2,16,8,128]{3,2,1,0:T(8,128)S(1)} %get-tuple-element.21.vel_ref, f32[16,8,128]{2,1,0:T(8,128)S(1)} %get-tuple-element.22.diff_ref, ...), custom_call_target="tpu_custom_call" | custom-call | tf_op jit(solution)/shard_map/first/pallas_call | solution.py:470
  3.1 7.3 %all-to-all-start = ((bf16[32,8,128]{2,1,0:T(8,128)(2,1)}), bf16[32,8,128]{2,1,0:T(8,128)(2,1)S(1)}, u32[]{:S(2)}, u32[]{:S(2)}) async-start(bf16[32,8,128]{2,1,0:T(8,128)(2,1)} %get-tuple-element.29), calls=%async_computation | async-start | bytes 131072 | tf_op jit(solution)/shard_map/all_to_all | solution.py:451
  10.4 0.3 %collective-permute-start = (f32[6,16,128]{2,1,0:T(8,128)S(1)}, f32[6,16,128]{2,1,0:T(8,128)S(1)}, u32[]{:S(2)}, u32[]{:S(2)}) collective-permute-start(f32[6,16,128]{2,1,0:T(8,128)S(1)} %get-tuple-element.30), channel_id=1, source_target_pairs={{0,1},{2,3},{1,0},{3,2},{4,5},{6,7},{5,4},{7,6},{8,9},{10,11},{9,8... | collective-permute-start | bytes 147464 | tf_op jit(solution)/shard_map/ppermute | solution.py:456
  11.4 0.2 side.1
  11.6 1.2 %load.1 = (s32[1,4]{1,0:T(1,128)S(4)}, bf16[4,128,1024]{2,1,0:T(8,128)(2,1)S(1)}) custom-call(s32[1,4]{1,0:T(1,128)} %bitcast.6, bf16[4,128,1024]{2,1,0:T(8,128)(2,1)} %bitcast.4), custom_call_target="tpu_custom_call" | custom-call | flops 1048576 | bytes 4194304 | tf_op jit(solution)/shard_map/load/pallas_call | solution.py:104
  12.8 0.0 collective-permute-done.near_ref
  12.9 4.9 %all-to-all-done.recv_ref.first_ref = bf16[32,8,128]{2,1,0:T(8,128)(2,1)S(1)} async-done(((bf16[32,8,128]{2,1,0:T(8,128)(2,1)}), bf16[32,8,128]{2,1,0:T(8,128)(2,1)S(1)}, u32[]{:S(2)}, u32[]{:S(2)}) %all-to-all-start) | async-done | bytes 65568 | tf_op jit(solution)/shard_map/all_to_all | solution.py:451
  17.7 0.5 %middle.1 = (f32[6,1024]{1,0:T(8,128)S(1)}, f32[8,128]{1,0:T(8,128)S(1)}, f32[16,8,128]{2,1,0:T(8,128)S(1)}, f32[8,128]{1,0:T(8,128)S(1)}, bf16[32,8,128]{2,1,0:T(8,128)(2,1)S(1)}) custom-call(s32[1,1]{1,0:T(1,128)S(6)} %copy.12.mask_ref, s32[1]{0:T(128)S(6)} %copy.13.partner_ref, s32[1,4]{1,0:T(1,128)S(4)} %get-tuple-element.24.src_ref, ...), custom_call_target="tpu_custom_call" | custom-call | tf_op jit(solution)/shard_map/middle/pallas_call | solution.py:492
  18.2 9.0 %all_to_all.10.second_ref = bf16[32,8,128]{2,1,0:T(8,128)(2,1)S(1)} all-to-all(bf16[32,8,128]{2,1,0:T(8,128)(2,1)S(1)} %get-tuple-element.35), channel_id=1, replica_groups=mesh['ew'=8,'ns'=4] {'ns','ew'}, dimensions={0} | all-to-all | bytes 131072 | tf_op jit(solution)/shard_map/all_to_all | solution.py:451
  27.2 1.2 %last.1 = (f32[16,8,128]{2,1,0:T(8,128)}, f32[6,8,128]{2,1,0:T(8,128)}) custom-call(s32[1]{0:T(128)S(6)} %copy.13.partner_ref, f32[16,8,128]{2,1,0:T(8,128)S(1)} %get-tuple-element.20.theta_ref, f32[5,16,8,128]{3,2,1,0:T(8,128)S(1)} %get-tuple-element.23.points_ref, f32[6,1024]{1,0:T(8,128)S(1)} %get-tuple-element.31.total_ref, ...), custom_call_target="tpu_custom_call" | custom-call | tf_op jit(solution)/shard_map/last/pallas_call | solution.py:505
Async XLA Ops:
  3.1 14.6 %all-to-all-start = ((bf16[32,8,128]{2,1,0:T(8,128)(2,1)}), bf16[32,8,128]{2,1,0:T(8,128)(2,1)S(1)}, u32[]{:S(2)}, u32[]{:S(2)}) async-start(bf16[32,8,128]{2,1,0:T(8,128)(2,1)} %get-tuple-element.29), calls=%async_computation | async-start | bytes 131072 | tf_op jit(solution)/shard_map/all_to_all | solution.py:451
  10.4 2.4 %collective-permute-start = (f32[6,16,128]{2,1,0:T(8,128)S(1)}, f32[6,16,128]{2,1,0:T(8,128)S(1)}, u32[]{:S(2)}, u32[]{:S(2)}) collective-permute-start(f32[6,16,128]{2,1,0:T(8,128)S(1)} %get-tuple-element.30), channel_id=1, source_target_pairs={{0,1},{2,3},{1,0},{3,2},{4,5},{6,7},{5,4},{7,6},{8,9},{10,11},{9,8... | collective-permute-start | bytes 147464 | tf_op jit(solution)/shard_map/ppermute | solution.py:456
